TPU v7x, 32 devices: a whole 2x2x4 slice. The times are simulated.
32 devices in a mesh: dp: 2 (over y), pb: 4 (over z), ka: 4 (over x, core).
Axes of the slice: x: 2, y: 2, z: 4, core: 2. Of those that a mesh axis runs over, the one named last changes fastest.
Arguments:
- inputs: bfloat16 [4, 2048, 2048], P('dp', ('pb', 'ka')), may hold values from -6 to 6
- out_cotangent: bfloat16 [4, 2048, 2048], P('dp', ('pb', 'ka')), may hold values from -6 to 6
- doc_lengths: int32 [4, 4], P('dp'), may hold values from 0 to 2048, as said below
- ln1_gain: float32 [2048], P(('dp', 'pb', 'ka')), may hold values from 0.5 to 1.5
- w_query: float32 [2048, 2048], P(('dp', 'pb', 'ka'))
- w_key: float32 [2048, 2048], P(('dp', 'pb', 'ka'))
- w_value: float32 [2048, 4096], P(('dp', 'pb', 'ka')), may hold values from -0.125 to 0.125
- w_gate: float32 [2048, 4096], P(('dp', 'pb', 'ka')), may hold values from -0.125 to 0.125
- w_out: float32 [4096, 2048], P(('dp', 'pb', 'ka')), may hold values from -0.09375 to 0.09375
- ln2_gain: float32 [2048], P(('dp', 'pb', 'ka')), may hold values from 0.5 to 1.5
- w_up: float32 [2048, 4096], P(('dp', 'pb', 'ka')), may hold values from -0.125 to 0.125
- up_bias: float32 [4096], P(('dp', 'pb', 'ka')), may hold values from -3 to 3
- w_down: float32 [4096, 2048], P(('dp', 'pb', 'ka')), may hold values from -0.09375 to 0.09375
Outputs:
- output: bfloat16 [4, 2048, 2048], P('dp', ('pb', 'ka'))
- grad_inputs: float32 [4, 2048, 2048], P('dp', ('pb', 'ka'))
- grad_ln1_gain: float32 [2048], P(('dp', 'pb', 'ka'))
- grad_w_query: float32 [2048, 2048], P(('dp', 'pb', 'ka'))
- grad_w_key: float32 [2048, 2048], P(('dp', 'pb', 'ka'))
- grad_w_value: float32 [2048, 4096], P(('dp', 'pb', 'ka'))
- grad_w_gate: float32 [2048, 4096], P(('dp', 'pb', 'ka'))
- grad_w_out: float32 [4096, 2048], P(('dp', 'pb', 'ka'))
- grad_ln2_gain: float32 [2048], P(('dp', 'pb', 'ka'))
- grad_w_up: float32 [2048, 4096], P(('dp', 'pb', 'ka'))
- grad_up_bias: float32 [4096], P(('dp', 'pb', 'ka'))
- grad_w_down: float32 [4096, 2048], P(('dp', 'pb', 'ka'))
Inputs may be any that keep to these rules, and one draw needn't show every extreme that they name: `doc_lengths`: each row packs its 2048 positions with documents of 512, 1024 or 2048 positions that sum to 2048, followed by zeros; in each aligned block of 2 rows exactly one row holds one document of 2048 positions, and every other row holds two or more documents.
All inputs are finite; a program needn't handle non-finite values.
Results may differ from a plain program's by a relative error of at most 0.017.
Values may be sent and summed in bfloat16 or wider, within the bound.
A program may use at most 448 MiB of HBM per device.

v0:
```python
import jax
import jax.numpy as jnp
from jax import lax
from jax.sharding import PartitionSpec as P

H = 8
XPOS_BASE = 512


epsilon = 1e-05


def layer_norm(values, gain_vec):
    row_mean = jnp.mean(values, axis=-1, keepdims=True)
    centered = values - row_mean
    inv_scale = lax.rsqrt(jnp.mean(centered * centered, axis=-1, keepdims=True) + epsilon)
    return centered * inv_scale * gain_vec


def group_norm(values, head_count):
    shaped = values.reshape(values.shape[:-1] + (head_count, values.shape[-1] // head_count))
    row_mean = jnp.mean(shaped, axis=-1, keepdims=True)
    centered = shaped - row_mean
    inv_scale = lax.rsqrt(jnp.mean(centered * centered, axis=-1, keepdims=True) + epsilon)
    return (centered * inv_scale).reshape(values.shape)


def xpos_turn(values, positions, head_count, scale_base, direction):
    head_size = values.shape[-1] // head_count
    half_size = head_size // 2
    pair_index = jnp.arange(half_size, dtype=jnp.float32)
    frequency = jnp.exp(-jnp.log(10000.0) * pair_index / half_size)
    xpos_zeta = (pair_index / half_size + 0.4) / 1.4
    angles = positions[:, None] * frequency[None, :]
    factor = jnp.exp(direction * positions[:, None] / scale_base * jnp.log(xpos_zeta)[None, :])
    cosine = (jnp.cos(angles) * factor)[:, None, :]
    sine_part = (jnp.sin(angles) * factor)[:, None, :]
    shaped = values.reshape(values.shape[:-1] + (head_count, head_size))
    first_half = shaped[..., :half_size]
    second = shaped[..., half_size:]
    turned = jnp.concatenate(
        [first_half * cosine - second * sine_part, second * cosine + first_half * sine_part],
        axis=-1,
    )
    return turned.reshape(values.shape)


def doc_starts(lengths, positions):
    doc_ends = jnp.cumsum(lengths, axis=-1)
    before = (doc_ends[:, None, :] <= positions[None, :, None]).astype(jnp.int32)
    return jnp.sum(before * lengths[:, None, :], axis=-1)


def decay_mask(query_pos, key_pos, starts, head_count):
    distance = query_pos[:, None] - key_pos[None, :]
    allowed = (distance >= 0)[None, :, :] & (key_pos[None, None, :] >= starts[:, :, None])
    head_index = jnp.arange(head_count, dtype=jnp.float32)
    log_gamma = jnp.log(1.0 - jnp.exp2(-5.0 - head_index))
    decay_rate = jnp.exp(
        jnp.maximum(distance, 0).astype(jnp.float32)[None, :, :] * log_gamma[:, None, None]
    )
    return jnp.where(allowed[:, None, :, :], decay_rate[None, :, :, :], jnp.float32(0.0))


def project(left, weight):
    return jnp.einsum("bti,io->bto", left, weight, preferred_element_type=jnp.float32)


def project_back(grad_rows, weight):
    return jnp.einsum("bto,io->bti", grad_rows, weight, preferred_element_type=jnp.float32)


def weight_grad(left, grad_rows):
    return jnp.einsum("bti,bto->io", left, grad_rows, preferred_element_type=jnp.float32)


def on_device(
    inputs,
    out_cotangent,
    doc_lengths,
    ln1_gain,
    w_query,
    w_key,
    w_value,
    w_gate,
    w_out,
    ln2_gain,
    w_up,
    up_bias,
    w_down,
):
    fetched = (
        lax.all_gather(ln1_gain.astype(jnp.bfloat16), ("dp", "pb", "ka"), axis=0, tiled=True),
        lax.all_gather(w_query.astype(jnp.bfloat16), ("dp", "pb", "ka"), axis=0, tiled=True),
        lax.all_gather(w_key.astype(jnp.bfloat16), ("dp", "pb", "ka"), axis=0, tiled=True),
        lax.all_gather(w_value.astype(jnp.bfloat16), ("dp", "pb", "ka"), axis=0, tiled=True),
        lax.all_gather(w_gate.astype(jnp.bfloat16), ("dp", "pb", "ka"), axis=0, tiled=True),
        lax.all_gather(w_out.astype(jnp.bfloat16), ("dp", "pb", "ka"), axis=0, tiled=True),
        lax.all_gather(ln2_gain.astype(jnp.bfloat16), ("dp", "pb", "ka"), axis=0, tiled=True),
        lax.all_gather(w_up.astype(jnp.bfloat16), ("dp", "pb", "ka"), axis=0, tiled=True),
        lax.all_gather(up_bias.astype(jnp.bfloat16), ("dp", "pb", "ka"), axis=0, tiled=True),
        lax.all_gather(w_down.astype(jnp.bfloat16), ("dp", "pb", "ka"), axis=0, tiled=True),
    )
    (
        gain_one,
        weight_query,
        weight_key,
        weight_value,
        weight_gate,
        weight_out,
        gain_two,
        weight_up,
        bias_up,
        weight_down,
    ) = fetched
    batch_rows, piece_len, model_width = inputs.shape
    count_pb = lax.axis_size("pb")
    count_ka = lax.axis_size("ka")
    block_pb = lax.axis_index("pb")
    block_ka = lax.axis_index("ka")
    query_span = count_ka * piece_len
    key_span = count_pb * piece_len
    key_width = weight_query.shape[1] // H
    value_width = weight_value.shape[1] // H
    score_scale = key_width ** (-0.5)
    own_pos = (block_pb * count_ka + block_ka) * piece_len + jnp.arange(piece_len, dtype=jnp.int32)
    own_places = own_pos.astype(jnp.float32)
    query_pos = block_pb * query_span + jnp.arange(query_span, dtype=jnp.int32)
    key_pos = (
        (jnp.arange(count_pb, dtype=jnp.int32) * count_ka + block_ka)[:, None] * piece_len
        + jnp.arange(piece_len, dtype=jnp.int32)[None, :]
    ).reshape(key_span)
    starts = doc_starts(doc_lengths, query_pos)
    decay = decay_mask(query_pos, key_pos, starts, H)
    input_rows = inputs.astype(jnp.float32)
    gain_one_f = gain_one.astype(jnp.float32)
    normed_one = layer_norm(input_rows, gain_one_f).astype(jnp.bfloat16)
    query_pre = project(normed_one, weight_query)
    key_pre = project(normed_one, weight_key)
    value_pre = project(normed_one, weight_value)
    gate_pre = project(normed_one, weight_gate)
    query_rot = (xpos_turn(query_pre, own_places, H, XPOS_BASE, 1.0) * score_scale).astype(
        jnp.bfloat16
    )
    key_rot = xpos_turn(key_pre, own_places, H, XPOS_BASE, -1.0).astype(jnp.bfloat16)
    value_low = value_pre.astype(jnp.bfloat16)
    query_block = lax.all_gather(query_rot, "ka", axis=1, tiled=True)
    key_set, value_set = (
        lax.all_gather(key_rot, "pb", axis=1, tiled=True),
        lax.all_gather(value_low, "pb", axis=1, tiled=True),
    )
    query_heads = query_block.reshape(batch_rows, query_span, H, key_width)
    key_heads = key_set.reshape(batch_rows, key_span, H, key_width)
    value_heads = value_set.reshape(batch_rows, key_span, H, value_width)
    raw_scores = jnp.einsum(
        "bqhd,bkhd->bhqk", query_heads, key_heads, preferred_element_type=jnp.float32
    )
    scores = (raw_scores * decay).astype(jnp.bfloat16)
    partial_sum = jnp.einsum(
        "bhqk,bkhe->bqhe", scores, value_heads, preferred_element_type=jnp.float32
    ).reshape(batch_rows, query_span, H * value_width)
    retained = lax.psum_scatter(partial_sum, "ka", scatter_dimension=1, tiled=True)

    def mix_gate(gate_in, retained_in):
        return jax.nn.silu(gate_in) * group_norm(retained_in, H)

    gated = mix_gate(gate_pre, retained).astype(jnp.bfloat16)
    middle = input_rows + project(gated, weight_out)
    gain_two_f = gain_two.astype(jnp.float32)
    normed_two = layer_norm(middle, gain_two_f).astype(jnp.bfloat16)

    def gelu_exact(hidden):
        return jax.nn.gelu(hidden, approximate=False)

    up_pre = project(normed_two, weight_up) + bias_up.astype(jnp.float32)
    active = gelu_exact(up_pre).astype(jnp.bfloat16)
    output = (middle + project(active, weight_down)).astype(jnp.bfloat16)
    fetched = (
        lax.all_gather(ln1_gain.astype(jnp.bfloat16), ("dp", "pb", "ka"), axis=0, tiled=True),
        lax.all_gather(w_query.astype(jnp.bfloat16), ("dp", "pb", "ka"), axis=0, tiled=True),
        lax.all_gather(w_key.astype(jnp.bfloat16), ("dp", "pb", "ka"), axis=0, tiled=True),
        lax.all_gather(w_value.astype(jnp.bfloat16), ("dp", "pb", "ka"), axis=0, tiled=True),
        lax.all_gather(w_gate.astype(jnp.bfloat16), ("dp", "pb", "ka"), axis=0, tiled=True),
        lax.all_gather(w_out.astype(jnp.bfloat16), ("dp", "pb", "ka"), axis=0, tiled=True),
        lax.all_gather(ln2_gain.astype(jnp.bfloat16), ("dp", "pb", "ka"), axis=0, tiled=True),
        lax.all_gather(w_up.astype(jnp.bfloat16), ("dp", "pb", "ka"), axis=0, tiled=True),
        lax.all_gather(up_bias.astype(jnp.bfloat16), ("dp", "pb", "ka"), axis=0, tiled=True),
        lax.all_gather(w_down.astype(jnp.bfloat16), ("dp", "pb", "ka"), axis=0, tiled=True),
    )
    (
        gain_one,
        weight_query,
        weight_key,
        weight_value,
        weight_gate,
        weight_out,
        gain_two,
        weight_up,
        bias_up,
        weight_down,
    ) = fetched
    cotangent = out_cotangent.astype(jnp.float32)
    grad_down = weight_grad(active, out_cotangent)
    grad_active = project_back(out_cotangent, weight_down)
    unused_gelu, gelu_backward = jax.vjp(gelu_exact, up_pre)
    grad_up_pre = gelu_backward(grad_active)[0].astype(jnp.bfloat16)
    grad_up = weight_grad(normed_two, grad_up_pre)
    grad_bias = jnp.sum(grad_up_pre.astype(jnp.float32), axis=(0, 1))
    grad_normed_two = project_back(grad_up_pre, weight_up)
    unused_norm_two, norm_two_backward = jax.vjp(layer_norm, middle, gain_two.astype(jnp.float32))
    grad_middle_norm, grad_gain_two = norm_two_backward(grad_normed_two)
    grad_middle = cotangent + grad_middle_norm
    grad_attended = grad_middle.astype(jnp.bfloat16)
    grad_out = weight_grad(gated, grad_attended)
    grad_gated = project_back(grad_attended, weight_out)
    unused_mix, mix_backward = jax.vjp(mix_gate, gate_pre, retained)
    grad_gate_f, grad_retained_f = mix_backward(grad_gated)
    grad_gate_pre = grad_gate_f.astype(jnp.bfloat16)
    grad_retained = grad_retained_f.astype(jnp.bfloat16)
    grad_block = lax.all_gather(grad_retained, "ka", axis=1, tiled=True)
    grad_heads = grad_block.reshape(batch_rows, query_span, H, value_width)
    again_scores = jnp.einsum(
        "bqhd,bkhd->bhqk", query_heads, key_heads, preferred_element_type=jnp.float32
    )
    scores_low = (again_scores * decay).astype(jnp.bfloat16)
    grad_value_part = jnp.einsum(
        "bhqk,bqhe->bkhe", scores_low, grad_heads, preferred_element_type=jnp.float32
    ).reshape(batch_rows, key_span, H * value_width)
    grad_scores = (
        jnp.einsum("bqhe,bkhe->bhqk", grad_heads, value_heads, preferred_element_type=jnp.float32)
        * decay
    ).astype(jnp.bfloat16)
    grad_query_part = jnp.einsum(
        "bhqk,bkhd->bqhd", grad_scores, key_heads, preferred_element_type=jnp.float32
    ).reshape(batch_rows, query_span, H * key_width)
    grad_key_part = jnp.einsum(
        "bhqk,bqhd->bkhd", grad_scores, query_heads, preferred_element_type=jnp.float32
    ).reshape(batch_rows, key_span, H * key_width)
    grad_query_own = lax.psum_scatter(
        grad_query_part.astype(jnp.bfloat16), "ka", scatter_dimension=1, tiled=True
    ).astype(jnp.float32)
    grad_key_own, grad_value_own = (
        lax.psum_scatter(
            grad_key_part.astype(jnp.bfloat16), "pb", scatter_dimension=1, tiled=True
        ).astype(jnp.float32),
        lax.psum_scatter(
            grad_value_part.astype(jnp.bfloat16), "pb", scatter_dimension=1, tiled=True
        ).astype(jnp.float32),
    )
    unused_query, query_backward = jax.vjp(
        lambda query_in: xpos_turn(query_in, own_places, H, XPOS_BASE, 1.0) * score_scale, query_pre
    )
    unused_key, key_backward = jax.vjp(
        lambda key_in: xpos_turn(key_in, own_places, H, XPOS_BASE, -1.0), key_pre
    )
    grad_query_pre = query_backward(grad_query_own)[0].astype(jnp.bfloat16)
    grad_key_pre = key_backward(grad_key_own)[0].astype(jnp.bfloat16)
    grad_value_pre = grad_value_own.astype(jnp.bfloat16)
    grad_query = weight_grad(normed_one, grad_query_pre)
    grad_key = weight_grad(normed_one, grad_key_pre)
    grad_value = weight_grad(normed_one, grad_value_pre)
    grad_gate = weight_grad(normed_one, grad_gate_pre)
    grad_normed_one = (
        project_back(grad_query_pre, weight_query)
        + project_back(grad_key_pre, weight_key)
        + project_back(grad_value_pre, weight_value)
        + project_back(grad_gate_pre, weight_gate)
    )
    unused_norm_one, norm_one_backward = jax.vjp(
        layer_norm, input_rows, gain_one.astype(jnp.float32)
    )
    grad_input_norm, grad_gain_one = norm_one_backward(grad_normed_one)
    grad_inputs = grad_middle + grad_input_norm
    (
        shard_gain_one,
        shard_query,
        shard_key,
        shard_value,
        shard_gate,
        shard_out,
        shard_gain_two,
        shard_up,
        shard_bias,
        shard_down,
    ) = (
        lax.psum_scatter(grad_gain_one, ("dp", "pb", "ka"), scatter_dimension=0, tiled=True),
        lax.psum_scatter(grad_query, ("dp", "pb", "ka"), scatter_dimension=0, tiled=True),
        lax.psum_scatter(grad_key, ("dp", "pb", "ka"), scatter_dimension=0, tiled=True),
        lax.psum_scatter(grad_value, ("dp", "pb", "ka"), scatter_dimension=0, tiled=True),
        lax.psum_scatter(grad_gate, ("dp", "pb", "ka"), scatter_dimension=0, tiled=True),
        lax.psum_scatter(grad_out, ("dp", "pb", "ka"), scatter_dimension=0, tiled=True),
        lax.psum_scatter(grad_gain_two, ("dp", "pb", "ka"), scatter_dimension=0, tiled=True),
        lax.psum_scatter(grad_up, ("dp", "pb", "ka"), scatter_dimension=0, tiled=True),
        lax.psum_scatter(grad_bias, ("dp", "pb", "ka"), scatter_dimension=0, tiled=True),
        lax.psum_scatter(grad_down, ("dp", "pb", "ka"), scatter_dimension=0, tiled=True),
    )
    return (
        output,
        grad_inputs,
        shard_gain_one,
        shard_query,
        shard_key,
        shard_value,
        shard_gate,
        shard_out,
        shard_gain_two,
        shard_up,
        shard_bias,
        shard_down,
    )


def solution(mesh):
    return jax.shard_map(
        on_device,
        mesh=mesh,
        in_specs=(
            P("dp", ("pb", "ka"), None),
            P("dp", ("pb", "ka"), None),
            P("dp", None),
            P(("dp", "pb", "ka")),
            P(("dp", "pb", "ka"), None),
            P(("dp", "pb", "ka"), None),
            P(("dp", "pb", "ka"), None),
            P(("dp", "pb", "ka"), None),
            P(("dp", "pb", "ka"), None),
            P(("dp", "pb", "ka")),
            P(("dp", "pb", "ka"), None),
            P(("dp", "pb", "ka")),
            P(("dp", "pb", "ka"), None),
        ),
        out_specs=(
            P("dp", ("pb", "ka"), None),
            P("dp", ("pb", "ka"), None),
            P(("dp", "pb", "ka")),
            P(("dp", "pb", "ka"), None),
            P(("dp", "pb", "ka"), None),
            P(("dp", "pb", "ka"), None),
            P(("dp", "pb", "ka"), None),
            P(("dp", "pb", "ka"), None),
            P(("dp", "pb", "ka")),
            P(("dp", "pb", "ka"), None),
            P(("dp", "pb", "ka")),
            P(("dp", "pb", "ka"), None),
        ),
        check_vma=False,
    )
```

profile of v0, /device:TPU:2, one launch (start us, length us, event | category | flops | bytes accessed | tf_op | source)
XLA Modules:
  0.0 3831.6 jit_solution(9372803715858394031)
XLA Ops:
  13.7 41.8 %all-reduce.10 = (bf16[2048]{0:T(1024)(128)(2,1)S(1)}, bf16[2048]{0:T(1024)(128)(2,1)S(1)}) all-reduce(bf16[2048]{0:T(1024)(128)(2,1)S(1)} %dynamic-update-slice, bf16[2048]{0:T(1024)(128)(2,1)S(1)} %dynamic-update-slice.1), channel_id=1, replica_groups=mesh['dp'=2,'pb'=4,'ka'=4] {'dp','pb','ka'}, use_global_device_ids=true, to_apply=%add.4 | all-reduce | flops 4096 | bytes 16384
  56.6 33.7 all-gather.19.cloned.1.call-done
  99.3 70.6 %all-gather.23.cloned.1.call-done = bf16[2048,2048]{1,0:T(8,128)(2,1)} async-done(((bf16[64,2048]{1,0:T(8,128)(2,1)}), bf16[2048,2048]{1,0:T(8,128)(2,1)}) %all-gather.23.cloned.1.call-update) | async-done | bytes 8388624 | tf_op jit(solution)/shard_map/all_gather | solution.py:95
  178.9 107.7 %all-gather.15.cloned.1.call-done = bf16[2048,4096]{1,0:T(8,128)(2,1)} async-done(((bf16[64,4096]{1,0:T(8,128)(2,1)}), bf16[2048,4096]{1,0:T(8,128)(2,1)}) %all-gather.15.cloned.1.call-update) | async-done | bytes 16777232 | tf_op jit(solution)/shard_map/all_gather | solution.py:96
  286.6 11.7 fusion.39
  304.2 16.7 all-gather.21.cloned.1.call-done
  320.9 83.7 %all-gather.25.cloned.1.call-done = bf16[2,512,2048]{1,2,0:T(8,128)(2,1)} async-done(((bf16[2,128,2048]{1,2,0:T(8,128)(2,1)}), bf16[2,512,2048]{1,2,0:T(8,128)(2,1)}) %all-gather.25.cloned.1.call-update) | async-done | bytes 4194320 | tf_op jit(solution)/shard_map/all_gather | solution.py:149
  404.6 10.0 fusion
  414.6 139.9 %all-gather.17.cloned.1.call-done = bf16[2,512,4096]{2,1,0:T(8,128)(2,1)} async-done(((bf16[2,128,4096]{2,1,0:T(8,128)(2,1)}), bf16[2,512,4096]{2,1,0:T(8,128)(2,1)}) %all-gather.17.cloned.1.call-update) | async-done | bytes 8388624 | tf_op jit(solution)/shard_map/all_gather | solution.py:150
  554.5 12.9 fusion.22
  567.4 17.5 copy.166
  591.3 37.0 all-gather
  628.3 79.9 %reduce-scatter.16.cloned.1.call-done = f32[2,128,4096]{2,1,0:T(8,128)} async-done(((f32[2,512,4096]{2,1,0:T(8,128)}), f32[2,128,4096]{2,1,0:T(8,128)}) %reduce-scatter.16.cloned.1.call-update) | async-done | bytes 4194320 | tf_op jit(solution)/shard_map/reduce_scatter | solution.py:162
  735.0 92.8 %all-gather.13.cloned.1.call-done = bf16[2048,4096]{1,0:T(8,128)(2,1)} async-done(((bf16[64,4096]{1,0:T(8,128)(2,1)}), bf16[2048,4096]{1,0:T(8,128)(2,1)}) %all-gather.13.cloned.1.call-update) | async-done | bytes 16777232 | tf_op jit(solution)/shard_map/all_gather | solution.py:97
  827.9 16.6 multiply_convert_fusion.1
  844.5 100.3 %all-gather.27.cloned.1.call-done = bf16[4096,2048]{1,0:T(8,128)(2,1)} async-done(((bf16[128,2048]{1,0:T(8,128)(2,1)}), bf16[4096,2048]{1,0:T(8,128)(2,1)}) %all-gather.27.cloned.1.call-update) | async-done | bytes 16777232 | tf_op jit(solution)/shard_map/all_gather | solution.py:98
  954.0 107.5 %all-gather.29.cloned.1.call-done = bf16[2048,4096]{1,0:T(8,128)(2,1)} async-done(((bf16[64,4096]{1,0:T(8,128)(2,1)}), bf16[2048,4096]{1,0:T(8,128)(2,1)}) %all-gather.29.cloned.1.call-update) | async-done | bytes 16777232 | tf_op jit(solution)/shard_map/all_gather | solution.py:100
  1061.5 15.1 fusion.91
  1076.6 101.9 %all-gather.31.cloned.1.call-done = bf16[4096,2048]{1,0:T(8,128)(2,1)} async-done(((bf16[128,2048]{1,0:T(8,128)(2,1)}), bf16[4096,2048]{1,0:T(8,128)(2,1)}) %all-gather.31.cloned.1.call-update) | async-done | bytes 16777232 | tf_op jit(solution)/shard_map/all_gather | solution.py:102
  1178.5 20.4 convert_reduce_fusion
  1198.9 13.2 multiply_reduce_fusion.1
  1216.1 12.5 fusion.93
  1254.6 10.5 fusion.44
  1265.2 55.7 %all-gather.33.cloned.1.call-done = bf16[2,512,4096]{2,1,0:T(8,128)(2,1)} async-done(((bf16[2,128,4096]{2,1,0:T(8,128)(2,1)}), bf16[2,512,4096]{2,1,0:T(8,128)(2,1)}) %all-gather.33.cloned.1.call-update) | async-done | bytes 8388624 | tf_op jit(solution)/shard_map/all_gather | solution.py:220
  1320.9 12.4 copy.175
  1333.2 13.4 fusion.1
  1355.6 11.4 copy.167
  1382.8 11.7 copy.169
  1401.1 13.6 convolution_convert_fusion
  1414.7 11.5 copy.149
  1445.3 53.1 %reduce-scatter.36.cloned.1.call-done = bf16[128,4096]{1,0:T(8,128)(2,1)} async-done(((bf16[512,4096]{1,0:T(8,128)(2,1)}), bf16[128,4096]{1,0:T(8,128)(2,1)}) %reduce-scatter.36.cloned.1.call-update) | async-done | bytes 1048592
  1523.4 14.9 convolution_bitcast_fusion.3
  1538.4 14.8 convolution_bitcast_fusion.2
  1554.9 15.6 convolution_bitcast_fusion.1
  1570.7 21.6 convolution_bitcast_fusion
  1592.4 53.4 %reduce-scatter.18.cloned.1.call-done = bf16[2,128,4096]{2,1,0:T(8,128)(2,1)} async-done(((bf16[2,512,4096]{2,1,0:T(8,128)(2,1)}), bf16[2,128,4096]{2,1,0:T(8,128)(2,1)}) %reduce-scatter.18.cloned.1.call-update) | async-done | bytes 2097168 | tf_op jit(solution)/shard_map/reduce_scatter | solution.py:246
  1645.7 15.5 convolution_bitcast_fusion.4
  1661.3 12.4 fusion.18
  1673.7 18.0 fusion.78
  1699.1 9.6 fusion.14
  1718.2 46.9 %all-reduce.9 = (f32[2048]{0:T(1024)S(1)}, f32[2048]{0:T(1024)S(1)}, f32[4096]{0:T(1024)S(1)}) all-reduce(f32[2048]{0:T(1024)S(1)} %get-tuple-element.16, f32[2048]{0:T(1024)S(1)} %copy-done.44, f32[4096]{0:T(1024)S(1)} %copy-done.39), channel_id=6, replica_groups=mesh['dp'=2,'pb'=4,'ka'=4] {'dp','pb','ka'}, use_global_device_ids=true, to_apply=%region_19.20.clone | all-reduce | flops 8192 | bytes 65536
  1771.0 62.4 %reduce-scatter.20.cloned.1.call-done = f32[64,2048]{1,0:T(8,128)} async-done(((f32[2048,2048]{1,0:T(8,128)}), f32[64,2048]{1,0:T(8,128)}) %reduce-scatter.20.cloned.1.call-update) | async-done | bytes 524304 | tf_op jit(solution)/shard_map/reduce_scatter | solution.py:287
  1833.4 187.1 %reduce-scatter.22.cloned.1.call-done = f32[64,2048]{1,0:T(8,128)} async-done(((f32[2048,2048]{1,0:T(8,128)}), f32[64,2048]{1,0:T(8,128)}) %reduce-scatter.22.cloned.1.call-update) | async-done | bytes 524304 | tf_op jit(solution)/shard_map/reduce_scatter | solution.py:288
  2020.5 361.5 %reduce-scatter.26.cloned.1.call-done = f32[64,4096]{1,0:T(8,128)} async-done(((f32[2048,4096]{1,0:T(8,128)}), f32[64,4096]{1,0:T(8,128)}) %reduce-scatter.26.cloned.1.call-update) | async-done | bytes 1048592 | tf_op jit(solution)/shard_map/reduce_scatter | solution.py:290
  2382.0 360.6 %reduce-scatter.28.cloned.1.call-done = f32[128,2048]{1,0:T(8,128)} async-done(((f32[4096,2048]{1,0:T(8,128)}), f32[128,2048]{1,0:T(8,128)}) %reduce-scatter.28.cloned.1.call-update) | async-done | bytes 1048592 | tf_op jit(solution)/shard_map/reduce_scatter | solution.py:291
  2742.6 360.5 %reduce-scatter.30.cloned.1.call-done = f32[64,4096]{1,0:T(8,128)} async-done(((f32[2048,4096]{1,0:T(8,128)}), f32[64,4096]{1,0:T(8,128)}) %reduce-scatter.30.cloned.1.call-update) | async-done | bytes 1048592 | tf_op jit(solution)/shard_map/reduce_scatter | solution.py:293
  3103.1 360.8 %reduce-scatter.32.cloned.1.call-done = f32[128,2048]{1,0:T(8,128)} async-done(((f32[4096,2048]{1,0:T(8,128)}), f32[128,2048]{1,0:T(8,128)}) %reduce-scatter.32.cloned.1.call-update) | async-done | bytes 1048592 | tf_op jit(solution)/shard_map/reduce_scatter | solution.py:295
  3463.9 360.6 %reduce-scatter.24.cloned.1.call-done = f32[64,4096]{1,0:T(8,128)} async-done(((f32[2048,4096]{1,0:T(8,128)}), f32[64,4096]{1,0:T(8,128)}) %reduce-scatter.24.cloned.1.call-update) | async-done | bytes 1048592 | tf_op jit(solution)/shard_map/reduce_scatter | solution.py:289
  (254 shorter events, 203.2 us)
Async XLA Ops:
  7.2 48.3 %copy-start.2 = (bf16[2,128,2048]{2,1,0:T(8,128)(2,1)S(1)}, bf16[2,128,2048]{2,1,0:T(8,128)(2,1)}, u32[]{:S(2)}) copy-start(bf16[2,128,2048]{2,1,0:T(8,128)(2,1)} %param.13) | copy-start | bytes 3145732
  7.2 83.1 %all-gather.19.cloned.1.call-start = ((), (), s32[]{:S(2)}) async-start(), calls=%async_computation.14 | async-start | bytes 8650752 | tf_op jit(solution)/shard_map/all_gather | solution.py:94
  9.1 160.7 %all-gather.23.cloned.1.call-start = ((), (), s32[]{:S(2)}) async-start(), calls=%async_computation.16 | async-start | bytes 8650752 | tf_op jit(solution)/shard_map/all_gather | solution.py:95
  11.0 275.6 %all-gather.15.cloned.1.call-start = ((), (), s32[]{:S(2)}) async-start(), calls=%async_computation.12 | async-start | bytes 17301504 | tf_op jit(solution)/shard_map/all_gather | solution.py:96
  13.1 307.8 %all-gather.21.cloned.1.call-start = ((), (), s32[]{:S(2)}) async-start(), calls=%async_computation.15 | async-start | bytes 5242880 | tf_op jit(solution)/shard_map/all_gather | solution.py:147
  55.5 772.4 %copy-start.16 = (f32[2048]{0:T(1024)}, f32[2048]{0:T(1024)S(1)}, u32[]{:S(2)}) copy-start(f32[2048]{0:T(1024)S(1)} %convert_element_type.174) | copy-start | bytes 24580
  55.8 772.1 %copy-start.29 = (f32[2,128]{1,0:T(2,128)}, f32[2,128]{1,0:T(2,128)S(1)}, u32[]{:S(2)}) copy-start(f32[2,128]{1,0:T(2,128)S(1)} %broadcast_multiply_fusion.2) | copy-start | bytes 3076
  56.2 39.9 %copy-start.42 = (f32[2,128]{1,0:T(2,128)}, f32[2,128]{1,0:T(2,128)S(1)}, u32[]{:S(2)}) copy-start(f32[2,128]{1,0:T(2,128)S(1)} %fusion.85) | copy-start | bytes 3076
  56.2 771.6 %copy-start.33 = (f32[2,128]{1,0:T(2,128)}, f32[2,128]{1,0:T(2,128)S(1)}, u32[]{:S(2)}) copy-start(f32[2,128]{1,0:T(2,128)S(1)} %fusion.99) | copy-start | bytes 3076
  56.6 40.5 %copy-start.21 = (f32[128,128]{1,0:T(8,128)}, f32[128,128]{1,0:T(8,128)S(1)}, u32[]{:S(2)}) copy-start(f32[128,128]{1,0:T(8,128)S(1)} %get-tuple-element.46) | copy-start | bytes 196612
  56.6 40.4 %copy-start.23 = (f32[128,128]{1,0:T(8,128)}, f32[128,128]{1,0:T(8,128)S(1)}, u32[]{:S(2)}) copy-start(f32[128,128]{1,0:T(8,128)S(1)} %get-tuple-element.47) | copy-start | bytes 196612
  56.6 119.9 %copy-start.25 = (f32[128,128]{1,0:T(8,128)}, f32[128,128]{1,0:T(8,128)S(1)}, u32[]{:S(2)}) copy-start(f32[128,128]{1,0:T(8,128)S(1)} %get-tuple-element.42) | copy-start | bytes 196612
  56.6 119.9 %copy-start.27 = (f32[128,128]{1,0:T(8,128)}, f32[128,128]{1,0:T(8,128)S(1)}, u32[]{:S(2)}) copy-start(f32[128,128]{1,0:T(8,128)S(1)} %get-tuple-element.43) | copy-start | bytes 196612
  99.2 305.4 %all-gather.25.cloned.1.call-start = ((), (), s32[]{:S(2)}) async-start(), calls=%async_computation.17 | async-start | bytes 5242880 | tf_op jit(solution)/shard_map/all_gather | solution.py:149
  178.7 119.7 %copy-start.45 = (s32[2,4]{1,0:T(2,128)S(1)}, s32[2,4]{1,0:T(2,128)}, u32[]{:S(2)}) copy-start(s32[2,4]{1,0:T(2,128)} %param.15) | copy-start | bytes 100
  178.7 375.8 %all-gather.17.cloned.1.call-start = ((), (), s32[]{:S(2)}) async-start(), calls=%async_computation.13 | async-start | bytes 10485760 | tf_op jit(solution)/shard_map/all_gather | solution.py:150
  298.3 409.9 %reduce-scatter.16.cloned.1.call-start = ((), (), s32[]{:S(2)}) async-start(), calls=%async_computation.18 | async-start | bytes 20971520 | tf_op jit(solution)/shard_map/reduce_scatter | solution.py:162
  299.5 105.2 %copy-start.10 = (pred[2,512,512]{2,1,0:T(8,128)(4,1)}, pred[2,512,512]{2,1,0:T(8,128)(4,1)S(1)}, u32[]{:S(2)}) copy-start(pred[2,512,512]{2,1,0:T(8,128)(4,1)S(1)} %compare_and_fusion) | copy-start | bytes 1572868
  584.9 243.0 %all-gather.13.cloned.1.call-start = ((), (), s32[]{:S(2)}) async-start(), calls=%async_computation.11 | async-start | bytes 17301504 | tf_op jit(solution)/shard_map/all_gather | solution.py:97
  586.9 357.8 %all-gather.27.cloned.1.call-start = ((), (), s32[]{:S(2)}) async-start(), calls=%async_computation.19 | async-start | bytes 17301504 | tf_op jit(solution)/shard_map/all_gather | solution.py:98
  587.9 473.6 %all-gather.29.cloned.1.call-start = ((), (), s32[]{:S(2)}) async-start(), calls=%async_computation.20 | async-start | bytes 17301504 | tf_op jit(solution)/shard_map/all_gather | solution.py:100
  590.3 588.2 %all-gather.31.cloned.1.call-start = ((), (), s32[]{:S(2)}) async-start(), calls=%async_computation.21 | async-start | bytes 17301504 | tf_op jit(solution)/shard_map/all_gather | solution.py:102
  591.2 729.6 %all-gather.33.cloned.1.call-start = ((), (), s32[]{:S(2)}) async-start(), calls=%async_computation.22 | async-start | bytes 10485760 | tf_op jit(solution)/shard_map/all_gather | solution.py:220
  628.3 583.8 %copy-start.31 = (f32[2048]{0:T(1024)}, f32[2048]{0:T(1024)S(1)}, u32[]{:S(2)}) copy-start(f32[2048]{0:T(1024)S(1)} %convert_element_type.190) | copy-start | bytes 24580
  953.6 258.5 %copy-start.5 = (f32[2,128,2048]{2,1,0:T(8,128)}, f32[2,128,2048]{2,1,0:T(8,128)S(1)}, u32[]{:S(2)}) copy-start(f32[2,128,2048]{2,1,0:T(8,128)S(1)} %get-tuple-element.50) | copy-start | bytes 6291460
  953.6 258.5 %copy-start.35 = (f32[2,128]{1,0:T(2,128)}, f32[2,128]{1,0:T(2,128)S(1)}, u32[]{:S(2)}) copy-start(f32[2,128]{1,0:T(2,128)S(1)} %broadcast_multiply_fusion.1) | copy-start | bytes 3076
  954.0 258.1 %copy-start.37 = (f32[2,128]{1,0:T(2,128)}, f32[2,128]{1,0:T(2,128)S(1)}, u32[]{:S(2)}) copy-start(f32[2,128]{1,0:T(2,128)S(1)} %fusion.100) | copy-start | bytes 3076
  1061.5 116.9 %copy-start.12 = (bf16[2,128,2048]{2,1,0:T(8,128)(2,1)S(1)}, bf16[2,128,2048]{2,1,0:T(8,128)(2,1)}, u32[]{:S(2)}) copy-start(bf16[2,128,2048]{2,1,0:T(8,128)(2,1)} %param.14) | copy-start | bytes 3145732
  1214.4 14.2 copy-start.40
  1265.1 68.1 %copy-start.11 = (pred[2,512,512]{2,1,0:T(8,128)(4,1)S(1)}, pred[2,512,512]{2,1,0:T(8,128)(4,1)}, u32[]{:S(2)}) copy-start(pred[2,512,512]{2,1,0:T(8,128)(4,1)} %copy-done.10) | copy-start | bytes 1572868
  1265.1 161.2 %reduce-scatter.34.cloned.1.call-start = ((), (), s32[]{:S(2)}) async-start(), calls=%async_computation.31 | async-start | bytes 5242880
  1373.7 124.7 %reduce-scatter.36.cloned.1.call-start = ((), (), s32[]{:S(2)}) async-start(), calls=%async_computation.32 | async-start | bytes 5242880
  1401.0 244.7 %reduce-scatter.18.cloned.1.call-start = ((), (), s32[]{:S(2)}) async-start(), calls=%async_computation.23 | async-start | bytes 10485760 | tf_op jit(solution)/shard_map/reduce_scatter | solution.py:246
  1426.2 407.1 %reduce-scatter.20.cloned.1.call-start = ((), (), s32[]{:S(2)}) async-start(), calls=%async_computation.24 | async-start | bytes 17301504 | tf_op jit(solution)/shard_map/reduce_scatter | solution.py:287
  1436.9 8.4 copy-start.9
  1445.3 575.2 %reduce-scatter.22.cloned.1.call-start = ((), (), s32[]{:S(2)}) async-start(), calls=%async_computation.25 | async-start | bytes 17301504 | tf_op jit(solution)/shard_map/reduce_scatter | solution.py:288
  1515.0 8.3 copy-start.13
  1523.4 858.6 %reduce-scatter.26.cloned.1.call-start = ((), (), s32[]{:S(2)}) async-start(), calls=%async_computation.27 | async-start | bytes 34603008 | tf_op jit(solution)/shard_map/reduce_scatter | solution.py:290
  1538.4 1204.2 %reduce-scatter.28.cloned.1.call-start = ((), (), s32[]{:S(2)}) async-start(), calls=%async_computation.28 | async-start | bytes 34603008 | tf_op jit(solution)/shard_map/reduce_scatter | solution.py:291
  1553.3 1549.8 %reduce-scatter.30.cloned.1.call-start = ((), (), s32[]{:S(2)}) async-start(), calls=%async_computation.29 | async-start | bytes 34603008 | tf_op jit(solution)/shard_map/reduce_scatter | solution.py:293
  1570.6 1893.3 %reduce-scatter.32.cloned.1.call-start = ((), (), s32[]{:S(2)}) async-start(), calls=%async_computation.30 | async-start | bytes 34603008 | tf_op jit(solution)/shard_map/reduce_scatter | solution.py:295
  1592.3 2232.2 %reduce-scatter.24.cloned.1.call-start = ((), (), s32[]{:S(2)}) async-start(), calls=%async_computation.26 | async-start | bytes 34603008 | tf_op jit(solution)/shard_map/reduce_scatter | solution.py:289
  1673.7 18.1 copy-start.14
  1691.7 7.4 copy-start.15
  1708.8 8.5 copy-start.43
  1708.8 9.4 copy-start.39
  1708.8 9.4 copy-start.44
  1708.8 58.1 %copy-start.41 = (f32[2,128]{1,0:T(2,128)S(1)}, f32[2,128]{1,0:T(2,128)}, u32[]{:S(2)}) copy-start(f32[2,128]{1,0:T(2,128)} %copy-done.40) | copy-start | bytes 3076
  (23 other events, 84.6 us)
Sparse Core Ops, SparseCore 0:
  11.5 78.8 all-gather.18
  93.8 76.0 all-gather.22
  173.3 113.2 all-gather.14
  288.6 32.2 all-gather.20
  322.9 81.7 all-gather.24
  406.6 147.8 all-gather.16
  585.0 123.1 reduce-scatter.15
  712.0 115.8 all-gather.12
  831.7 113.0 all-gather.26
  948.4 113.0 all-gather.28
  1065.3 113.0 all-gather.30
  1265.3 55.5 all-gather.32
  1373.8 44.4 reduce-scatter.33
  1420.5 77.9 reduce-scatter.35
  1500.7 144.9 reduce-scatter.17
  1648.6 184.7 reduce-scatter.19
  1836.2 184.2 reduce-scatter.21
  2023.3 358.6 reduce-scatter.25
  2385.0 357.6 reduce-scatter.27
  2745.4 357.6 reduce-scatter.29
  3106.1 357.8 reduce-scatter.31
  3466.9 357.6 reduce-scatter.23
where the time goes:
time: 3840 us; the launch traced here: 3830 us
  waiting for transfers between devices  3150 us (82%)
  matrix products  333 us (9%)
  local copies, waits for them, and re-layouts  155 us (4%)
  blocking collectives  126 us (3%)
  other arithmetic  51.1 us (1%)
    reduce_scatter x1, waiting for transfers between devices, on_device(): lax.psum_scatter(grad_gate, ('dp', 'pb', 'ka'), scatter_dimension=0, tile...  362 us
    reduce_scatter x1, waiting for transfers between devices, on_device(): lax.psum_scatter(grad_down, ('dp', 'pb', 'ka'), scatter_dimension=0, tile...  361 us
    reduce_scatter x1, waiting for transfers between devices, on_device(): lax.psum_scatter(grad_out, ('dp', 'pb', 'ka'), scatter_dimension=0, tiled...  361 us
    reduce_scatter x1, waiting for transfers between devices, on_device(): lax.psum_scatter(grad_value, ('dp', 'pb', 'ka'), scatter_dimension=0, til...  361 us
    reduce_scatter x1, waiting for transfers between devices, on_device(): lax.psum_scatter(grad_up, ('dp', 'pb', 'ka'), scatter_dimension=0, tiled=...  360 us
    reduce_scatter x1, waiting for transfers between devices, on_device(): lax.psum_scatter(grad_key, ('dp', 'pb', 'ka'), scatter_dimension=0, tiled...  187 us
    all_gather x1, waiting for transfers between devices, on_device(): lax.all_gather(value_low, 'pb', axis=1, tiled=True)  140 us
    all_gather x1, waiting for transfers between devices, on_device(): lax.all_gather(w_value.astype(jnp.bfloat16), ('dp', 'pb', 'ka'), axis=0,...  108 us
  transfers between devices with their start and end apart: 22, of which 21 were waited for; matrix products, arithmetic and copies ran while one was open for 9% of the time, Pallas kernels for 0%

commit v1 on v0

v1 whole, which is shorter than its diff:
```python
import functools
import math

import jax
import jax.numpy as jnp
import numpy as np
from jax import lax
from jax.experimental import pallas as pl
from jax.experimental.pallas import tpu as pltpu
from jax.sharding import Mesh
from jax.sharding import PartitionSpec as P

H = 8
XPOS_BASE = 512.0
EPSILON = 1e-05
MESH = pl.DeviceIdType.MESH
F32 = jnp.float32
BF16 = jnp.bfloat16

PLANE = ("dpl", "ka")
LINE = ("dph", "pb")


def plane_ids():
    row = lax.axis_index("dpl")
    col = lax.axis_index("ka")
    other_row = 1 - row
    across = lax.rem(col + 2, 4)
    sibling = col + 1 - 2 * lax.rem(col, 2)
    return row, col, other_row, across, sibling


def greet(targets):
    barrier = pltpu.get_barrier_semaphore()
    for target in targets:
        pl.semaphore_signal(barrier, inc=1, device_id=target, device_id_type=MESH)
    pl.semaphore_wait(barrier, len(targets))


def gather_kernel(shard, full, local_sem, send_sem, recv_sem):
    batch, length, _ = shard.shape
    half = length // 2
    row, col, other_row, across, sibling = plane_ids()
    to_x = {"ka": across}
    to_y = {"dpl": other_row}
    to_s = {"ka": sibling}

    def slot(r, c, start=0, size=length):
        return full.at[pl.ds(r * batch, batch), pl.ds(c * length + start, size), :]

    sent = []

    def send(src, dst, index, target):
        copy = pltpu.make_async_remote_copy(
            src_ref=src,
            dst_ref=dst,
            send_sem=send_sem.at[index],
            recv_sem=recv_sem.at[index],
            device_id=target,
            device_id_type=MESH,
        )
        copy.start()
        sent.append(copy)
        return copy

    greet((to_x, to_y, to_s))
    mine = pltpu.make_async_copy(shard, slot(row, col), local_sem)
    from_x = send(shard, slot(row, col), 0, to_x)
    from_y = send(shard, slot(row, col), 1, to_y)
    own_s = send(shard, slot(row, col), 2, to_s)
    mine.start()

    def onward(r, c, start, size, index, target):
        return send(slot(r, c, start, size), slot(r, c, start, size), index, target)

    from_x.wait_recv()
    diag_y = onward(row, across, 0, half, 3, to_y)
    relay_x = onward(row, across, 0, length, 4, to_s)
    from_y.wait_recv()
    diag_x = onward(other_row, col, half, half, 5, to_x)
    relay_y = onward(other_row, col, 0, length, 6, to_s)
    diag_y.wait_recv()
    relay_a = onward(other_row, across, 0, half, 7, to_s)
    diag_x.wait_recv()
    relay_b = onward(other_row, across, half, half, 8, to_s)
    for copy in (own_s, relay_x, relay_y, relay_a, relay_b):
        copy.wait_recv()
    for copy in sent:
        copy.wait_send()
    mine.wait()


def plane_gather(shard, collective_id):
    batch, length, width = shard.shape
    return pl.pallas_call(
        gather_kernel,
        out_shape=jax.ShapeDtypeStruct((2 * batch, 4 * length, width), shard.dtype),
        in_specs=[pl.BlockSpec(memory_space=pl.ANY)],
        out_specs=pl.BlockSpec(memory_space=pl.ANY),
        scratch_shapes=[
            pltpu.SemaphoreType.DMA,
            pltpu.SemaphoreType.DMA((9,)),
            pltpu.SemaphoreType.DMA((9,)),
        ],
        compiler_params=pltpu.CompilerParams(
            collective_id=collective_id, has_side_effects=True
        ),
        name="plane_gather",
    )(shard)


def scatter_kernel(
    part, total, own, sib, from_x, from_y, diag_a, diag_b, load_sem, send_sem, recv_sem
):
    batch, length, width = total.shape
    half = length // 2
    row, col, other_row, across, sibling = plane_ids()
    across_s = lax.rem(sibling + 2, 4)
    to_x = {"ka": across}
    to_y = {"dpl": other_row}
    to_s = {"ka": sibling}
    mine = ((other_row, across), (row, across), (other_row, col), (row, col))
    theirs = ((other_row, across_s), (row, across_s), (other_row, sibling), (row, sibling))

    def piece(r, c):
        return part.at[pl.ds(r * batch, batch), pl.ds(c * length, length), :]

    def send(src, dst, index, target):
        copy = pltpu.make_async_remote_copy(
            src_ref=src,
            dst_ref=dst,
            send_sem=send_sem.at[index],
            recv_sem=recv_sem.at[index],
            device_id=target,
            device_id_type=MESH,
        )
        copy.start()
        return copy

    loads = []
    for j in range(4):
        copy = pltpu.make_async_copy(piece(*mine[j]), own.at[j], load_sem.at[j])
        copy.start()
        loads.append(copy)
    greet((to_x, to_y, to_s))
    swaps = [send(piece(*theirs[j]), sib.at[j], j, to_s) for j in range(4)]

    step = 16

    def add(out_ref, refs, start, size):
        def body(i, carry):
            rows = pl.ds(start + i * step, step)
            value = refs[0][:, rows, :].astype(F32)
            for other in refs[1:]:
                value = value + other[:, rows, :].astype(F32)
            out_ref[:, rows, :] = value.astype(out_ref.dtype)
            return carry

        lax.fori_loop(0, size // step, body, 0)

    def add_at(out_ref, out_start, first, first_start, size):
        def body(i, carry):
            rows = pl.ds(out_start + i * step, step)
            value = out_ref[:, rows, :].astype(F32) + first[
                :, pl.ds(first_start + i * step, step), :
            ].astype(F32)
            out_ref[:, rows, :] = value.astype(out_ref.dtype)
            return carry

        lax.fori_loop(0, size // step, body, 0)

    lower, upper = pl.ds(0, half), pl.ds(half, half)

    def merge(j):
        loads[j].wait()
        swaps[j].wait_recv()
        add(own.at[j], (own.at[j], sib.at[j]), 0, length)

    merge(0)
    first_a = send(own.at[0, :, lower, :], diag_a, 4, to_x)
    first_b = send(own.at[0, :, upper, :], diag_b, 5, to_y)
    merge(1)
    x_lower = send(own.at[1, :, lower, :], from_x.at[:, lower, :], 6, to_x)
    merge(2)
    y_upper = send(own.at[2, :, upper, :], from_y.at[:, upper, :], 7, to_y)
    first_b.wait_recv()
    add_at(own.at[1], half, diag_b, 0, half)
    x_upper = send(own.at[1, :, upper, :], from_x.at[:, upper, :], 8, to_x)
    first_a.wait_recv()
    add_at(own.at[2], 0, diag_a, 0, half)
    y_lower = send(own.at[2, :, lower, :], from_y.at[:, lower, :], 9, to_y)
    merge(3)
    x_lower.wait_recv()
    y_lower.wait_recv()
    add(total, (own.at[3], from_x, from_y), 0, half)
    y_upper.wait_recv()
    x_upper.wait_recv()
    add(total, (own.at[3], from_x, from_y), half, half)
    for copy in swaps:
        copy.wait_send()
    for copy in (first_a, first_b, x_lower, x_upper, y_lower, y_upper):
        copy.wait_send()


def plane_scatter(part, collective_id):
    batch, length, width = part.shape[0] // 2, part.shape[1] // 4, part.shape[2]
    shape = (batch, length, width)
    return pl.pallas_call(
        scatter_kernel,
        out_shape=jax.ShapeDtypeStruct(shape, F32),
        in_specs=[pl.BlockSpec(memory_space=pl.ANY)],
        out_specs=pl.BlockSpec(memory_space=pltpu.VMEM),
        scratch_shapes=[
            pltpu.VMEM((4,) + shape, BF16),
            pltpu.VMEM((4,) + shape, BF16),
            pltpu.VMEM(shape, BF16),
            pltpu.VMEM(shape, BF16),
            pltpu.VMEM((batch, length // 2, width), BF16),
            pltpu.VMEM((batch, length // 2, width), BF16),
            pltpu.SemaphoreType.DMA((4,)),
            pltpu.SemaphoreType.DMA((10,)),
            pltpu.SemaphoreType.DMA((10,)),
        ],
        compiler_params=pltpu.CompilerParams(
            collective_id=collective_id,
            has_side_effects=True,
            vmem_limit_bytes=40 * 1024 * 1024,
        ),
        name="plane_scatter",
    )(part)


def scan_kernel(count, forward, state, coef, total, message, landed, send_sem, recv_sem):
    place = lax.axis_index("pb")
    if not forward:
        place = count - 1 - place
    rows = state.shape[0]
    has_prev = place > 0
    has_next = place < count - 1
    step = 1 if forward else -1
    here = lax.axis_index("pb")
    barrier = pltpu.get_barrier_semaphore()

    @pl.when(has_prev)
    def _():
        pl.semaphore_signal(barrier, inc=1, device_id={"pb": here - step}, device_id_type=MESH)

    @pl.when(has_next)
    def _():
        pl.semaphore_signal(barrier, inc=1, device_id={"pb": here + step}, device_id_type=MESH)

    pl.semaphore_wait(barrier, has_prev.astype(jnp.int32) + has_next.astype(jnp.int32))

    def hop(s):
        return pltpu.make_async_remote_copy(
            src_ref=message.at[s],
            dst_ref=landed.at[s],
            send_sem=send_sem.at[s],
            recv_sem=recv_sem.at[s],
            device_id={"pb": here + step},
            device_id_type=MESH,
        )

    for s in range(rows):

        @pl.when(has_prev)
        def _():
            hop(s).wait_recv()
            total[s] = (coef[0, s] * landed[s].astype(F32)).astype(BF16)

        @pl.when(jnp.logical_not(has_prev))
        def _():
            total[s] = jnp.zeros(total.shape[1:], BF16)

        @pl.when(has_next)
        def _():
            message[s] = (state[s] + coef[1, s] * total[s].astype(F32)).astype(BF16)
            hop(s).start()

    @pl.when(has_next)
    def _():
        for s in range(rows):
            hop(s).wait_send()


def line_scan(state, coef, count, forward, collective_id):
    return pl.pallas_call(
        functools.partial(scan_kernel, count, forward),
        out_shape=jax.ShapeDtypeStruct(state.shape, BF16),
        in_specs=[
            pl.BlockSpec(memory_space=pltpu.VMEM),
            pl.BlockSpec(memory_space=pltpu.SMEM),
        ],
        out_specs=pl.BlockSpec(memory_space=pltpu.VMEM),
        scratch_shapes=[
            pltpu.VMEM(state.shape, BF16),
            pltpu.VMEM(state.shape, BF16),
            pltpu.SemaphoreType.DMA((state.shape[0],)),
            pltpu.SemaphoreType.DMA((state.shape[0],)),
        ],
        compiler_params=pltpu.CompilerParams(
            collective_id=collective_id,
            has_side_effects=True,
            vmem_limit_bytes=24 * 1024 * 1024,
        ),
        name="line_scan",
    )(state, coef)


def normalize(values):
    mean = jnp.mean(values, axis=-1, keepdims=True)
    centered = values - mean
    inv = lax.rsqrt(jnp.mean(centered * centered, axis=-1, keepdims=True) + EPSILON)
    return centered * inv, inv


def normalize_back(normed, inv, grad):
    mean = jnp.mean(grad, axis=-1, keepdims=True)
    along = jnp.mean(grad * normed, axis=-1, keepdims=True)
    return inv * (grad - mean - normed * along)


def turn_tables(positions, half, direction):
    pair = jnp.arange(half, dtype=F32)
    frequency = jnp.exp(-jnp.log(10000.0) * pair / half)
    zeta = (pair / half + 0.4) / 1.4
    angles = positions[:, None] * frequency[None, :]
    factor = jnp.exp(direction * positions[:, None] / XPOS_BASE * jnp.log(zeta)[None, :])
    return jnp.cos(angles) * factor, jnp.sin(angles) * factor


def turn(values, tables):
    cosine, sine = tables
    half = values.shape[-1] // 2
    first, second = values[..., :half], values[..., half:]
    return jnp.concatenate(
        [first * cosine - second * sine, second * cosine + first * sine], axis=-1
    )


def turn_back(values, tables):
    cosine, sine = tables
    return turn(values, (cosine, -sine))


def mm(left, right):
    return jnp.einsum("sti,io->sto", left, right, preferred_element_type=F32)


def mm_back(left, right):
    return jnp.einsum("sto,io->sti", left, right, preferred_element_type=F32)


def mm_grad(left, right):
    return jnp.einsum("sti,sto->io", left, right, preferred_element_type=F32)


def on_device(
    inputs,
    out_cotangent,
    doc_lengths,
    ln1_gain,
    w_query,
    w_key,
    w_value,
    w_gate,
    w_out,
    ln2_gain,
    w_up,
    up_bias,
    w_down,
):
    n_dph, n_dpl, n_pb, n_ka = (lax.axis_size(a) for a in ("dph", "dpl", "pb", "ka"))
    at_dpl, at_pb, at_ka = (lax.axis_index(a) for a in ("dpl", "pb", "ka"))
    batch, length, width = inputs.shape
    span = n_ka * length
    rows = w_query.shape[0]
    wide_rows = w_down.shape[0]
    key_width = w_query.shape[1] // H
    value_width = w_value.shape[1] // H
    units = n_dph * n_pb * wide_rows
    group = n_dpl * n_ka
    heads_pb = H // (n_dpl * n_dph)

    def to_inner(values):
        lead = values.shape[:-1]
        cut = values.reshape(lead + (n_dph, n_dpl, n_pb, n_ka * rows))
        return jnp.swapaxes(cut, -3, -2).reshape(values.shape)

    def to_outer(values):
        lead = values.shape[:-1]
        cut = values.reshape(lead + (n_dph, n_pb, n_dpl, n_ka * rows))
        return jnp.swapaxes(cut, -3, -2).reshape(values.shape)

    def by_head(weight):
        cut = weight.reshape(rows, H // (n_dpl * heads_pb), n_dpl, heads_pb, -1)
        return jnp.swapaxes(cut, 1, 2).reshape(rows, group, -1)

    def from_head(values):
        cut = values.reshape(rows, n_dpl, H // (n_dpl * heads_pb), heads_pb, -1)
        return jnp.swapaxes(cut, 1, 2).reshape(rows, -1)

    def by_unit(weight):
        cut = weight.reshape(rows, n_dph, n_dpl, n_pb, n_ka, wide_rows)
        return jnp.transpose(cut, (0, 2, 4, 1, 3, 5)).reshape(rows, group, units)

    def from_unit(values):
        cut = values.reshape(rows, n_dpl, n_ka, n_dph, n_pb, wide_rows)
        return jnp.transpose(cut, (0, 3, 1, 4, 2, 5)).reshape(rows, -1)

    def swap_plane(values):
        return lax.all_to_all(values, PLANE, split_axis=1, concat_axis=0, tiled=True).reshape(
            group * rows, -1
        )

    def swap_plane_back(values):
        cut = values.reshape(group * rows, 1, -1)
        return lax.all_to_all(cut, PLANE, split_axis=0, concat_axis=1, tiled=True)

    def gather_line(values):
        return lax.all_gather(values, LINE, axis=0, tiled=True)

    def scatter_line(values):
        return lax.psum_scatter(values, LINE, scatter_dimension=0, tiled=True)

    gain_one = ln1_gain.astype(BF16).astype(F32)[:, None]
    gain_two = ln2_gain.astype(BF16).astype(F32)[:, None]
    firsts = [w.astype(BF16) for w in (w_query, w_key, w_value, w_gate)]
    up_low = w_up.astype(BF16)

    def scaled(weight, gain):
        return (weight.astype(F32) * gain).astype(BF16)

    first_pack = jnp.concatenate([by_head(scaled(w, gain_one)) for w in firsts], axis=-1)
    weight_first = gather_line(swap_plane(first_pack))
    weight_out_rows = gather_line(to_inner(w_out.astype(BF16)))
    weight_out = lax.all_to_all(weight_out_rows, "ka", split_axis=0, concat_axis=0, tiled=True)
    weight_out = (
        weight_out.reshape(n_ka, n_pb // heads_pb, wide_rows, width)
        .swapaxes(0, 1)
        .reshape(value_width, width)
    )
    weight_up = gather_line(swap_plane(by_unit(scaled(up_low, gain_two))))
    down_pack = jnp.concatenate(
        [
            to_inner(w_down.astype(BF16)),
            jnp.broadcast_to(up_bias.astype(BF16)[:, None], (wide_rows, 128)),
        ],
        axis=-1,
    )
    down_pack = gather_line(down_pack)
    weight_down = down_pack[:, :width]
    bias_up = down_pack[:, width].astype(F32)

    head = (
        (at_ka // heads_pb) * (n_dpl * heads_pb) + at_dpl * heads_pb + at_ka % heads_pb
    ).astype(F32)
    log_gamma = jnp.log(1.0 - jnp.exp2(-5.0 - head))
    offsets = jnp.arange(span, dtype=jnp.int32)
    places = (at_pb * span + offsets).astype(F32)
    tables_q = turn_tables(places, key_width // 2, 1.0)
    tables_k = turn_tables(places, key_width // 2, -1.0)
    distance = offsets[:, None] - offsets[None, :]
    decay = jnp.where(
        distance >= 0, jnp.exp(jnp.maximum(distance, 0).astype(F32) * log_gamma), 0.0
    )
    decay_in = jnp.exp(offsets.astype(F32) * log_gamma)[:, None]
    decay_out = jnp.exp((span - offsets).astype(F32) * log_gamma)[:, None]
    decay_span = jnp.exp(span * log_gamma)
    lengths = lax.all_gather(doc_lengths, "dpl", axis=0, tiled=True)
    ends = jnp.cumsum(lengths, axis=-1)
    edge = at_pb * span

    def goes_on(start):
        return jnp.all(ends != start, axis=-1).astype(F32)

    coef_forward = jnp.stack([goes_on(edge), jnp.full((n_dpl * batch,), decay_span)])
    coef_backward = jnp.stack([goes_on(edge + span), jnp.full((n_dpl * batch,), decay_span)])

    rows_in = to_inner(inputs).astype(F32)
    rows_cot = to_inner(out_cotangent)
    normed_one, inv_one = normalize(rows_in)
    normed_one_all = plane_gather(normed_one.astype(BF16), 0)
    cot_all = plane_gather(rows_cot, 1)
    first = mm(normed_one_all, weight_first)
    query_pre = first[..., :key_width]
    key_pre = first[..., key_width : 2 * key_width]
    value = first[..., 2 * key_width : 2 * key_width + value_width].astype(BF16)
    gate = first[..., 2 * key_width + value_width :]
    scale = key_width ** (-0.5)
    query = (turn(query_pre, tables_q) * scale).astype(BF16)
    key = turn(key_pre, tables_k).astype(BF16)
    key_out = (key.astype(F32) * decay_out).astype(BF16)
    state = jnp.einsum("smd,sme->sde", key_out, value, preferred_element_type=F32)
    carried = line_scan(state, coef_forward, n_pb, True, 2)
    raw = jnp.einsum("snd,smd->snm", query, key, preferred_element_type=F32)
    scores = (raw * decay).astype(BF16)
    retained = jnp.einsum("snm,sme->sne", scores, value, preferred_element_type=F32)
    retained = retained + decay_in * jnp.einsum(
        "snd,sde->sne", query, carried, preferred_element_type=F32
    )
    normed_ret, inv_ret = normalize(retained)
    opened = jax.nn.sigmoid(gate)
    silu = gate * opened
    gated = (silu * normed_ret).astype(BF16)
    attended = plane_scatter(mm(gated, weight_out).astype(BF16), 3)
    middle = rows_in + attended
    normed_two, inv_two = normalize(middle)
    normed_two_all = plane_gather(normed_two.astype(BF16), 4)
    up_pre = mm(normed_two_all, weight_up) + bias_up
    bell = 0.5 * (1.0 + lax.erf(up_pre * np.float32(math.sqrt(0.5))))
    active = (up_pre * bell).astype(BF16)

    slope = bell + up_pre * (
        jnp.exp(-0.5 * up_pre * up_pre) * np.float32(1.0 / math.sqrt(2.0 * math.pi))
    )
    grad_up_pre = (mm_back(cot_all, weight_down) * slope).astype(BF16)
    normed_two_back = plane_scatter(mm_back(grad_up_pre, weight_up).astype(BF16), 5)
    grad_middle = rows_cot.astype(F32) + normalize_back(normed_two, inv_two, normed_two_back)
    grad_down = mm_grad(active, cot_all).astype(BF16)
    grad_bias = jnp.sum(grad_up_pre.astype(F32), axis=(0, 1)).astype(BF16)
    grad_down = scatter_line(
        jnp.concatenate(
            [grad_down, jnp.broadcast_to(grad_bias[:, None], (units, 128))], axis=-1
        )
    )
    grad_up = scatter_line(mm_grad(normed_two_all, grad_up_pre).astype(BF16))
    grad_mid_all = plane_gather(grad_middle.astype(BF16), 6)
    grad_gated = mm_back(grad_mid_all, weight_out)
    grad_gate = (grad_gated * normed_ret * (opened + silu * (1.0 - opened))).astype(BF16)
    grad_ret = normalize_back(normed_ret, inv_ret, grad_gated * silu).astype(BF16)
    query_in = (query.astype(F32) * decay_in).astype(BF16)
    grad_state = jnp.einsum("snd,sne->sde", query_in, grad_ret, preferred_element_type=F32)
    grad_carried = line_scan(grad_state, coef_backward, n_pb, False, 7)
    grad_out = mm_grad(gated, grad_mid_all).astype(BF16)
    grad_gate_w = scatter_line(mm_grad(normed_one_all, grad_gate).astype(BF16))
    grad_scores = (
        jnp.einsum("sne,sme->snm", grad_ret, value, preferred_element_type=F32) * decay
    ).astype(BF16)
    grad_query = jnp.einsum("snm,smd->snd", grad_scores, key, preferred_element_type=F32)
    grad_query = grad_query + decay_in * jnp.einsum(
        "sne,sde->snd", grad_ret, carried, preferred_element_type=F32
    )
    grad_key = jnp.einsum("snm,snd->smd", grad_scores, query, preferred_element_type=F32)
    grad_key = grad_key + decay_out * jnp.einsum(
        "sme,sde->smd", value, grad_carried, preferred_element_type=F32
    )
    grad_value = jnp.einsum("snm,sne->sme", scores, grad_ret, preferred_element_type=F32)
    grad_value = grad_value + decay_out * jnp.einsum(
        "smd,sde->sme", key, grad_carried, preferred_element_type=F32
    )
    grad_qkv = jnp.concatenate(
        [
            (turn_back(grad_query, tables_q) * scale).astype(BF16),
            turn_back(grad_key, tables_k).astype(BF16),
            grad_value.astype(BF16),
        ],
        axis=-1,
    )
    grad_qkv_w = scatter_line(mm_grad(normed_one_all, grad_qkv).astype(BF16))
    qkv_width = grad_qkv.shape[-1]
    normed_one_back = mm_back(grad_qkv, weight_first[:, :qkv_width]) + mm_back(
        grad_gate, weight_first[:, qkv_width:]
    )
    normed_one_back = plane_scatter(normed_one_back.astype(BF16), 8)
    grad_inputs = to_outer(
        grad_middle + normalize_back(normed_one, inv_one, normed_one_back)
    )
    ff_out = plane_scatter(mm(active, weight_down).astype(BF16), 9)
    output = to_outer((middle + ff_out).astype(BF16))

    grad_out = (
        grad_out.reshape(n_pb // heads_pb, n_ka, wide_rows, width)
        .swapaxes(0, 1)
        .reshape(value_width, width)
    )
    grad_out = lax.all_to_all(grad_out, "ka", split_axis=0, concat_axis=0, tiled=True)
    shard_out = to_outer(scatter_line(grad_out).astype(F32))
    shard_down = to_outer(grad_down[:, :width].astype(F32))
    shard_bias = grad_down[:, width].astype(F32)
    shard_up = from_unit(swap_plane_back(grad_up)).astype(F32)
    shard_gate = from_head(swap_plane_back(grad_gate_w)).astype(F32)
    back = swap_plane_back(grad_qkv_w)
    shard_query = from_head(back[..., :key_width]).astype(F32)
    shard_key = from_head(back[..., key_width : 2 * key_width]).astype(F32)
    shard_value = from_head(back[..., 2 * key_width :]).astype(F32)
    shards = (shard_query, shard_key, shard_value, shard_gate)
    shard_gain_one = sum(
        jnp.sum(low.astype(F32) * grad, axis=-1) for low, grad in zip(firsts, shards)
    )
    shard_gain_two = jnp.sum(up_low.astype(F32) * shard_up, axis=-1)
    shard_query, shard_key, shard_value, shard_gate = (gain_one * g for g in shards)
    return (
        output,
        grad_inputs,
        shard_gain_one,
        shard_query,
        shard_key,
        shard_value,
        shard_gate,
        shard_out,
        shard_gain_two,
        gain_two * shard_up,
        shard_bias,
        shard_down,
    )


def solution(mesh):
    dp, pb, ka = (mesh.shape[a] for a in ("dp", "pb", "ka"))
    fine = Mesh(mesh.devices.reshape(dp // 2, 2, pb, ka), ("dph", "dpl", "pb", "ka"))
    dp_axes = ("dph", "dpl")
    every = ("dph", "dpl", "pb", "ka")
    tokens = P(dp_axes, ("pb", "ka"), None)
    matrix = P(every, None)
    vector = P(every)
    return jax.shard_map(
        on_device,
        mesh=fine,
        in_specs=(
            tokens,
            tokens,
            P(dp_axes, None),
            vector,
            matrix,
            matrix,
            matrix,
            matrix,
            matrix,
            vector,
            matrix,
            vector,
            matrix,
        ),
        out_specs=(
            tokens,
            tokens,
            vector,
            matrix,
            matrix,
            matrix,
            matrix,
            matrix,
            vector,
            matrix,
            vector,
            matrix,
        ),
        check_vma=False,
    )
```

time: 3840 us -> 874 us (0.23)
  waiting for transfers between devices: 3150 us -> 61.4 us
  Pallas kernels: 0 us -> 425 us
  matrix products: 333 us -> 164 us
  blocking collectives: 126 us -> 32.2 us
  local copies, waits for them, and re-layouts: 155 us -> 83.9 us
    reduce_scatter x9 -> x4, waiting for transfers between devices: 2190 us -> 0.04 us  [scatter_line(): return lax.psum_scatter(values, LINE, scatter_dimension=0, tiled=True)]
    all_gather x11 -> x4, waiting for transfers between devices: 911 us -> 50.3 us  [gather_line(): return lax.all_gather(values, LINE, axis=0, tiled=True)]
    pallas_call x0 -> x10, Pallas kernels: none -> 425 us  [the longest x4 164 us: plane_gather(): pl.pallas_call(gather_kernel, out_shape=jax.ShapeDtypeStruct((2 * batch,...]
    dot_general x27 -> x26, matrix products: 333 us -> 164 us  [the longest x5 56.4 us: mm_back(): return jnp.einsum('sto,io->sti', left, right, preferred_element_type=F32)]
    unnamed x2 -> x0, blocking collectives: 88.7 us -> none
    unnamed x24 -> x10, waiting for transfers between devices: 53.5 us -> 0.15 us
  transfers between devices with their start and end apart: 22 -> 15, of which waited for: 21 -> 2; matrix products, arithmetic and copies ran while one was open for 9% -> 28% of each run, Pallas kernels for 0% -> 49%
where the time goes in v1:
time: 874 us; the launch traced here: 868 us
  Pallas kernels  425 us (49%)
  matrix products  164 us (19%)
  local copies, waits for them, and re-layouts  83.9 us (10%)
  waiting for transfers between devices  61.4 us (7%)
  other arithmetic  53.2 us (6%)
  starting transfers between devices  32.7 us (4%)
  blocking collectives  32.2 us (4%)
  between operations  15.7 us (2%)
    pallas_call x4, Pallas kernels, plane_gather(): pl.pallas_call(gather_kernel, out_shape=jax.ShapeDtypeStruct((2 * batch,...  164 us
    pallas_call x4, Pallas kernels, plane_scatter(): pl.pallas_call(scatter_kernel, out_shape=jax.ShapeDtypeStruct(shape, F32)...  162 us
    pallas_call x2, Pallas kernels, line_scan(): pl.pallas_call(functools.partial(scan_kernel, count, forward), out_shape=...  99.2 us
    dot_general x5, matrix products, mm_back(): return jnp.einsum('sto,io->sti', left, right, preferred_element_type=F32)  56.4 us
    all_gather x4, waiting for transfers between devices, gather_line(): return lax.all_gather(values, LINE, axis=0, tiled=True)  50.3 us
    dot_general x5, matrix products, mm_grad(): return jnp.einsum('sti,sto->io', left, right, preferred_element_type=F32)  44 us
    dot_general x4, matrix products, mm(): return jnp.einsum('sti,io->sto', left, right, preferred_element_type=F32)  41.7 us
    unnamed x155, local copies, waits for them, and re-layouts  38.8 us
  transfers between devices with their start and end apart: 15, of which 2 were waited for; matrix products, arithmetic and copies ran while one was open for 28% of the time, Pallas kernels for 49%

profile of v1, /device:TPU:2, one launch (start us, length us, event | category | flops | bytes accessed | tf_op | source)
XLA Modules:
  0.0 868.3 jit_solution(3770566519432233105)
XLA Ops:
  15.0 23.8 %all_to_all.93 = bf16[64,8,1536]{2,0,1:T(8,128)(2,1)} all-to-all(bf16[64,8,1536]{2,0,1:T(8,128)(2,1)S(1)} %pad_maximum_fusion.2), channel_id=1, replica_groups=mesh['dp'=2,'pb'=4,'ka'=4] {'dp','ka'}, dimensions={1} | all-to-all | bytes 3145728 | tf_op jit(solution)/shard_map/all_to_all | solution.py:412
  41.1 5.5 all-to-all-start.2
  46.6 8.4 all-gather
  59.4 2.9 reshape.623
  62.5 4.0 fusion.44
  66.5 3.9 multiply_reduce_fusion.5
  76.4 40.3 %plane_gather.4 = bf16[4,512,2048]{2,1,0:T(8,128)(2,1)} custom-call(bf16[2,128,2048]{2,1,0:T(8,128)(2,1)} %fusion.15.shard), custom_call_target="tpu_custom_call" | custom-call | tf_op jit(solution)/shard_map/plane_gather/pallas_call | solution.py:95
  116.7 42.1 %plane_gather.6 = bf16[4,512,2048]{2,1,0:T(8,128)(2,1)} custom-call(bf16[2,128,2048]{2,1,0:T(8,128)(2,1)} %reshape.611.shard), custom_call_target="tpu_custom_call" | custom-call | tf_op jit(solution)/shard_map/plane_gather/pallas_call | solution.py:95
  161.0 4.0 copy.331
  165.0 5.7 all-to-all-start.1
  171.9 50.3 %all-gather.6.cloned.1.call-done = bf16[2048,1536]{1,0:T(8,128)(2,1)} async-done(((bf16[512,1536]{1,0:T(8,128)(2,1)}), bf16[2048,1536]{1,0:T(8,128)(2,1)}) %all-gather.6.cloned.1.call-update) | async-done | bytes 6291472 | tf_op jit(solution)/shard_map/all_gather | solution.py:421
  222.2 17.1 %fusion = f32[4,512,1536]{2,1,0:T(8,128)S(1)} fusion(bf16[4,512,2048]{2,1,0:T(8,128)(2,1)} %plane_gather.4, bf16[2048,1536]{1,0:T(8,128)(2,1)} %all-gather.6.cloned.1.call-done), kind=kOutput, calls=%fused_computation.2 | convolution fusion | flops 12884901888 | bytes 27262976 | tf_op jit(solution)/shard_map/sti,io->sto/dot_general | solution.py:347
  243.9 42.7 %line_scan.2 = bf16[4,256,512]{2,1,0:T(8,128)(2,1)S(1)} custom-call(f32[4,256,512]{2,1,0:T(8,128)S(1)} %fusion.23.state, f32[2,4]{1,0:T(2,128)S(1)} %stack.8.coef), custom_call_target="tpu_custom_call" | custom-call | tf_op jit(solution)/shard_map/line_scan/pallas_call | solution.py:287
  291.3 7.1 convolution_convert_fusion.2.part
  298.4 40.5 %plane_scatter.4 = f32[2,128,2048]{2,1,0:T(8,128)S(1)} custom-call(bf16[4,512,2048]{2,1,0:T(8,128)(2,1)S(1)} %convolution_convert_fusion.2.part), custom_call_target="tpu_custom_call" | custom-call | tf_op jit(solution)/shard_map/plane_scatter/pallas_call | solution.py:208
  341.8 41.0 %plane_gather.5 = bf16[4,512,2048]{2,1,0:T(8,128)(2,1)} custom-call(bf16[2,128,2048]{2,1,0:T(8,128)(2,1)} %fusion.14.shard), custom_call_target="tpu_custom_call" | custom-call | tf_op jit(solution)/shard_map/plane_gather/pallas_call | solution.py:95
  382.9 10.7 %multiply_convert_fusion.3 = (bf16[4,512,512]{2,1,0:T(8,128)(2,1)}, f32[4,512,512]{2,1,0:T(8,128)S(1)}) fusion(f32[512]{0:T(512)S(1)} %convert_reduce_fusion, bf16[4,512,2048]{2,1,0:T(8,128)(2,1)} %plane_gather.5, bf16[2048,512]{1,0:T(8,128)(2,1)} %all-gather.10.cloned.1.call-done), kind=kOutput, calls=%fused_computation.26 | convolution fusion | flops 4301258752 | bytes 16779264 | tf_op jit(solution)/shard_map/sti,io->sto/dot_general | solution.py:347
  393.6 8.5 fusion.51
  403.4 5.8 bitcast_convert_fusion.2
  410.7 6.5 convolution_convert_fusion.part
  417.3 40.5 %plane_scatter.6 = f32[2,128,2048]{2,1,0:T(8,128)S(1)} custom-call(bf16[4,512,2048]{2,1,0:T(8,128)(2,1)S(1)} %convolution_convert_fusion.part), custom_call_target="tpu_custom_call" | custom-call | tf_op jit(solution)/shard_map/plane_scatter/pallas_call | solution.py:208
  460.8 40.7 %plane_gather.7 = bf16[4,512,2048]{2,1,0:T(8,128)(2,1)} custom-call(bf16[2,128,2048]{2,1,0:T(8,128)(2,1)} %fusion.28.shard), custom_call_target="tpu_custom_call" | custom-call | tf_op jit(solution)/shard_map/plane_gather/pallas_call | solution.py:95
  501.6 11.8 %fusion.45 = (f32[4,512]{1,0:T(4,128)S(1)}, f32[4,512]{1,0:T(4,128)S(1)}, f32[4,512,512]{2,1,0:T(8,128)S(1)}, bf16[4,512,512]{2,1,0:T(8,128)(2,1)}) fusion(f32[4,512]{1,0:T(4,128)S(1)} %add_rsqrt_fusion, f32[4,512,512]{2,1,0:T(8,128)} %copy-done.6, f32[4,512]{1,0:T(4,128)S(1)} %broadcast_multiply_fusion.7, f32[4,512,1536]{2,1,0:T(8,128)} %copy-done.11, ...), kind=kOutput, calls=%fused_computation.161 | convolution fusion | flops 4311740416 | bytes 25198592 | tf_op jit(solution)/shard_map/sto,io->sti/dot_general | solution.py:351
  515.0 4.3 multiply_convert_fusion.1
  527.9 56.5 %line_scan.3 = bf16[4,256,512]{2,1,0:T(8,128)(2,1)S(1)} custom-call(f32[4,256,512]{2,1,0:T(8,128)S(1)} %fusion.24.state, f32[2,4]{1,0:T(2,128)S(1)} %stack.9.coef), custom_call_target="tpu_custom_call" | custom-call | tf_op jit(solution)/shard_map/line_scan/pallas_call | solution.py:287
  585.3 3.0 multiply_add_fusion.2
  593.7 3.7 fusion.58
  600.9 5.7 bitcast_convert_fusion.4
  607.9 13.9 %bitcast_convert_fusion = bf16[2048,1024]{1,0:T(8,128)(2,1)} fusion(bf16[4,512,2048]{2,1,0:T(8,128)(2,1)} %plane_gather.4, bf16[4,512,512]{1,2,0:T(8,128)(2,1)} %add_convert_fusion.1, bf16[4,512,128]{1,2,0:T(8,128)(2,1)} %copy.287, bf16[4,512,128]{1,2,0:T(8,128)(2,1)} %copy.286, bf16[4,512,256]{1,2,0:T(8,128)(2,1)S(1)} %copy-done.48), kind=kOutput, calls=%fused_computation.1 | convolution fusion | flops 8608808960 | bytes 16777216 | tf_op jit(solution)/shard_map/sti,sto->io/dot_general | solution.py:355
  622.3 8.6 bitcast_convert_fusion.1
  632.7 10.0 %bitcast_convert_fusion.3 = bf16[512,2048]{1,0:T(8,128)(2,1)} fusion(bf16[4,512,512]{2,1,0:T(8,128)(2,1)} %copy-done.40, bf16[4,512,2048]{2,1,0:T(8,128)(2,1)} %plane_gather.7), kind=kOutput, calls=%fused_computation.19 | convolution fusion | flops 4296015872 | bytes 12582912 | tf_op jit(solution)/shard_map/sti,sto->io/dot_general | solution.py:355
  642.7 4.9 all-to-all-start.5
  647.7 13.1 %fusion.8 = f32[4,512,2048]{2,1,0:T(8,128)} fusion(bf16[4,512,512]{2,1,0:T(8,128)(2,1)} %get-tuple-element.71, bf16[2048,1536]{1,0:T(8,128)(2,1)} %all-gather.6.cloned.1.call-done), kind=kOutput, calls=%fused_computation.37 | convolution fusion | flops 4294967296 | bytes 20971520 | tf_op jit(solution)/shard_map/sto,io->sti/dot_general | solution.py:351
  660.8 10.8 %all-to-all-done.5 = bf16[4,128,2048]{2,1,0:T(8,128)(2,1)} async-done(((bf16[4,128,2048]{2,1,0:T(8,128)(2,1)}), bf16[4,128,2048]{2,1,0:T(8,128)(2,1)}, u32[]{:S(2)}, u32[]{:S(2)}) %all-to-all-start.5) | async-done | bytes 2097184 | tf_op jit(solution)/shard_map/all_to_all | solution.py:577
  671.7 16.4 %add_convert_fusion.part = bf16[4,512,2048]{2,1,0:T(8,128)(2,1)} fusion(f32[4,512,2048]{2,1,0:T(8,128)} %fusion.8, bf16[2048,1536]{1,0:T(8,128)(2,1)} %all-gather.6.cloned.1.call-done, bf16[4,512,512]{1,2,0:T(8,128)(2,1)} %add_convert_fusion.1, bf16[4,512,128]{1,2,0:T(8,128)(2,1)} %copy.287, bf16[4,512,128]{1,2,0:T(8,128)(2,1)} %copy.286, ...), kind=kOutput, calls=%fused_computation | convolution fusion | flops 8615100416 | bytes 33554432 | tf_op jit(solution)/shard_map/sto,io->sti/dot_general | solution.py:351
  688.1 3.5 copy-done.3
  691.6 40.8 %plane_scatter.7 = f32[2,128,2048]{2,1,0:T(8,128)S(1)} custom-call(bf16[4,512,2048]{2,1,0:T(8,128)(2,1)S(1)} %copy-done.3), custom_call_target="tpu_custom_call" | custom-call | tf_op jit(solution)/shard_map/plane_scatter/pallas_call | solution.py:208
  733.7 6.8 convolution_convert_fusion.1.part
  744.3 5.6 all-to-all-start.6
  750.0 2.7 fusion.46
  752.7 3.4 copy-done.2
  756.2 40.4 %plane_scatter.5 = f32[2,128,2048]{2,1,0:T(8,128)S(1)} custom-call(bf16[4,512,2048]{2,1,0:T(8,128)(2,1)S(1)} %copy-done.2), custom_call_target="tpu_custom_call" | custom-call | tf_op jit(solution)/shard_map/plane_scatter/pallas_call | solution.py:208
  798.0 2.8 reduce.7
  803.0 5.5 all-to-all-start.4
  808.5 5.1 multiply_add_fusion.1
  813.7 3.0 reshape.612
  818.5 3.4 reshape.613
  829.1 4.5 all-to-all-start.3
  (291 shorter events, 110.4 us)
Async XLA Ops:
  7.2 153.8 %all-gather.8.cloned.1.call-start = ((), (), s32[]{:S(2)}) async-start(), calls=%async_computation.13 | async-start | bytes 2621440 | tf_op jit(solution)/shard_map/all_gather | solution.py:421
  9.7 161.2 %all-gather.12.cloned.1.call-start = ((), (), s32[]{:S(2)}) async-start(), calls=%async_computation.15 | async-start | bytes 2785280 | tf_op jit(solution)/shard_map/all_gather | solution.py:421
  10.2 3.9 copy-start.63
  10.2 3.9 copy-start.41
  10.2 3.9 copy-start.43
  14.0 208.2 %all-gather.6.cloned.1.call-start = ((), (), s32[]{:S(2)}) async-start(), calls=%async_computation.12 | async-start | bytes 7864320 | tf_op jit(solution)/shard_map/all_gather | solution.py:421
  14.9 23.9 %copy-start.64 = (f32[64]{0:T(128)S(1)}, f32[64]{0:T(128)}, u32[]{:S(2)}) copy-start(f32[64]{0:T(128)} %param.22) | copy-start | bytes 772
  14.9 24.4 %copy-start.31 = (f32[64,4096]{1,0:T(8,128)S(1)}, f32[64,4096]{1,0:T(8,128)}, u32[]{:S(2)}) copy-start(f32[64,4096]{1,0:T(8,128)} %param.23) | copy-start | bytes 3145732
  39.5 7.1 copy-start.60
  39.5 15.8 %copy-start.46 = (bf16[2,128,2048]{2,1,0:T(8,128)(2,1)S(1)}, bf16[2,128,2048]{2,1,0:T(8,128)(2,1)}, u32[]{:S(2)}) copy-start(bf16[2,128,2048]{2,1,0:T(8,128)(2,1)} %param.13) | copy-start | bytes 3145732
  41.1 119.9 %all-to-all-start.2 = ((bf16[64,8,512]{2,0,1:T(8,128)(2,1)}), bf16[64,8,512]{2,0,1:T(8,128)(2,1)}, u32[]{:S(2)}, u32[]{:S(2)}) async-start(bf16[64,8,512]{2,0,1:T(8,128)(2,1)} %reshape.604), calls=%async_computation.2 | async-start | bytes 1048576 | tf_op jit(solution)/shard_map/all_to_all | solution.py:412
  46.6 336.3 %all-gather.10.cloned.1.call-start = ((), (), s32[]{:S(2)}) async-start(), calls=%async_computation.14 | async-start | bytes 2621440 | tf_op jit(solution)/shard_map/all_gather | solution.py:421
  62.3 8.1 copy-start.8
  62.3 4.2 copy-start.13
  66.5 5.2 copy-start.50
  159.0 82.1 %copy-start.28 = (f32[512,512]{1,0:T(8,128)}, f32[512,512]{1,0:T(8,128)S(1)}, u32[]{:S(2)}) copy-start(f32[512,512]{1,0:T(8,128)S(1)} %exponential_select_fusion) | copy-start | bytes 3145732
  160.9 78.4 %copy-start.38 = (f32[512,128]{1,0:T(8,128)}, f32[512,128]{1,0:T(8,128)S(1)}, u32[]{:S(2)}) copy-start(f32[512,128]{1,0:T(8,128)S(1)} %get-tuple-element.98) | copy-start | bytes 786436
  165.0 126.3 %all-to-all-start.1 = ((bf16[4,128,2048]{2,1,0:T(8,128)(2,1)}), bf16[4,128,2048]{2,1,0:T(8,128)(2,1)}, u32[]{:S(2)}, u32[]{:S(2)}) async-start(bf16[4,128,2048]{2,1,0:T(8,128)(2,1)} %bitcast.181), calls=%async_computation.1 | async-start | bytes 4194304 | tf_op jit(solution)/shard_map/all_to_all | solution.py:437
  170.7 569.9 %reduce-scatter.12.cloned.1.call-start = ((), (), s32[]{:S(2)}) async-start(), calls=%async_computation.18 | async-start | bytes 2621440 | tf_op jit(solution)/shard_map/reduce_scatter | solution.py:424
  239.3 48.9 %copy-start.11 = (f32[4,512,1536]{2,1,0:T(8,128)}, f32[4,512,1536]{2,1,0:T(8,128)S(1)}, u32[]{:S(2)}) copy-start(f32[4,512,1536]{2,1,0:T(8,128)S(1)} %fusion) | copy-start | bytes 37748740
  240.1 46.5 %copy-start.14 = (bf16[4,512,256]{2,1,0:T(8,128)(2,1)}, bf16[4,512,256]{2,1,0:T(8,128)(2,1)S(1)}, u32[]{:S(2)}) copy-start(bf16[4,512,256]{2,1,0:T(8,128)(2,1)S(1)} %fusion.9) | copy-start | bytes 3145732
  291.3 7.1 copy-start.40
  298.4 40.5 %copy-start.9 = (f32[2,128,2048]{2,1,0:T(8,128)S(1)}, f32[2,128,2048]{2,1,0:T(8,128)}, u32[]{:S(2)}) copy-start(f32[2,128,2048]{2,1,0:T(8,128)} %copy-done.8) | copy-start | bytes 6291460
  382.9 10.7 %copy-start.56 = (bf16[512,2176]{1,0:T(8,128)(2,1)S(1)}, bf16[512,2176]{1,0:T(8,128)(2,1)}, u32[]{:S(2)}) copy-start(bf16[512,2176]{1,0:T(8,128)(2,1)} %all-gather.12.cloned.1.call-done) | copy-start | bytes 6684676
  382.9 20.5 %slice-start.2 = ((s8[8388608]{0:T(1024)(128)(4,1)}), s8[4194304]{0:T(1024)(128)(4,1)S(1)}, s32[]{:S(2)}) async-start(s8[8388608]{0:T(1024)(128)(4,1)} %bitcast.179), calls=%async_computation.23 | async-start | bytes 8388608
  393.6 9.8 %slice-start.3 = ((s8[8388608]{0:T(1024)(128)(4,1)}), s8[4194304]{0:T(1024)(128)(4,1)S(1)}, s32[]{:S(2)}) async-start(s8[8388608]{0:T(1024)(128)(4,1)} %bitcast.179), calls=%async_computation.24 | async-start | bytes 8388608
  409.2 388.8 %reduce-scatter.10.cloned.1.call-start = ((), (), s32[]{:S(2)}) async-start(), calls=%async_computation.17 | async-start | bytes 2621440 | tf_op jit(solution)/shard_map/reduce_scatter | solution.py:424
  417.3 40.5 %copy-start.5 = (f32[2,128,2048]{2,1,0:T(8,128)S(1)}, f32[2,128,2048]{2,1,0:T(8,128)}, u32[]{:S(2)}) copy-start(f32[2,128,2048]{2,1,0:T(8,128)} %copy-done.4) | copy-start | bytes 6291460
  501.6 11.9 %copy-start.7 = (f32[4,512,512]{2,1,0:T(8,128)S(1)}, f32[4,512,512]{2,1,0:T(8,128)}, u32[]{:S(2)}) copy-start(f32[4,512,512]{2,1,0:T(8,128)} %copy-done.6) | copy-start | bytes 12582916
  514.9 5.1 copy-start.10
  514.9 4.4 copy-start.23
  514.9 4.3 copy-start.26
  527.9 56.5 %copy-start.16 = (bf16[4,512,256]{2,1,0:T(8,128)(2,1)S(1)}, bf16[4,512,256]{2,1,0:T(8,128)(2,1)}, u32[]{:S(2)}) copy-start(bf16[4,512,256]{2,1,0:T(8,128)(2,1)} %copy-done.14) | copy-start | bytes 3145732
  527.9 56.5 %copy-start.19 = (bf16[4,512,512]{2,1,0:T(8,128)(2,1)S(1)}, bf16[4,512,512]{2,1,0:T(8,128)(2,1)}, u32[]{:S(2)}) copy-start(bf16[4,512,512]{2,1,0:T(8,128)(2,1)} %copy-done.18) | copy-start | bytes 6291460
  593.7 3.7 copy-start.27
  593.7 5.9 slice-start
  606.7 218.2 %reduce-scatter.8.cloned.1.call-start = ((), (), s32[]{:S(2)}) async-start(), calls=%async_computation.16 | async-start | bytes 5242880 | tf_op jit(solution)/shard_map/reduce_scatter | solution.py:424
  621.8 211.8 %reduce-scatter.14.cloned.1.call-start = ((), (), s32[]{:S(2)}) async-start(), calls=%async_computation.19 | async-start | bytes 2785280 | tf_op jit(solution)/shard_map/reduce_scatter | solution.py:424
  642.7 29.0 %all-to-all-start.5 = ((bf16[4,128,2048]{2,1,0:T(8,128)(2,1)}), bf16[4,128,2048]{2,1,0:T(8,128)(2,1)}, u32[]{:S(2)}, u32[]{:S(2)}) async-start(bf16[4,128,2048]{2,1,0:T(8,128)(2,1)} %bitcast.202), calls=%async_computation.7 | async-start | bytes 4194304 | tf_op jit(solution)/shard_map/all_to_all | solution.py:577
  647.5 204.2 %reduce-scatter.16.cloned.1.call-start = ((), (), s32[]{:S(2)}) async-start(), calls=%async_computation.20 | async-start | bytes 2621440
  691.6 42.2 %copy-start.57 = (bf16[512,2176]{1,0:T(8,128)(2,1)S(1)}, bf16[512,2176]{1,0:T(8,128)(2,1)}, u32[]{:S(2)}) copy-start(bf16[512,2176]{1,0:T(8,128)(2,1)} %all-gather.12.cloned.1.call-done) | copy-start | bytes 6684676
  691.6 42.2 %copy-start.66 = (bf16[4,512,512]{2,1,0:T(8,128)(2,1)S(1)}, bf16[4,512,512]{2,1,0:T(8,128)(2,1)}, u32[]{:S(2)}) copy-start(bf16[4,512,512]{2,1,0:T(8,128)(2,1)} %get-tuple-element.115) | copy-start | bytes 6291460
  740.5 9.4 %copy-start.51 = (f32[2,128]{1,0:T(2,128)S(1)}, f32[2,128]{1,0:T(2,128)}, u32[]{:S(2)}) copy-start(f32[2,128]{1,0:T(2,128)} %copy-done.50) | copy-start | bytes 3076
  740.5 9.4 %copy-start.53 = (f32[2,128]{1,0:T(2,128)S(1)}, f32[2,128]{1,0:T(2,128)}, u32[]{:S(2)}) copy-start(f32[2,128]{1,0:T(2,128)} %copy-done.52) | copy-start | bytes 3076
  744.3 58.7 %all-to-all-start.6 = ((bf16[8,2,16384]{2,1,0:T(2,128)(2,1)}), bf16[8,2,16384]{2,1,0:T(2,128)(2,1)}, u32[]{:S(2)}, u32[]{:S(2)}) async-start(bf16[8,2,16384]{2,1,0:T(2,128)(2,1)} %reshape.670), calls=%async_computation.9 | async-start | bytes 1048576 | tf_op jit(solution)/shard_map/all_to_all | solution.py:418
  798.0 10.6 %copy-start.21 = (bf16[2,128,2048]{2,1,0:T(8,128)(2,1)S(1)}, bf16[2,128,2048]{2,1,0:T(8,128)(2,1)}, u32[]{:S(2)}) copy-start(bf16[2,128,2048]{2,1,0:T(8,128)(2,1)} %reshape.611.shard) | copy-start | bytes 3145732
  803.0 26.1 %all-to-all-start.4 = ((bf16[8,2,16384]{2,1,0:T(2,128)(2,1)}), bf16[8,2,16384]{2,1,0:T(2,128)(2,1)}, u32[]{:S(2)}, u32[]{:S(2)}) async-start(bf16[8,2,16384]{2,1,0:T(2,128)(2,1)} %reshape.666), calls=%async_computation.6 | async-start | bytes 1048576 | tf_op jit(solution)/shard_map/all_to_all | solution.py:418
  829.1 25.4 %all-to-all-start.3 = ((bf16[8,2,32768]{2,1,0:T(2,128)(2,1)}), bf16[8,2,32768]{2,1,0:T(2,128)(2,1)S(1)}, u32[]{:S(2)}, u32[]{:S(2)}) async-start(bf16[8,2,32768]{2,1,0:T(2,128)(2,1)} %reshape.668), calls=%async_computation.4 | async-start | bytes 2097152 | tf_op jit(solution)/shard_map/all_to_all | solution.py:418
  (39 other events, 76.9 us)
Sparse Core Ops, SparseCore 0:
  10.2 47.4 all-gather.7
  59.9 46.5 all-gather.11
  108.0 114.1 all-gather.5
  223.6 59.5 all-gather.9
  409.3 58.6 reduce-scatter.11
  606.8 41.0 reduce-scatter.9
  650.2 76.0 reduce-scatter.7
  728.8 46.4 reduce-scatter.13
  777.7 43.2 reduce-scatter.15

commit v2 on v1

v2 whole, which is shorter than its diff:
```python
import functools
import math

import jax
import jax.numpy as jnp
import numpy as np
from jax import lax
from jax.experimental import pallas as pl
from jax.experimental.pallas import tpu as pltpu
from jax.sharding import Mesh
from jax.sharding import PartitionSpec as P

H = 8
XPOS_BASE = 512.0
EPSILON = 1e-05
MESH = pl.DeviceIdType.MESH
F32 = jnp.float32
BF16 = jnp.bfloat16

PLANE = ("dpl", "ka")
LINE = ("dph", "pb")


def plane_ids():
    row = lax.axis_index("dpl")
    col = lax.axis_index("ka")
    other_row = 1 - row
    across = lax.rem(col + 2, 4)
    sibling = col + 1 - 2 * lax.rem(col, 2)
    return row, col, other_row, across, sibling


def greet(targets):
    barrier = pltpu.get_barrier_semaphore()
    for target in targets:
        pl.semaphore_signal(barrier, inc=1, device_id=target, device_id_type=MESH)
    pl.semaphore_wait(barrier, len(targets))


def gather_stages(shard, full, local_sem, send_sem, recv_sem):
    batch, length, _ = shard.shape
    half = length // 2
    row, col, other_row, across, sibling = plane_ids()
    to_x = {"ka": across}
    to_y = {"dpl": other_row}
    to_s = {"ka": sibling}

    def slot(r, c, start=0, size=length):
        return full.at[pl.ds(r * batch, batch), pl.ds(c * length + start, size), :]

    def hop(index, target, dst, src=None):
        return pltpu.make_async_remote_copy(
            src_ref=dst if src is None else src,
            dst_ref=dst,
            send_sem=send_sem.at[index],
            recv_sem=recv_sem.at[index],
            device_id=target,
            device_id_type=MESH,
        )

    mine = pltpu.make_async_copy(shard, slot(row, col), local_sem)
    from_x = hop(0, to_x, slot(row, col), shard)
    from_y = hop(1, to_y, slot(row, col), shard)
    own_s = hop(2, to_s, slot(row, col), shard)
    diag_y = hop(3, to_y, slot(row, across, 0, half))
    relay_x = hop(4, to_s, slot(row, across))
    diag_x = hop(5, to_x, slot(other_row, col, half, half))
    relay_y = hop(6, to_s, slot(other_row, col))
    relay_a = hop(7, to_s, slot(other_row, across, 0, half))
    relay_b = hop(8, to_s, slot(other_row, across, half, half))

    def begin():
        from_x.start()
        from_y.start()
        own_s.start()
        mine.start()

    def relay():
        from_x.wait_recv()
        diag_y.start()
        relay_x.start()
        from_y.wait_recv()
        diag_x.start()
        relay_y.start()

    def diagonal():
        diag_y.wait_recv()
        relay_a.start()
        diag_x.wait_recv()
        relay_b.start()

    def end():
        for copy in (own_s, relay_x, relay_y, relay_a, relay_b):
            copy.wait_recv()
        for copy in (from_x, from_y, own_s, diag_y, relay_x, diag_x, relay_y, relay_a, relay_b):
            copy.wait_send()
        mine.wait()

    return (to_x, to_y, to_s), (begin, relay, diagonal, end)


GATHER_SCRATCH = (
    pltpu.SemaphoreType.DMA,
    pltpu.SemaphoreType.DMA((9,)),
    pltpu.SemaphoreType.DMA((9,)),
)


def gathered_shape(shard):
    batch, length, width = shard.shape
    return jax.ShapeDtypeStruct((2 * batch, 4 * length, width), shard.dtype)


def gather_kernel(shard, *refs):
    targets, stages = gather_stages(shard, *refs[-4:])
    greet(targets)
    for stage in stages:
        stage()


def read_rows(ref, b, at, order):
    if not order:
        return ref[b, at, :]
    size = ref.shape[-1] // len(order)
    return jnp.concatenate([ref[b, at, i * size : (i + 1) * size] for i in order], axis=-1)


def write_rows(ref, b, at, order, values):
    if not order:
        ref[b, at, :] = values
        return
    size = ref.shape[-1] // len(order)
    for j, i in enumerate(order):
        ref[b, at, i * size : (i + 1) * size] = values[:, j * size : (j + 1) * size]


def normalize_rows(source, target, order):
    batch, length, _ = source.shape
    step = 16

    def body(i, carry):
        at = pl.ds(i * step, step)
        for b in range(batch):
            normed, _ = normalize(read_rows(source, b, at, order).astype(F32))
            target[b, at, :] = normed.astype(BF16)
        return carry

    lax.fori_loop(0, length // step, body, 0)


def owners_stages(sources, targets, keep_sem, send_sem, recv_sem):
    row, col, other_row, _, _ = plane_ids()
    me = row * 4 + col
    peers = [(row, lax.rem(col + away, 4)) for away in (1, 2, 3)]
    peers += [(other_row, lax.rem(col + away, 4)) for away in (0, 1, 2, 3)]
    copies = []
    for a in range(len(sources)):
        copies.append(
            pltpu.make_async_copy(sources[a].at[me], targets[a].at[me], keep_sem.at[a])
        )
        for i in (6, 5, 4, 3, 2, 1, 0):
            r, c = peers[i]
            copies.append(
                pltpu.make_async_remote_copy(
                    src_ref=sources[a].at[r * 4 + c],
                    dst_ref=targets[a].at[me],
                    send_sem=send_sem.at[a, i],
                    recv_sem=recv_sem.at[a, i],
                    device_id={"dpl": r, "ka": c},
                    device_id_type=MESH,
                )
            )

    def begin():
        for copy in copies:
            copy.start()

    def end():
        for copy in copies:
            copy.wait()

    return [{"dpl": r, "ka": c} for r, c in peers], (begin, end)


def owners_scratch(count):
    return [
        pltpu.SemaphoreType.DMA((count,)),
        pltpu.SemaphoreType.DMA((count, 7)),
        pltpu.SemaphoreType.DMA((count, 7)),
    ]


def trade_stages(line, source, target, sems):
    place, col = lax.axis_index(line), lax.axis_index("ka")
    moves = place != col
    partner = {line: col, "ka": place}

    def trade():
        return pltpu.make_async_remote_copy(
            src_ref=source,
            dst_ref=target,
            send_sem=sems.at[0],
            recv_sem=sems.at[1],
            device_id=partner,
            device_id_type=MESH,
        )

    def keep():
        return pltpu.make_async_copy(source, target, sems.at[2])

    def greet_partner(barrier):
        @pl.when(moves)
        def _():
            pl.semaphore_signal(barrier, inc=1, device_id=partner, device_id_type=MESH)

        return moves.astype(jnp.int32)

    def begin():
        @pl.when(moves)
        def _():
            trade().start()

        @pl.when(jnp.logical_not(moves))
        def _():
            keep().start()

    def end():
        @pl.when(moves)
        def _():
            trade().wait()

        @pl.when(jnp.logical_not(moves))
        def _():
            keep().wait()

    return greet_partner, (begin, end)


TRADE_SCRATCH = (pltpu.SemaphoreType.DMA((3,)),)


def open_kernel(line, order, x, up, out, *refs):
    normed_all, up_mine, out_mine, normed = refs[:4]
    sems = refs[4:]
    targets, owners = owners_stages((up,), (up_mine,), *sems[3:6])
    _, gather = gather_stages(normed, normed_all, *sems[:3])
    greet_partner, trade = trade_stages(line, out, out_mine, sems[6])
    barrier = pltpu.get_barrier_semaphore()
    for target in targets:
        pl.semaphore_signal(barrier, inc=1, device_id=target, device_id_type=MESH)
    extra = greet_partner(barrier)
    normalize_rows(x, normed, order)
    pl.semaphore_wait(barrier, len(targets) + extra)
    gather[0]()
    trade[0]()
    owners[0]()
    for stage in gather[1:]:
        stage()
    owners[1]()
    trade[1]()


def open_plane(x, up, out, line, order, collective_id, *before):
    anywhere = pl.BlockSpec(memory_space=pl.ANY)
    return pl.pallas_call(
        lambda a, b, c, *refs: open_kernel(line, order, a, b, c, *refs[len(before) :]),
        out_shape=[
            gathered_shape(x),
            jax.ShapeDtypeStruct(up.shape, up.dtype),
            jax.ShapeDtypeStruct(out.shape, out.dtype),
        ],
        in_specs=[pl.BlockSpec(memory_space=pltpu.VMEM)] + [anywhere] * (2 + len(before)),
        out_specs=[anywhere] * 3,
        scratch_shapes=[
            pltpu.VMEM(x.shape, BF16),
            *GATHER_SCRATCH,
            *owners_scratch(1),
            *TRADE_SCRATCH,
        ],
        compiler_params=pltpu.CompilerParams(
            collective_id=collective_id,
            has_side_effects=True,
            vmem_limit_bytes=16 * 1024 * 1024,
        ),
        name="open_plane",
    )(x, up, out, *before)


def scatter_stages(
    terms, finish, sent, own, sib, from_x, from_y, diag_a, diag_b, sems, recvs, earlier=()
):
    _, batch, length, width = own.shape
    half = length // 2
    row, col, other_row, across, sibling = plane_ids()
    across_s = lax.rem(sibling + 2, 4)
    to_x = {"ka": across}
    to_y = {"dpl": other_row}
    to_s = {"ka": sibling}
    mine = ((other_row, across), (row, across), (other_row, col), (row, col))
    theirs = ((other_row, across_s), (row, across_s), (other_row, sibling), (row, sibling))
    lower, upper = pl.ds(0, half), pl.ds(half, half)
    step = 16
    tile = 512

    def hop(src, dst, index, target):
        return pltpu.make_async_remote_copy(
            src_ref=src,
            dst_ref=dst,
            send_sem=sems.at[index],
            recv_sem=recvs.at[index],
            device_id=target,
            device_id_type=MESH,
        )

    swaps = [hop(sent.at[j], sib.at[j], j, to_s) for j in range(4)]
    first_a = hop(own.at[0, :, lower, :], diag_a, 4, to_x)
    first_b = hop(own.at[0, :, upper, :], diag_b, 5, to_y)
    x_lower = hop(own.at[1, :, lower, :], from_x.at[:, lower, :], 6, to_x)
    y_upper = hop(own.at[2, :, upper, :], from_y.at[:, upper, :], 7, to_y)
    x_upper = hop(own.at[1, :, upper, :], from_x.at[:, upper, :], 8, to_x)
    y_lower = hop(own.at[2, :, lower, :], from_y.at[:, lower, :], 9, to_y)

    def make(r, c, out):
        def body(n, carry):
            columns = pl.ds(pl.multiple_of(n * tile, tile), tile)
            value = 0.0
            for left, right, flipped in terms:
                block = left[pl.ds(r * batch, batch), pl.ds(c * length, length), :]
                block = block.reshape(batch * length, left.shape[2])
                if flipped:
                    value = value + lax.dot_general(
                        block,
                        right[columns, :],
                        (((1,), (1,)), ((), ())),
                        preferred_element_type=F32,
                    )
                else:
                    value = value + jnp.dot(
                        block, right[:, columns], preferred_element_type=F32
                    )
            out[:, :, columns] = value.reshape(batch, length, tile).astype(BF16)
            return carry

        lax.fori_loop(0, width // tile, body, 0)

    def give(j):
        if earlier:
            earlier[j].wait_send()
        make(*theirs[j], sent.at[j])
        swaps[j].start()

    def add(out_ref, out_start, parts, size):
        def body(i, carry):
            value = 0.0
            for ref, start in parts:
                value = value + ref[:, pl.ds(start + i * step, step), :].astype(F32)
            out_ref[:, pl.ds(out_start + i * step, step), :] = value.astype(out_ref.dtype)
            return carry

        lax.fori_loop(0, size // step, body, 0)

    def merge(j):
        swaps[j].wait_recv()
        add(own.at[j], 0, ((own.at[j], 0), (sib.at[j], 0)), length)

    def stage_begin():
        give(0)
        make(*mine[0], own.at[0])

    def stage_diag():
        merge(0)
        first_a.start()
        first_b.start()
        give(1)
        make(*mine[1], own.at[1])

    def stage_x():
        merge(1)
        x_lower.start()
        give(2)
        make(*mine[2], own.at[2])

    def stage_y():
        merge(2)
        y_upper.start()
        give(3)
        make(*mine[3], own.at[3])

    def stage_rest():
        first_b.wait_recv()
        add(own.at[1], half, ((own.at[1], half), (diag_b, 0)), half)
        x_upper.start()
        first_a.wait_recv()
        add(own.at[2], 0, ((own.at[2], 0), (diag_a, 0)), half)
        y_lower.start()
        merge(3)

    def close(start):
        def body(i, carry):
            at = pl.ds(start + i * step, step)
            for b in range(batch):
                value = own[3, b, at, :].astype(F32)
                value = value + from_x[b, at, :].astype(F32) + from_y[b, at, :].astype(F32)
                finish(b, at, value)
            return carry

        lax.fori_loop(0, half // step, body, 0)

    def stage_end():
        x_lower.wait_recv()
        y_lower.wait_recv()
        close(0)
        y_upper.wait_recv()
        x_upper.wait_recv()
        close(half)
        for copy in (first_a, first_b, x_lower, x_upper, y_lower, y_upper):
            copy.wait_send()

    def stage_free():
        for copy in swaps:
            copy.wait_send()

    stages = (stage_begin, stage_diag, stage_x, stage_y, stage_rest, stage_end, stage_free)
    return (to_x, to_y, to_s), stages, swaps


def scatter_scratch(shape):
    batch, length, width = shape
    return [
        pltpu.VMEM((4,) + shape, BF16),
        pltpu.VMEM((4,) + shape, BF16),
        pltpu.VMEM((4,) + shape, BF16),
        pltpu.VMEM(shape, BF16),
        pltpu.VMEM(shape, BF16),
        pltpu.VMEM((batch, length // 2, width), BF16),
        pltpu.VMEM((batch, length // 2, width), BF16),
        pltpu.SemaphoreType.DMA((10,)),
        pltpu.SemaphoreType.DMA((10,)),
    ]


VMEM = pl.BlockSpec(memory_space=pltpu.VMEM)
ANY = pl.BlockSpec(memory_space=pl.ANY)


def mix_kernel(order, gated, weight, x, *refs):
    middle, normed_all, normed = refs[-15:-12]

    def finish(b, at, value):
        value = value + read_rows(x, b, at, order).astype(F32)
        middle[b, at, :] = value
        normed[b, at, :] = normalize(value)[0].astype(BF16)

    targets, stages, _ = scatter_stages(((gated, weight, False),), finish, *refs[-12:-3])
    _, gather = gather_stages(normed, normed_all, *refs[-3:])
    greet(targets)
    for stage in stages + gather:
        stage()


def plane_mix(gated, weight, x, order, collective_id, *before):
    shape = x.shape
    return pl.pallas_call(
        functools.partial(mix_kernel, order),
        out_shape=[jax.ShapeDtypeStruct(shape, F32), gathered_shape(x)],
        in_specs=[VMEM] * 3 + [ANY] * len(before),
        out_specs=[VMEM, ANY],
        scratch_shapes=[
            pltpu.VMEM(shape, BF16),
            *scatter_scratch(shape),
            *GATHER_SCRATCH,
        ],
        compiler_params=pltpu.CompilerParams(
            collective_id=collective_id,
            has_side_effects=True,
            vmem_limit_bytes=48 * 1024 * 1024,
        ),
        name="plane_mix",
    )(gated, weight, x, *before)


def turn_kernel(order, grad, weight, middle, cot, *refs):
    grad_middle, grad_all, low = refs[-15:-12]

    def finish(b, at, value):
        normed, inv = normalize(middle[b, at, :])
        value = normalize_back(normed, inv, value)
        value = value + read_rows(cot, b, at, order).astype(F32)
        grad_middle[b, at, :] = value
        low[b, at, :] = value.astype(BF16)

    targets, stages, _ = scatter_stages(((grad, weight, True),), finish, *refs[-12:-3])
    _, gather = gather_stages(low, grad_all, *refs[-3:])
    greet(targets)
    for stage in stages + gather:
        stage()


def plane_turn(grad, weight, middle, cot, order, collective_id, *before):
    shape = middle.shape
    return pl.pallas_call(
        functools.partial(turn_kernel, order),
        out_shape=[jax.ShapeDtypeStruct(shape, F32), gathered_shape(cot)],
        in_specs=[VMEM] * 4 + [ANY] * len(before),
        out_specs=[VMEM, ANY],
        scratch_shapes=[
            pltpu.VMEM(shape, BF16),
            *scatter_scratch(shape),
            *GATHER_SCRATCH,
        ],
        compiler_params=pltpu.CompilerParams(
            collective_id=collective_id,
            has_side_effects=True,
            vmem_limit_bytes=48 * 1024 * 1024,
        ),
        name="plane_turn",
    )(grad, weight, middle, cot, *before)


def last_kernel(order, owned, *refs):
    grad_a, weight_a, grad_b, weight_b, x, grad_middle, active, weight_down, middle = refs[:9]
    outs, scratch = refs[-22 - owned : -20], refs[-20:]

    def finish_grad(b, at, value):
        normed, inv = normalize(read_rows(x, b, at, order).astype(F32))
        value = grad_middle[b, at, :] + normalize_back(normed, inv, value)
        write_rows(outs[0], b, at, order, value)

    def finish_out(b, at, value):
        write_rows(outs[1], b, at, order, (middle[b, at, :] + value).astype(BF16))

    terms = ((grad_a, weight_a, True), (grad_b, weight_b, True))
    _, grads, swaps = scatter_stages(terms, finish_grad, *scratch[:9])
    _, out, _ = scatter_stages(
        ((active, weight_down, False),), finish_out, scratch[0], *scratch[9:17], earlier=swaps
    )
    targets, owners = owners_stages(refs[9 : 9 + owned], outs[2:], *scratch[17:])
    greet(targets)
    for stage in grads[:4] + out[:2]:
        stage()
    grads[4]()
    out[2]()
    out[3]()
    owners[0]()
    grads[5]()
    for stage in out[4:]:
        stage()
    owners[1]()


def plane_last(terms, x, grad_middle, summed, owned, order, collective_id, *before):
    shape = x.shape
    return pl.pallas_call(
        functools.partial(last_kernel, order, len(owned)),
        out_shape=[jax.ShapeDtypeStruct(shape, F32), jax.ShapeDtypeStruct(shape, BF16)]
        + [jax.ShapeDtypeStruct(a.shape, a.dtype) for a in owned],
        in_specs=[VMEM] * 9 + [ANY] * (len(owned) + len(before)),
        out_specs=[VMEM] * 2 + [ANY] * len(owned),
        scratch_shapes=scatter_scratch(shape)
        + scatter_scratch(shape)[1:]
        + owners_scratch(len(owned)),
        compiler_params=pltpu.CompilerParams(
            collective_id=collective_id,
            has_side_effects=True,
            vmem_limit_bytes=60 * 1024 * 1024,
        ),
        name="plane_last",
    )(*terms, x, grad_middle, *summed, *owned, *before)


def scan_kernel(count, forward, cuts, gathers, order, state, coef, *refs):
    targets, stages = (), ()
    if gathers:
        moved = refs[0]
        total, result, message, landed, send_sem, recv_sem = refs[-11:-5]
        shard, shard_sem = refs[-5:-3]
        targets, stages = gather_stages(shard, result, *refs[-3:])
    else:
        total, message, landed, send_sem, recv_sem = refs[-5:]
    here = lax.axis_index("pb")
    place = here if forward else count - 1 - here
    step = 1 if forward else -1
    has_prev = place > 0
    has_next = place < count - 1
    barrier = pltpu.get_barrier_semaphore()

    @pl.when(has_prev)
    def _():
        pl.semaphore_signal(barrier, inc=1, device_id={"pb": here - step}, device_id_type=MESH)

    @pl.when(has_next)
    def _():
        pl.semaphore_signal(barrier, inc=1, device_id={"pb": here + step}, device_id_type=MESH)

    greeted = has_prev.astype(jnp.int32) + has_next.astype(jnp.int32)
    for target in targets:
        pl.semaphore_signal(barrier, inc=1, device_id=target, device_id_type=MESH)
    pl.semaphore_wait(barrier, greeted + len(targets))

    height = state.shape[1] // cuts
    pieces = [(s, c) for s in range(state.shape[0]) for c in range(cuts)]

    def hop(i):
        s, c = pieces[i]
        rows = pl.ds(c * height, height)
        return pltpu.make_async_remote_copy(
            src_ref=message.at[s, rows],
            dst_ref=landed.at[s, rows],
            send_sem=send_sem.at[i],
            recv_sem=recv_sem.at[i],
            device_id={"pb": here + step},
            device_id_type=MESH,
        )

    def emit(i):
        s, c = pieces[i]
        rows = pl.ds(c * height, height)

        @pl.when(jnp.logical_not(has_prev))
        def _():
            message[s, rows] = state[s, rows].astype(BF16)
            hop(i).start()
            total[s, rows] = jnp.zeros((height, state.shape[2]), BF16)

        @pl.when(has_prev)
        def _():
            hop(i).wait_recv()
            total[s, rows] = (coef[0, s] * landed[s, rows].astype(F32)).astype(BF16)

            @pl.when(has_next)
            def _():
                message[s, rows] = (
                    state[s, rows] + coef[1, s] * total[s, rows].astype(F32)
                ).astype(BF16)
                hop(i).start()

    emit(0)
    if gathers:
        size = shard.shape[-1] // max(len(order), 1)
        for move in (0, 1):
            for j, i in enumerate(order or (0,)):
                copy = pltpu.make_async_copy(
                    moved.at[:, :, pl.ds(i * size, size)],
                    shard.at[:, :, pl.ds(j * size, size)],
                    shard_sem.at[j],
                )
                if move:
                    copy.wait()
                else:
                    copy.start()
        stages[0]()
    for i in range(1, len(pieces)):
        emit(i)
        if gathers and i == len(pieces) // 2:
            stages[1]()
        if gathers and i == 3 * len(pieces) // 4:
            stages[2]()
    if gathers:
        stages[3]()

    @pl.when(has_next)
    def _():
        for i in range(len(pieces)):
            hop(i).wait_send()


def line_scan(state, coef, count, forward, order, collective_id, *before, gathered=None):
    cuts = 4
    pieces = state.shape[0] * cuts
    shapes, specs, operands = [jax.ShapeDtypeStruct(state.shape, BF16)], [VMEM], [state, coef]
    scratch = [
        pltpu.VMEM(state.shape, BF16),
        pltpu.VMEM(state.shape, BF16),
        pltpu.SemaphoreType.DMA((pieces,)),
        pltpu.SemaphoreType.DMA((pieces,)),
    ]
    if gathered is not None:
        operands.append(gathered)
        shapes.append(gathered_shape(gathered))
        specs.append(ANY)
        scratch += [
            pltpu.VMEM(gathered.shape, gathered.dtype),
            pltpu.SemaphoreType.DMA((max(len(order), 1),)),
            *GATHER_SCRATCH,
        ]
    results = pl.pallas_call(
        functools.partial(scan_kernel, count, forward, cuts, gathered is not None, order),
        out_shape=shapes,
        in_specs=[VMEM, pl.BlockSpec(memory_space=pltpu.SMEM)]
        + [ANY] * (len(operands) - 2 + len(before)),
        out_specs=specs,
        scratch_shapes=scratch,
        compiler_params=pltpu.CompilerParams(
            collective_id=collective_id,
            has_side_effects=True,
            vmem_limit_bytes=16 * 1024 * 1024,
        ),
        name="line_scan",
    )(*operands, *before)
    return results if gathered is not None else results[0]


def owners_kernel(arrays, line, *refs):
    trades = 1 if line else 0
    scratch = refs[-3 - trades :]
    outs = refs[-3 - trades - arrays - trades : -3 - trades]
    targets, stages = owners_stages(refs[:arrays], outs[:arrays], *scratch[:3])
    barrier = pltpu.get_barrier_semaphore()
    for target in targets:
        pl.semaphore_signal(barrier, inc=1, device_id=target, device_id_type=MESH)
    greeted = len(targets)
    if line:
        greet_partner, trade = trade_stages(line, refs[arrays], outs[arrays], scratch[3])
        greeted = greeted + greet_partner(barrier)
    pl.semaphore_wait(barrier, greeted)
    stages[0]()
    if line:
        trade[0]()
        trade[1]()
    stages[1]()


def to_owners(arrays, collective_id, *before, line="", traded=()):
    count = len(arrays)
    operands = [*arrays, *traded]
    anywhere = pl.BlockSpec(memory_space=pl.ANY)
    return pl.pallas_call(
        functools.partial(owners_kernel, count, line),
        out_shape=[jax.ShapeDtypeStruct(a.shape, a.dtype) for a in operands],
        in_specs=[anywhere] * (len(operands) + len(before)),
        out_specs=[anywhere] * len(operands),
        scratch_shapes=owners_scratch(count) + (list(TRADE_SCRATCH) if line else []),
        compiler_params=pltpu.CompilerParams(
            collective_id=collective_id, has_side_effects=True
        ),
        name="to_owners",
    )(*operands, *before)


def normalize(values):
    mean = jnp.mean(values, axis=-1, keepdims=True)
    centered = values - mean
    inv = lax.rsqrt(jnp.mean(centered * centered, axis=-1, keepdims=True) + EPSILON)
    return centered * inv, inv


def normalize_back(normed, inv, grad):
    mean = jnp.mean(grad, axis=-1, keepdims=True)
    along = jnp.mean(grad * normed, axis=-1, keepdims=True)
    return inv * (grad - mean - normed * along)


def turn_tables(positions, half, direction):
    pair = jnp.arange(half, dtype=F32)
    frequency = jnp.exp(-jnp.log(10000.0) * pair / half)
    zeta = (pair / half + 0.4) / 1.4
    angles = positions[:, None] * frequency[None, :]
    factor = jnp.exp(direction * positions[:, None] / XPOS_BASE * jnp.log(zeta)[None, :])
    return jnp.cos(angles) * factor, jnp.sin(angles) * factor


def turn(values, tables):
    cosine, sine = tables
    half = values.shape[-1] // 2
    first, second = values[..., :half], values[..., half:]
    return jnp.concatenate(
        [first * cosine - second * sine, second * cosine + first * sine], axis=-1
    )


def turn_back(values, tables):
    cosine, sine = tables
    return turn(values, (cosine, -sine))


def mm(left, right):
    return jnp.einsum("sti,io->sto", left, right, preferred_element_type=F32)


def mm_back(left, right):
    return jnp.einsum("sto,io->sti", left, right, preferred_element_type=F32)


def mm_grad(left, right):
    return jnp.einsum("sti,sto->io", left, right, preferred_element_type=F32)


def after(value, *others):
    for other in others:
        value = value + (0.0 * other[(0,) * other.ndim].astype(F32)).astype(value.dtype)
    return value


def on_device(
    inputs,
    out_cotangent,
    doc_lengths,
    ln1_gain,
    w_query,
    w_key,
    w_value,
    w_gate,
    w_out,
    ln2_gain,
    w_up,
    up_bias,
    w_down,
):
    n_dph, n_dpl, n_pb, n_ka = (lax.axis_size(a) for a in ("dph", "dpl", "pb", "ka"))
    at_dpl, at_pb, at_ka = (lax.axis_index(a) for a in ("dpl", "pb", "ka"))
    batch, length, width = inputs.shape
    span = n_ka * length
    rows = w_query.shape[0]
    wide_rows = w_down.shape[0]
    key_width = w_query.shape[1] // H
    value_width = w_value.shape[1] // H
    units = n_dph * n_pb * wide_rows
    group = n_dpl * n_ka
    heads_pb = H // (n_dpl * n_dph)

    chunk = n_ka * rows

    def pick(values, order):
        return jnp.concatenate(
            [values[..., i * chunk : (i + 1) * chunk] for i in order], axis=-1
        )

    inner = [
        (d * n_dpl + r) * n_pb + p
        for d in range(n_dph)
        for p in range(n_pb)
        for r in range(n_dpl)
    ]

    def to_inner(values):
        return pick(values, inner)

    def to_outer(values):
        return pick(values, [inner.index(i) for i in range(len(inner))])

    def by_head(weight):
        cut = weight.reshape(rows, H // (n_dpl * heads_pb), n_dpl, heads_pb, -1)
        return jnp.transpose(cut, (2, 1, 3, 0, 4)).reshape(group, rows, -1)

    def from_head(values):
        cut = values.reshape(n_dpl, H // (n_dpl * heads_pb), heads_pb, rows, -1)
        return jnp.transpose(cut, (3, 1, 0, 2, 4)).reshape(rows, -1)

    def by_unit(weight):
        cut = weight.reshape(rows, n_dph, n_dpl, n_pb, n_ka, wide_rows)
        return jnp.transpose(cut, (2, 4, 0, 1, 3, 5)).reshape(group, rows, units)

    def from_unit(values):
        cut = values.reshape(n_dpl, n_ka, rows, n_dph, n_pb, wide_rows)
        return jnp.transpose(cut, (2, 3, 0, 4, 1, 5)).reshape(rows, -1)

    def gather_line(values):
        return lax.all_gather(values, LINE, axis=0, tiled=True)

    def scatter_line(values):
        return lax.psum_scatter(values, LINE, scatter_dimension=0, tiled=True)

    line = "dph" if n_dph > 1 else "pb"

    gain_one = ln1_gain.astype(BF16).astype(F32)[:, None]
    gain_two = ln2_gain.astype(BF16).astype(F32)[:, None]
    firsts = [w.astype(BF16) for w in (w_query, w_key, w_value, w_gate)]
    up_low = w_up.astype(BF16)

    def scaled(weight, gain):
        return (weight.astype(F32) * gain).astype(BF16)

    query_pack, key_pack, value_pack, gate_pack = (by_head(scaled(w, gain_one)) for w in firsts)
    qkv_swapped, gate_swapped = to_owners(
        [jnp.concatenate([query_pack, key_pack, value_pack], axis=-1), gate_pack], 0
    )
    order = tuple(inner) if chunk % 128 == 0 else ()
    rows_in, rows_cot = inputs, out_cotangent
    if not order:
        rows_in, rows_cot = to_inner(inputs), to_inner(out_cotangent)
    head = (
        (at_ka // heads_pb) * (n_dpl * heads_pb) + at_dpl * heads_pb + at_ka % heads_pb
    ).astype(F32)
    log_gamma = jnp.log(1.0 - jnp.exp2(-5.0 - head))
    offsets = jnp.arange(span, dtype=jnp.int32)
    places = (at_pb * span + offsets).astype(F32)
    tables_q = turn_tables(places, key_width // 2, 1.0)
    tables_k = turn_tables(places, key_width // 2, -1.0)
    distance = offsets[:, None] - offsets[None, :]
    decay = jnp.where(
        distance >= 0, jnp.exp(jnp.maximum(distance, 0).astype(F32) * log_gamma), 0.0
    )
    decay_in = jnp.exp(offsets.astype(F32) * log_gamma)[:, None]
    decay_out = jnp.exp((span - offsets).astype(F32) * log_gamma)[:, None]
    decay_span = jnp.exp(span * log_gamma)
    lengths = lax.all_gather(doc_lengths, "dpl", axis=0, tiled=True)
    ends = jnp.cumsum(lengths, axis=-1)
    edge = at_pb * span

    def goes_on(start):
        return jnp.all(ends != start, axis=-1).astype(F32)

    coef_forward = jnp.stack([goes_on(edge), jnp.full((n_dpl * batch,), decay_span)])
    coef_backward = jnp.stack([goes_on(edge + span), jnp.full((n_dpl * batch,), decay_span)])

    down_pack = jnp.concatenate(
        [
            to_inner(w_down.astype(BF16)),
            jnp.broadcast_to(up_bias.astype(BF16)[:, None], (wide_rows, 128)),
        ],
        axis=-1,
    )
    normed_one_all, up_swapped, out_moved = open_plane(
        rows_in,
        by_unit(scaled(up_low, gain_two)),
        to_inner(w_out.astype(BF16)),
        line,
        order,
        1,
        qkv_swapped,
        down_pack,
        coef_forward,
        coef_backward,
        *tables_q,
        *tables_k,
        decay,
    )
    weight_qkv = gather_line(qkv_swapped.reshape(group * rows, -1))
    blocks = width // units
    gate_out = jnp.concatenate(
        [after(gate_swapped.reshape(group * rows, -1), normed_one_all)]
        + [out_moved[:, i * units : (i + 1) * units] for i in range(blocks)],
        axis=0,
    )
    gate_out = gather_line(gate_out)
    first = mm(normed_one_all, weight_qkv)
    query_pre = first[..., :key_width]
    key_pre = first[..., key_width : 2 * key_width]
    value = first[..., 2 * key_width :].astype(BF16)
    scale = key_width ** (-0.5)
    query = (turn(query_pre, tables_q) * scale).astype(BF16)
    key = turn(key_pre, tables_k).astype(BF16)
    key_out = (key.astype(F32) * decay_out).astype(BF16)
    state = jnp.einsum("smd,sme->sde", key_out, value, preferred_element_type=F32)
    carried, cot_all = line_scan(
        state, coef_forward, n_pb, True, order, 2, gathered=rows_cot
    )
    raw = jnp.einsum("snd,smd->snm", query, key, preferred_element_type=F32)
    scores = (raw * decay).astype(BF16)
    retained = jnp.einsum("snm,sme->sne", scores, value, preferred_element_type=F32)
    retained = retained + decay_in * jnp.einsum(
        "snd,sde->sne", query, carried, preferred_element_type=F32
    )
    gate_out = after(gate_out, retained).reshape(n_dph * n_pb, -1, units)
    weight_gate = gate_out[:, : group * rows].reshape(width, units)
    weight_out = (
        gate_out[:, group * rows :]
        .reshape(-1, n_pb // heads_pb, blocks, wide_rows, units)
        .transpose(1, 0, 3, 2, 4)
        .reshape(value_width, width)
    )
    weight_up = gather_line(after(up_swapped.reshape(group * rows, -1), weight_out))
    down_pack = gather_line(after(down_pack, weight_out))
    weight_down = down_pack[:, :width]
    bias_up = down_pack[:, width].astype(F32)
    normed_ret, inv_ret = normalize(retained)
    gate = mm(normed_one_all, weight_gate)
    opened = jax.nn.sigmoid(gate)
    silu = gate * opened
    gated = (silu * normed_ret).astype(BF16)
    middle, normed_two_all = plane_mix(gated, weight_out, rows_in, order, 3)
    up_pre = mm(normed_two_all, weight_up) + bias_up
    bell = 0.5 * (1.0 + lax.erf(up_pre * np.float32(math.sqrt(0.5))))
    active = (up_pre * bell).astype(BF16)

    slope = bell + up_pre * (
        jnp.exp(-0.5 * up_pre * up_pre) * np.float32(1.0 / math.sqrt(2.0 * math.pi))
    )
    grad_up_pre = (mm_back(cot_all, weight_down) * slope).astype(BF16)
    grad_bias = jnp.sum(grad_up_pre.astype(F32), axis=(0, 1)).astype(BF16)
    grad_down = jnp.concatenate(
        [
            mm_grad(active, cot_all).astype(BF16),
            jnp.broadcast_to(grad_bias[:, None], (units, 128)),
        ],
        axis=-1,
    )
    grad_up = mm_grad(normed_two_all, grad_up_pre).astype(BF16)
    grad_middle, grad_mid_all = plane_turn(
        grad_up_pre, weight_up, middle, rows_cot, order, 5, grad_down, grad_up
    )
    grad_down = scatter_line(grad_down)
    grad_up = scatter_line(grad_up)
    grad_gated = after(mm_back(grad_mid_all, weight_out), grad_up, grad_down)
    grad_gate = (grad_gated * normed_ret * (opened + silu * (1.0 - opened))).astype(BF16)
    grad_ret = normalize_back(normed_ret, inv_ret, grad_gated * silu).astype(BF16)
    query_in = (query.astype(F32) * decay_in).astype(BF16)
    grad_state = jnp.einsum("snd,sne->sde", query_in, grad_ret, preferred_element_type=F32)
    grad_out = mm_grad(gated, grad_mid_all).astype(BF16)
    grad_out = (
        grad_out.reshape(n_pb // heads_pb, -1, wide_rows, width)
        .swapaxes(0, 1)
        .reshape(value_width, width)
    )
    grad_gate_w = mm_grad(normed_one_all, grad_gate).astype(BF16)
    grad_carried = line_scan(
        grad_state,
        coef_backward,
        n_pb,
        False,
        order,
        7,
        grad_gate_w,
        grad_out,
    )
    grad_gate_w = scatter_line(grad_gate_w)
    grad_out = scatter_line(grad_out)
    grad_scores = (
        jnp.einsum("sne,sme->snm", grad_ret, value, preferred_element_type=F32) * decay
    ).astype(BF16)
    grad_query = jnp.einsum("snm,smd->snd", grad_scores, key, preferred_element_type=F32)
    grad_query = grad_query + decay_in * jnp.einsum(
        "sne,sde->snd", grad_ret, carried, preferred_element_type=F32
    )
    grad_key = jnp.einsum("snm,snd->smd", grad_scores, query, preferred_element_type=F32)
    grad_key = grad_key + decay_out * jnp.einsum(
        "sme,sde->smd", value, grad_carried, preferred_element_type=F32
    )
    grad_value = jnp.einsum("snm,sne->sme", scores, grad_ret, preferred_element_type=F32)
    grad_value = grad_value + decay_out * jnp.einsum(
        "smd,sde->sme", key, grad_carried, preferred_element_type=F32
    )
    grad_qkv = jnp.concatenate(
        [
            (turn_back(grad_query, tables_q) * scale).astype(BF16),
            turn_back(grad_key, tables_k).astype(BF16),
            grad_value.astype(BF16),
        ],
        axis=-1,
    )
    grad_qkv_w = mm_grad(normed_one_all, after(grad_qkv, grad_gate_w)).astype(BF16)
    grad_qkv_sum = scatter_line(grad_qkv_w)
    cut = (group, rows, -1)
    grad_inputs, output, back_up, back_gate = plane_last(
        (grad_qkv, weight_qkv, grad_gate, weight_gate),
        rows_in,
        grad_middle,
        (active, down_pack, middle),
        (grad_up.reshape(cut), grad_gate_w.reshape(cut)),
        order,
        8,
        grad_qkv_w,
    )
    if not order:
        output, grad_inputs = to_outer(output), to_outer(grad_inputs)

    shard_down = to_outer(grad_down[:, :width].astype(F32))
    shard_bias = grad_down[:, width].astype(F32)
    back, shard_out = to_owners(
        [grad_qkv_sum.reshape(cut)], 9, grad_inputs, line=line, traded=(grad_out,)
    )
    shard_out = to_outer(shard_out.astype(F32))
    shard_up = from_unit(back_up).astype(F32)
    shard_gate = from_head(back_gate).astype(F32)
    shard_query = from_head(back[..., :key_width]).astype(F32)
    shard_key = from_head(back[..., key_width : 2 * key_width]).astype(F32)
    shard_value = from_head(back[..., 2 * key_width :]).astype(F32)
    shards = (shard_query, shard_key, shard_value, shard_gate)
    shard_gain_one = sum(
        jnp.sum(low.astype(F32) * grad, axis=-1) for low, grad in zip(firsts, shards)
    )
    shard_gain_two = jnp.sum(up_low.astype(F32) * shard_up, axis=-1)
    shard_query, shard_key, shard_value, shard_gate = (gain_one * g for g in shards)
    return (
        output,
        grad_inputs,
        shard_gain_one,
        shard_query,
        shard_key,
        shard_value,
        shard_gate,
        shard_out,
        shard_gain_two,
        gain_two * shard_up,
        shard_bias,
        shard_down,
    )


def solution(mesh):
    dp, pb, ka = (mesh.shape[a] for a in ("dp", "pb", "ka"))
    fine = Mesh(mesh.devices.reshape(dp // 2, 2, pb, ka), ("dph", "dpl", "pb", "ka"))
    dp_axes = ("dph", "dpl")
    every = ("dph", "dpl", "pb", "ka")
    tokens = P(dp_axes, ("pb", "ka"), None)
    matrix = P(every, None)
    vector = P(every)
    return jax.shard_map(
        on_device,
        mesh=fine,
        in_specs=(
            tokens,
            tokens,
            P(dp_axes, None),
            vector,
            matrix,
            matrix,
            matrix,
            matrix,
            matrix,
            vector,
            matrix,
            vector,
            matrix,
        ),
        out_specs=(
            tokens,
            tokens,
            vector,
            matrix,
            matrix,
            matrix,
            matrix,
            matrix,
            vector,
            matrix,
            vector,
            matrix,
        ),
        check_vma=False,
    )
```

time: 874 us -> 807 us (0.923)
  Pallas kernels: 425 us -> 503 us
  matrix products: 164 us -> 126 us
  waiting for transfers between devices: 61.4 us -> 29 us
  starting transfers between devices: 32.7 us -> 0.37 us
  blocking collectives: 32.2 us -> 4.25 us
    pallas_call x10 -> x8, Pallas kernels: 425 us -> 503 us  [the longest x2 122 us: line_scan(): pl.pallas_call(functools.partial(scan_kernel, count, forward, cuts, gathe...]
    dot_general x5 -> x2, matrix products: 56.4 us -> 20.7 us  [mm_back(): return jnp.einsum('sto,io->sti', left, right, preferred_element_type=F32)]
    all_to_all x6 -> x0, starting transfers between devices: 31.7 us -> none  [the longest x3 15.6 us: swap_plane_back(): return lax.all_to_all(cut, PLANE, split_axis=0, concat_axis=1, tiled=True)]
    all_to_all x1 -> x0, blocking collectives: 23.8 us -> none  [swap_plane(): lax.all_to_all(values, PLANE, split_axis=1, concat_axis=0, tiled=True)]
    all_gather x4, waiting for transfers between devices: 50.3 us -> 28.8 us  [gather_line(): return lax.all_gather(values, LINE, axis=0, tiled=True)]
    dot_general x5, matrix products: 44 us -> 58.1 us  [mm_grad(): return jnp.einsum('sti,sto->io', left, right, preferred_element_type=F32)]
    all_to_all x6 -> x0, waiting for transfers between devices: 10.9 us -> none  [the longest x1 10.8 us: on_device(): lax.all_to_all(grad_out, 'ka', split_axis=0, concat_axis=0, tiled=True)]
    convert_element_type x7 -> x5, local copies, waits for them, and re-layouts: 13.2 us -> 3.8 us  [the longest x2 2.37 us: on_device(): shard_gate = from_head(back_gate).astype(F32)]
  transfers between devices with their start and end apart: 15 -> 9, of which waited for: 2 -> 2; matrix products, arithmetic and copies ran while one was open for 28% -> 16% of each run, Pallas kernels for 49% -> 57%
where the time goes in v2:
time: 807 us; the launch traced here: 802 us
  Pallas kernels  503 us (62%)
  matrix products  126 us (16%)
  local copies, waits for them, and re-layouts  75.8 us (9%)
  other arithmetic  44.6 us (6%)
  waiting for transfers between devices  29 us (4%)
  between operations  19.6 us (2%)
    pallas_call x2, Pallas kernels, line_scan(): pl.pallas_call(functools.partial(scan_kernel, count, forward, cuts, gathe...  122 us
    pallas_call x1, Pallas kernels, plane_last(): pl.pallas_call(functools.partial(last_kernel, order, len(owned)), out_sha...  99.3 us
    pallas_call x1, Pallas kernels, plane_turn(): pl.pallas_call(functools.partial(turn_kernel, order), out_shape=[jax.Shap...  86.5 us
    pallas_call x1, Pallas kernels, plane_mix(): pl.pallas_call(functools.partial(mix_kernel, order), out_shape=[jax.Shape...  85.3 us
    pallas_call x1, Pallas kernels, open_plane(): pl.pallas_call(lambda a, b, c, *refs: open_kernel(line, order, a, b, c, *...  62.3 us
    dot_general x5, matrix products, mm_grad(): return jnp.einsum('sti,sto->io', left, right, preferred_element_type=F32)  58.1 us
    pallas_call x2, Pallas kernels, to_owners(): pl.pallas_call(functools.partial(owners_kernel, count, line), out_shape=[...  47.7 us
    unnamed x174, local copies, waits for them, and re-layouts  44.2 us
  transfers between devices with their start and end apart: 9, of which 2 were waited for; matrix products, arithmetic and copies ran while one was open for 16% of the time, Pallas kernels for 57%

profile of v2, /device:TPU:2, one launch (start us, length us, event | category | flops | bytes accessed | tf_op | source)
XLA Modules:
  0.0 802.5 jit_solution(17042730097106405386)
XLA Ops:
  12.7 2.1 pad_maximum_fusion.2.refs_0_
  14.9 21.5 %to_owners.2 = (bf16[8,64,1024]{2,1,0:T(8,128)(2,1)}, bf16[8,64,512]{2,1,0:T(8,128)(2,1)}) custom-call(bf16[8,64,1024]{2,1,0:T(8,128)(2,1)} %pad_maximum_fusion.2.refs_0_, bf16[8,64,512]{2,1,0:T(8,128)(2,1)} %bitcast.140), custom_call_target="tpu_custom_call" | custom-call | tf_op jit(solution)/shard_map/to_owners/pallas_call | solution.py:727
  36.7 4.2 all-gather
  43.1 2.2 convert_element_type.344
  45.3 1.6 reshape.568
  62.1 1.9 fusion.35
  64.0 62.3 %open_plane.1 = (bf16[4,512,2048]{2,1,0:T(8,128)(2,1)S(1)}, bf16[8,64,512]{2,1,0:T(8,128)(2,1)S(1)}, bf16[128,2048]{1,0:T(8,128)(2,1)S(1)}) custom-call(bf16[2,128,2048]{2,1,0:T(8,128)(2,1)S(1)} %copy-done, bf16[8,64,512]{2,1,0:T(8,128)(2,1)S(1)} %copy-done.21, bf16[128,2048]{1,0:T(8,128)(2,1)S(1)} %constant_dynamic-update-slice_fusion.c, ...), custom_call_target="tpu_custom_call" | custom-call | tf_op jit(solution)/shard_map/open_plane/pallas_call | solution.py:265
  127.8 2.0 copy-done.24
  131.0 12.5 %fusion.6 = f32[4,512,1024]{2,1,0:T(8,128)S(1)} fusion(bf16[4,512,2048]{2,1,0:T(8,128)(2,1)} %copy-done.24, bf16[2048,1024]{1,0:T(8,128)(2,1)} %all-gather.6.cloned.1.call-done.refs_1_), kind=kOutput, calls=%fused_computation.14 | convolution fusion | flops 8589934592 | bytes 20971520 | tf_op jit(solution)/shard_map/sti,io->sto/dot_general | solution.py:777
  146.2 56.5 %line_scan.2 = (bf16[4,256,512]{2,1,0:T(8,128)(2,1)S(1)}, bf16[4,512,2048]{2,1,0:T(8,128)(2,1)S(1)}) custom-call(f32[4,256,512]{2,1,0:T(8,128)S(1)} %fusion.22.state, f32[2,4]{1,0:T(2,128)S(1)} %stack.8.refs_2_.coef, bf16[2,128,2048]{2,1,0:T(8,128)(2,1)S(1)} %copy-done.4), custom_call_target="tpu_custom_call" | custom-call | tf_op jit(solution)/shard_map/line_scan/pallas_call | solution.py:686
  202.7 3.3 copy-done.25
  209.2 2.0 copy-done.27
  212.3 27.3 %all-gather.8.cloned.1.call-done = bf16[4096,512]{1,0:T(8,128)(2,1)} async-done(((bf16[1024,512]{1,0:T(8,128)(2,1)}), bf16[4096,512]{1,0:T(8,128)(2,1)}) %all-gather.8.cloned.1.call-update) | async-done | bytes 4194320 | tf_op jit(solution)/shard_map/all_gather | solution.py:858
  239.6 2.5 broadcast_add_fusion
  242.1 1.6 fusion.42
  243.7 1.6 copy.158
  250.8 1.9 broadcast_add_fusion.2
  252.7 3.0 multiply_reduce_fusion.1
  256.2 9.6 %multiply_convert_fusion.4 = (bf16[4,512,512]{2,1,0:T(8,128)(2,1)S(1)}, f32[4,512,512]{2,1,0:T(8,128)}) fusion(f32[4,512,512]{2,1,0:T(8,128)S(1)} %copy-done.28, f32[4,512]{1,0:T(4,128)S(1)} %add_rsqrt_fusion, f32[4,512]{1,0:T(4,128)S(1)} %broadcast_multiply_fusion.7, bf16[4,512,2048]{2,1,0:T(8,128)(2,1)} %copy-done.24, bf16[2048,512,1]{1,0,2:T(8,128)(2,1)} %bitcast.136), kind=kOutput, calls=%fused_computation.25 | convolution fusion | flops 4303355904 | bytes 20987904 | tf_op jit(solution)/shard_map/sti,io->sto/dot_general | solution.py:777
  265.8 85.3 %plane_mix.1 = (f32[2,128,2048]{2,1,0:T(8,128)S(1)}, bf16[4,512,2048]{2,1,0:T(8,128)(2,1)}) custom-call(bf16[4,512,512]{2,1,0:T(8,128)(2,1)S(1)} %get-tuple-element.97.gated, bf16[512,2048]{1,0:T(8,128)(2,1)} %bitcast.134, bf16[2,128,2048]{2,1,0:T(8,128)(2,1)S(1)} %copy-done), custom_call_target="tpu_custom_call" | custom-call | tf_op jit(solution)/shard_map/plane_mix/pallas_call | solution.py:463
  354.7 1.4 all-gather.12.cloned.1.call-done.weight
  356.2 10.6 %multiply_convert_fusion.3 = (bf16[4,512,512]{2,1,0:T(8,128)(2,1)}, f32[4,512,512]{2,1,0:T(8,128)S(1)}) fusion(f32[512]{0:T(512)S(1)} %convert_reduce_fusion, bf16[4,512,2048]{2,1,0:T(8,128)(2,1)} %get-tuple-element.35, bf16[2048,512]{1,0:T(8,128)(2,1)} %all-gather.12.cloned.1.call-done.weight), kind=kOutput, calls=%fused_computation.23 | convolution fusion | flops 4301258752 | bytes 16779264 | tf_op jit(solution)/shard_map/sti,io->sto/dot_general | solution.py:777
  366.8 8.5 %fusion.45 = (bf16[512]{0:T(512)(128)(2,1)S(1)}, bf16[4,512,512]{2,1,0:T(8,128)(2,1)S(1)}) fusion(f32[4,512,512]{2,1,0:T(8,128)S(1)} %get-tuple-element.102, f32[512]{0:T(512)S(1)} %convert_reduce_fusion, bf16[4,512,2048]{2,1,0:T(8,128)(2,1)} %copy-done.25, bf16[512,2176]{1,0:T(8,128)(2,1)S(1)} %copy-done.48), kind=kOutput, calls=%fused_computation.172 | convolution fusion | flops 4307549696 | bytes 16780288 | tf_op jit(solution)/shard_map/sto,io->sti/dot_general | solution.py:781
  375.3 17.6 %bitcast_convert_fusion.3.refs_1_ = bf16[2048,512]{1,0:T(8,128)(2,1)} fusion(bf16[4,512,2048]{2,1,0:T(8,128)(2,1)S(1)} %bitcast.156, bf16[4,512,512]{2,1,0:T(8,128)(2,1)S(1)} %get-tuple-element.100.grad), kind=kOutput, calls=%fused_computation.12 | convolution fusion | flops 4296015872 | bytes 12582912 | tf_op jit(solution)/shard_map/sti,sto->io/dot_general | solution.py:785
  392.8 1.4 copy-done.19
  394.3 8.6 %bitcast_convert_fusion.4 = bf16[512,2048]{1,0:T(8,128)(2,1)S(1)} fusion(bf16[4,512,512]{2,1,0:T(8,128)(2,1)} %get-tuple-element.101.refs_6_, bf16[4,512,2048]{2,1,0:T(8,128)(2,1)} %copy-done.25), kind=kOutput, calls=%fused_computation.13 | convolution fusion | flops 4296015872 | bytes 12582912 | tf_op jit(solution)/shard_map/sti,sto->io/dot_general | solution.py:785
  403.0 1.6 pad_maximum_fusion.1.refs_0_
  404.7 4.5 reshape.608
  409.2 1.9 copy-done.20
  411.1 86.5 %plane_turn.1 = (f32[2,128,2048]{2,1,0:T(8,128)S(1)}, bf16[4,512,2048]{2,1,0:T(8,128)(2,1)}) custom-call(bf16[4,512,512]{2,1,0:T(8,128)(2,1)S(1)} %copy-done.20, bf16[2048,512]{1,0:T(8,128)(2,1)} %all-gather.12.cloned.1.call-done.weight, f32[2,128,2048]{2,1,0:T(8,128)} %copy-done.3, bf16[2,128,2048]{2,1,0:T(8,128)(2,1)S(1)} %copy-done.4, ...), custom_call_target="tpu_custom_call" | custom-call | tf_op jit(solution)/shard_map/plane_turn/pallas_call | solution.py:501
  497.6 1.4 copy-done.22
  502.6 12.3 %fusion.40 = (f32[4,512]{1,0:T(4,128)S(1)}, f32[4,512]{1,0:T(4,128)S(1)}, f32[4,512,512]{2,1,0:T(8,128)}, bf16[4,512,512]{2,1,0:T(8,128)(2,1)S(1)}) fusion(f32[4,512]{1,0:T(4,128)S(1)} %add_rsqrt_fusion, f32[4,512,512]{2,1,0:T(8,128)} %copy-done.27, f32[4,512]{1,0:T(4,128)S(1)} %broadcast_multiply_fusion.7, f32[4,512,512]{2,1,0:T(8,128)} %get-tuple-element.98, ...), kind=kOutput, calls=%fused_computation.168 | convolution fusion | flops 4313837568 | bytes 25198600 | tf_op jit(solution)/shard_map/sto,io->sti/dot_general | solution.py:781
  514.9 1.4 copy-done.50
  516.2 9.6 %bitcast_convert_fusion.2.refs_0_ = bf16[2048,512]{1,0:T(8,128)(2,1)} fusion(bf16[4,512,2048]{2,1,0:T(8,128)(2,1)} %copy-done.24, bf16[4,512,512]{2,1,0:T(8,128)(2,1)S(1)} %get-tuple-element.51.refs_2_), kind=kOutput, calls=%fused_computation.11 | convolution fusion | flops 4296015872 | bytes 12582912 | tf_op jit(solution)/shard_map/sti,sto->io/dot_general | solution.py:785
  525.9 9.1 %bitcast_convert_fusion.1.refs_1_ = bf16[512,2048]{1,0:T(8,128)(2,1)} fusion(bf16[4,512,512]{2,1,0:T(8,128)(2,1)S(1)} %copy-done.18, bf16[4,512,2048]{2,1,0:T(8,128)(2,1)} %get-tuple-element.38), kind=kOutput, calls=%fused_computation.10 | convolution fusion | flops 4296015872 | bytes 12582912 | tf_op jit(solution)/shard_map/sti,sto->io/dot_general | solution.py:785
  535.1 4.5 multiply_convert_fusion.2
  539.7 4.0 multiply_convert_fusion.1
  550.4 65.9 %line_scan.3 = bf16[4,256,512]{2,1,0:T(8,128)(2,1)S(1)} custom-call(f32[4,256,512]{2,1,0:T(8,128)S(1)} %fusion.23.state, f32[2,4]{1,0:T(2,128)S(1)} %stack.9.refs_3_.coef, bf16[2048,512]{1,0:T(8,128)(2,1)S(1)} %copy-done.2, bf16[512,2048]{1,0:T(8,128)(2,1)S(1)} %copy-done.1), custom_call_target="tpu_custom_call" | custom-call | tf_op jit(solution)/shard_map/line_scan/pallas_call | solution.py:686
  621.9 13.3 %bitcast_convert_fusion.refs_11_ = bf16[2048,1024]{1,0:T(8,128)(2,1)} fusion(bf16[4,512,2048]{2,1,0:T(8,128)(2,1)} %copy-done.24, bf16[]{:T(256)} %bitcast.35, bf16[4,512,512]{2,1,0:T(8,128)(2,1)S(1)} %add_convert_fusion, bf16[4,512,128]{2,1,0:T(8,128)(2,1)} %get-tuple-element.63, bf16[4,512,128]{2,1,0:T(8,128)(2,1)} %get-tuple-element.62, ...), kind=kOutput, calls=%fused_computation | convolution fusion | flops 8613003264 | bytes 16777218 | tf_op jit(solution)/shard_map/sti,sto->io/dot_general | solution.py:785
  635.3 1.4 convert_reduce_fusion.1
  643.1 3.4 pad_maximum_fusion.refs_0_
  646.5 99.3 %plane_last.1 = (f32[2,128,2048]{2,1,0:T(8,128)}, bf16[2,128,2048]{2,1,0:T(8,128)(2,1)}, bf16[8,64,512]{2,1,0:T(8,128)(2,1)}, bf16[8,64,512]{2,1,0:T(8,128)(2,1)}) custom-call(bf16[4,512,1024]{2,1,0:T(8,128)(2,1)} %pad_maximum_fusion.refs_0_, bf16[2048,1024]{1,0:T(8,128)(2,1)} %all-gather.6.cloned.1.call-done.refs_1_, bf16[4,512,512]{2,1,0:T(8,128)(2,1)} %copy-done.50, ...), custom_call_target="tpu_custom_call" | custom-call | tf_op jit(solution)/shard_map/plane_last/pallas_call | solution.py:553
  747.8 1.7 reshape.592
  750.9 1.7 broadcast_multiply_fusion.2
  752.7 26.2 %to_owners.3 = (bf16[8,64,1024]{2,1,0:T(8,128)(2,1)}, bf16[128,2048]{1,0:T(8,128)(2,1)}) custom-call(bf16[8,64,1024]{2,1,0:T(8,128)(2,1)} %bitcast.145, bf16[128,2048]{1,0:T(8,128)(2,1)} %reduce-scatter.14.cloned.1.call-done.refs_1_, f32[2,128,2048]{2,1,0:T(8,128)} %get-tuple-element.120.refs_2_), custom_call_target="tpu_custom_call" | custom-call | tf_op jit(solution)/shard_map/to_owners/pallas_call | solution.py:727
  785.9 1.7 reshape.591
  787.8 3.3 broadcast_multiply_fusion.3
  791.1 1.8 broadcast_multiply_fusion
  (276 shorter events, 73.5 us)
Async XLA Ops:
  7.2 3.4 copy-start.42
  7.2 123.8 %all-gather.6.cloned.1.call-start = ((), (), s32[]{:S(2)}) async-start(), calls=%async_computation.5 | async-start | bytes 5242880 | tf_op jit(solution)/shard_map/all_gather | solution.py:858
  8.0 4.1 copy-start.58
  11.2 25.4 %copy-start.63 = (f32[64]{0:T(128)S(1)}, f32[64]{0:T(128)}, u32[]{:S(2)}) copy-start(f32[64]{0:T(128)} %param.22) | copy-start | bytes 772
  11.2 25.5 %copy-start.64 = (f32[128]{0:T(128)S(1)}, f32[128]{0:T(128)}, u32[]{:S(2)}) copy-start(f32[128]{0:T(128)} %param.24) | copy-start | bytes 1540
  11.2 25.5 %copy-start.62 = (s32[2,4]{1,0:T(2,128)S(1)}, s32[2,4]{1,0:T(2,128)}, u32[]{:S(2)}) copy-start(s32[2,4]{1,0:T(2,128)} %param.15) | copy-start | bytes 100
  11.2 30.0 %copy-start.40 = (f32[64,4096]{1,0:T(8,128)S(1)}, f32[64,4096]{1,0:T(8,128)}, u32[]{:S(2)}) copy-start(f32[64,4096]{1,0:T(8,128)} %param.23) | copy-start | bytes 3145732
  12.6 29.7 %copy-start.52 = (f32[128,2048]{1,0:T(8,128)S(1)}, f32[128,2048]{1,0:T(8,128)}, u32[]{:S(2)}) copy-start(f32[128,2048]{1,0:T(8,128)} %param.21) | copy-start | bytes 3145732
  36.4 203.2 %all-gather.8.cloned.1.call-start = ((), (), s32[]{:S(2)}) async-start(), calls=%async_computation.6 | async-start | bytes 5242880 | tf_op jit(solution)/shard_map/all_gather | solution.py:858
  36.7 11.6 %copy-start.60 = (f32[64]{0:T(128)}, f32[64]{0:T(128)S(1)}, u32[]{:S(2)}) copy-start(f32[64]{0:T(128)S(1)} %convert_convert_fusion.1) | copy-start | bytes 772
  45.3 18.7 %copy-start = (bf16[2,128,2048]{2,1,0:T(8,128)(2,1)S(1)}, bf16[2,128,2048]{2,1,0:T(8,128)(2,1)}, u32[]{:S(2)}) copy-start(bf16[2,128,2048]{2,1,0:T(8,128)(2,1)} %refs_4_.1) | copy-start | bytes 3145732
  45.3 18.7 %copy-start.7 = (bf16[8,64,1024]{2,1,0:T(8,128)(2,1)S(1)}, bf16[8,64,1024]{2,1,0:T(8,128)(2,1)}, u32[]{:S(2)}) copy-start(bf16[8,64,1024]{2,1,0:T(8,128)(2,1)} %get-tuple-element.29.refs_0_) | copy-start | bytes 3145732
  48.1 16.0 %copy-start.21 = (bf16[8,64,512]{2,1,0:T(8,128)(2,1)S(1)}, bf16[8,64,512]{2,1,0:T(8,128)(2,1)}, u32[]{:S(2)}) copy-start(bf16[8,64,512]{2,1,0:T(8,128)(2,1)} %reshape.569.b) | copy-start | bytes 1572868
  55.2 71.2 %copy-start.11 = (bf16[128,2176]{1,0:T(8,128)(2,1)}, bf16[128,2176]{1,0:T(8,128)(2,1)S(1)}, u32[]{:S(2)}) copy-start(bf16[128,2176]{1,0:T(8,128)(2,1)S(1)} %constant_dynamic-update-slice_fusion.8.refs_1_) | copy-start | bytes 1671172
  56.1 71.5 %copy-start.56 = (bf16[8,64,512]{2,1,0:T(8,128)(2,1)S(1)}, bf16[8,64,512]{2,1,0:T(8,128)(2,1)}, u32[]{:S(2)}) copy-start(bf16[8,64,512]{2,1,0:T(8,128)(2,1)} %get-tuple-element.33) | copy-start | bytes 1572868
  64.0 63.8 %copy-start.8 = (f32[512,128]{1,0:T(8,128)}, f32[512,128]{1,0:T(8,128)S(1)}, u32[]{:S(2)}) copy-start(f32[512,128]{1,0:T(8,128)S(1)} %get-tuple-element.80.refs_4_) | copy-start | bytes 786436
  64.0 63.8 %copy-start.13 = (f32[512,128]{1,0:T(8,128)}, f32[512,128]{1,0:T(8,128)S(1)}, u32[]{:S(2)}) copy-start(f32[512,128]{1,0:T(8,128)S(1)} %get-tuple-element.79.refs_5_) | copy-start | bytes 786436
  64.0 63.8 %copy-start.15 = (f32[512,128]{1,0:T(8,128)}, f32[512,128]{1,0:T(8,128)S(1)}, u32[]{:S(2)}) copy-start(f32[512,128]{1,0:T(8,128)S(1)} %get-tuple-element.84.refs_7_) | copy-start | bytes 786436
  126.4 3.5 copy-start.24
  130.8 222.8 %all-gather.10.cloned.1.call-start = ((), (), s32[]{:S(2)}) async-start(), calls=%async_computation.7 | async-start | bytes 2785280 | tf_op jit(solution)/shard_map/all_gather | solution.py:858
  130.9 12.6 %copy-start.9 = (f32[512,128]{1,0:T(8,128)S(1)}, f32[512,128]{1,0:T(8,128)}, u32[]{:S(2)}) copy-start(f32[512,128]{1,0:T(8,128)} %copy-done.8) | copy-start | bytes 786436
  130.9 12.6 %copy-start.14 = (f32[512,128]{1,0:T(8,128)S(1)}, f32[512,128]{1,0:T(8,128)}, u32[]{:S(2)}) copy-start(f32[512,128]{1,0:T(8,128)} %copy-done.13) | copy-start | bytes 786436
  130.9 12.6 %copy-start.16 = (f32[512,128]{1,0:T(8,128)S(1)}, f32[512,128]{1,0:T(8,128)}, u32[]{:S(2)}) copy-start(f32[512,128]{1,0:T(8,128)} %copy-done.15) | copy-start | bytes 786436
  143.6 63.4 %copy-start.26 = (f32[4,512,1024]{2,1,0:T(8,128)}, f32[4,512,1024]{2,1,0:T(8,128)S(1)}, u32[]{:S(2)}) copy-start(f32[4,512,1024]{2,1,0:T(8,128)S(1)} %fusion.6) | copy-start | bytes 25165828
  144.2 62.0 %copy-start.34 = (bf16[4,512,128]{2,1,0:T(8,128)(2,1)}, bf16[4,512,128]{2,1,0:T(8,128)(2,1)S(1)}, u32[]{:S(2)}) copy-start(bf16[4,512,128]{2,1,0:T(8,128)(2,1)S(1)} %get-tuple-element.52) | copy-start | bytes 1572868
  144.2 62.0 %copy-start.36 = (bf16[4,512,128]{2,1,0:T(8,128)(2,1)}, bf16[4,512,128]{2,1,0:T(8,128)(2,1)S(1)}, u32[]{:S(2)}) copy-start(bf16[4,512,128]{2,1,0:T(8,128)(2,1)S(1)} %get-tuple-element.53) | copy-start | bytes 1572868
  243.7 6.1 copy-start.12
  250.7 105.4 %all-gather.12.cloned.1.call-start = ((), (), s32[]{:S(2)}) async-start(), calls=%async_computation.8 | async-start | bytes 2621440 | tf_op jit(solution)/shard_map/all_gather | solution.py:858
  252.7 246.3 %reduce-scatter.6.cloned.1.call-start = ((), (), s32[]{:S(2)}) async-start(), calls=%async_computation.9 | async-start | bytes 2621440 | tf_op jit(solution)/shard_map/reduce_scatter | solution.py:861
  252.7 3.5 copy-start.28
  356.1 10.6 %copy-start.48 = (bf16[512,2176]{1,0:T(8,128)(2,1)S(1)}, bf16[512,2176]{1,0:T(8,128)(2,1)}, u32[]{:S(2)}) copy-start(bf16[512,2176]{1,0:T(8,128)(2,1)} %all-gather.10.cloned.1.call-done.refs_7_) | copy-start | bytes 6684676
  356.2 19.1 %slice-start.2 = ((s8[8388608]{0:T(1024)(128)(4,1)}), s8[4194304]{0:T(1024)(128)(4,1)S(1)}, s32[]{:S(2)}) async-start(s8[8388608]{0:T(1024)(128)(4,1)} %bitcast.155), calls=%async_computation.16 | async-start | bytes 8388608
  366.8 8.5 %slice-start.3 = ((s8[8388608]{0:T(1024)(128)(4,1)}), s8[4194304]{0:T(1024)(128)(4,1)S(1)}, s32[]{:S(2)}) async-start(s8[8388608]{0:T(1024)(128)(4,1)} %bitcast.155), calls=%async_computation.17 | async-start | bytes 8388608
  394.2 106.5 %reduce-scatter.8.cloned.1.call-start = ((), (), s32[]{:S(2)}) async-start(), calls=%async_computation.10 | async-start | bytes 2785280 | tf_op jit(solution)/shard_map/reduce_scatter | solution.py:861
  404.6 215.4 %reduce-scatter.10.cloned.1.call-start = ((), (), s32[]{:S(2)}) async-start(), calls=%async_computation.11 | async-start | bytes 2621440 | tf_op jit(solution)/shard_map/reduce_scatter | solution.py:861
  516.2 9.6 %copy-start.18 = (bf16[4,512,512]{2,1,0:T(8,128)(2,1)S(1)}, bf16[4,512,512]{2,1,0:T(8,128)(2,1)}, u32[]{:S(2)}) copy-start(bf16[4,512,512]{2,1,0:T(8,128)(2,1)} %copy-done.17) | copy-start | bytes 6291460
  525.8 226.9 %reduce-scatter.14.cloned.1.call-start = ((), (), s32[]{:S(2)}) async-start(), calls=%async_computation.13 | async-start | bytes 2621440 | tf_op jit(solution)/shard_map/reduce_scatter | solution.py:861
  535.0 217.7 %reduce-scatter.12.cloned.1.call-start = ((), (), s32[]{:S(2)}) async-start(), calls=%async_computation.12 | async-start | bytes 5242880 | tf_op jit(solution)/shard_map/reduce_scatter | solution.py:861
  539.7 4.0 copy-start.30
  546.6 69.7 %slice-start = ((s8[8388608]{0:T(1024)(128)(4,1)}), s8[4194304]{0:T(1024)(128)(4,1)S(1)}, s32[]{:S(2)}) async-start(s8[8388608]{0:T(1024)(128)(4,1)} %bitcast.128), calls=%async_computation.14 | async-start | bytes 8388608
  547.9 68.4 %slice-start.1 = ((s8[8388608]{0:T(1024)(128)(4,1)}), s8[4194304]{0:T(1024)(128)(4,1)S(1)}, s32[]{:S(2)}) async-start(s8[8388608]{0:T(1024)(128)(4,1)} %bitcast.128), calls=%async_computation.15 | async-start | bytes 8388608
  745.8 3.6 copy-start.55
  785.9 5.1 copy-start.43
  787.6 3.5 copy-start.45
  787.6 3.5 copy-start.46
  787.6 3.5 copy-start.47
  787.8 5.1 copy-start.57
  787.8 5.6 copy-start.53
  (30 other events, 54.9 us)
Sparse Core Ops, SparseCore 0:
  36.5 88.4 all-gather.5
  131.0 108.6 all-gather.7
  250.8 58.4 all-gather.9
  311.4 44.7 all-gather.11
  394.3 53.0 reduce-scatter.5
  449.7 45.2 reduce-scatter.7
  525.9 66.7 reduce-scatter.9
  595.0 46.4 reduce-scatter.13
  643.8 75.0 reduce-scatter.11

commit v3 on v2

--- a/solution.py
+++ b/solution.py
@@ -37,28 +37,32 @@
     pl.semaphore_wait(barrier, len(targets))
 
 
-def gather_stages(shard, full, local_sem, send_sem, recv_sem):
+def gather_stages(shard, full, local_sem, send_sem, recv_sem, part=0, parts=1):
     batch, length, _ = shard.shape
-    half = length // 2
+    whole = length // parts
+    first = part * whole
+    half = whole // 2
     row, col, other_row, across, sibling = plane_ids()
     to_x = {"ka": across}
     to_y = {"dpl": other_row}
     to_s = {"ka": sibling}
 
-    def slot(r, c, start=0, size=length):
-        return full.at[pl.ds(r * batch, batch), pl.ds(c * length + start, size), :]
+    shard = shard.at[:, pl.ds(first, whole), :]
+
+    def slot(r, c, start=0, size=whole):
+        return full.at[pl.ds(r * batch, batch), pl.ds(c * length + first + start, size), :]
 
     def hop(index, target, dst, src=None):
         return pltpu.make_async_remote_copy(
             src_ref=dst if src is None else src,
             dst_ref=dst,
-            send_sem=send_sem.at[index],
-            recv_sem=recv_sem.at[index],
+            send_sem=send_sem.at[part * 9 + index],
+            recv_sem=recv_sem.at[part * 9 + index],
             device_id=target,
             device_id_type=MESH,
         )
 
-    mine = pltpu.make_async_copy(shard, slot(row, col), local_sem)
+    mine = pltpu.make_async_copy(shard, slot(row, col), local_sem.at[part])
     from_x = hop(0, to_x, slot(row, col), shard)
     from_y = hop(1, to_y, slot(row, col), shard)
     own_s = hop(2, to_s, slot(row, col), shard)
@@ -100,9 +104,9 @@
 
 
 GATHER_SCRATCH = (
-    pltpu.SemaphoreType.DMA,
-    pltpu.SemaphoreType.DMA((9,)),
-    pltpu.SemaphoreType.DMA((9,)),
+    pltpu.SemaphoreType.DMA((2,)),
+    pltpu.SemaphoreType.DMA((18,)),
+    pltpu.SemaphoreType.DMA((18,)),
 )
 
 
@@ -239,55 +243,161 @@
 TRADE_SCRATCH = (pltpu.SemaphoreType.DMA((3,)),)
 
 
-def open_kernel(line, order, x, up, out, *refs):
-    normed_all, up_mine, out_mine, normed = refs[:4]
-    sems = refs[4:]
-    targets, owners = owners_stages((up,), (up_mine,), *sems[3:6])
+def line_gather_stages(count, chunks, block, full, send_sem, recv_sem):
+    here = lax.axis_index("pb")
+    rows = block.shape[0]
+    size = rows // chunks
+
+    def hop(up, distance, c):
+        owner = here - distance if up else here + distance
+        place = full.at[pl.ds(owner * rows + c * size, size)]
+        source = block.at[pl.ds(c * size, size)] if distance == 0 else place
+        return pltpu.make_async_remote_copy(
+            src_ref=source,
+            dst_ref=place,
+            send_sem=send_sem.at[int(up), distance, c],
+            recv_sem=recv_sem.at[int(up), distance, c],
+            device_id={"pb": here + 1 if up else here - 1},
+            device_id_type=MESH,
+        )
+
+    def sends(up, distance):
+        if up:
+            return jnp.logical_and(here >= distance, here < count - 1)
+        return jnp.logical_and(here + distance <= count - 1, here > 0)
+
+    def arrives(up, distance):
+        return here >= distance if up else here + distance <= count - 1
+
+    def step(distance, c):
+        for up in (True, False):
+            if distance > 0:
+
+                @pl.when(arrives(up, distance))
+                def _():
+                    hop(up, distance - 1, c).wait_recv()
+
+            if distance < count - 1:
+
+                @pl.when(sends(up, distance))
+                def _():
+                    hop(up, distance, c).start()
+
+    def finish():
+        for distance in range(count - 1):
+            for c in range(chunks):
+                for up in (True, False):
+
+                    @pl.when(sends(up, distance))
+                    def _():
+                        hop(up, distance, c).wait_send()
+
+    return step, finish
+
+
+def open_kernel(
+    count, chunks, order, moves, unit_moves, x, up, first, gate, out, down, bias, gain, *refs
+):
+    normed_all, up_mine, first_all, gate_out, down_pack, normed, up_low, down_low = refs[:8]
+    sems = refs[8:]
+    targets, owners = owners_stages((up_low if unit_moves else up,), (up_mine,), *sems[3:6])
     _, gather = gather_stages(normed, normed_all, *sems[:3])
-    greet_partner, trade = trade_stages(line, out, out_mine, sems[6])
+    step, finish = line_gather_stages(count, chunks, first, first_all, *sems[6:8])
+    here = lax.axis_index("pb")
     barrier = pltpu.get_barrier_semaphore()
     for target in targets:
         pl.semaphore_signal(barrier, inc=1, device_id=target, device_id_type=MESH)
-    extra = greet_partner(barrier)
+
+    @pl.when(here > 0)
+    def _():
+        pl.semaphore_signal(barrier, inc=1, device_id={"pb": here - 1}, device_id_type=MESH)
+
+    @pl.when(here < count - 1)
+    def _():
+        pl.semaphore_signal(barrier, inc=1, device_id={"pb": here + 1}, device_id_type=MESH)
+
+    ends = (here > 0).astype(jnp.int32) + (here < count - 1).astype(jnp.int32)
+    pl.semaphore_wait(barrier, len(targets) + ends)
+    for c in range(chunks):
+        step(0, c)
     normalize_rows(x, normed, order)
-    pl.semaphore_wait(barrier, len(targets) + extra)
     gather[0]()
-    trade[0]()
+    for j, source, target, size in unit_moves:
+        block = up[:, source : source + size].astype(BF16).astype(F32) * gain[...]
+        up_low[j, :, target : target + size] = block.astype(BF16)
     owners[0]()
-    for stage in gather[1:]:
-        stage()
+    height, lanes, wide = gate.shape[0], gate.shape[1], out.shape[0]
+    for source, target, size in moves:
+        down_low[:, target : target + size] = down[:, source : source + size].astype(BF16)
+    down_low[:, down.shape[1] :] = jnp.broadcast_to(bias[...], (wide, 128)).astype(BF16)
+    pairs = [
+        (first, first_all.at[pl.ds(here * first.shape[0], first.shape[0])]),
+        (gate, gate_out.at[pl.ds(0, height)]),
+        (down_low, down_pack),
+    ]
+    for source, target, size in moves:
+        pairs.append(
+            (
+                out.at[:, pl.ds(source, size)],
+                gate_out.at[
+                    pl.ds(height + target // lanes * wide, wide), pl.ds(target % lanes, size)
+                ],
+            )
+        )
+    copies = [pltpu.make_async_copy(a, b, sems[8].at[i]) for i, (a, b) in enumerate(pairs)]
+    for copy in copies:
+        copy.start()
+    for c in range(chunks):
+        step(1, c)
+    gather[1]()
+    for distance in range(2, count):
+        for c in range(chunks):
+            step(distance, c)
+            if distance == 2 and c == chunks // 2:
+                gather[2]()
+    for copy in copies:
+        copy.wait()
+    gather[3]()
     owners[1]()
-    trade[1]()
-
-
-def open_plane(x, up, out, line, order, collective_id, *before):
-    anywhere = pl.BlockSpec(memory_space=pl.ANY)
+    finish()
+
+
+def open_plane(x, up, first, gate, out, down, bias, gain, up_shape, order, moves, unit_moves, count, collective_id, *before):
+    chunks = 4
     return pl.pallas_call(
-        lambda a, b, c, *refs: open_kernel(line, order, a, b, c, *refs[len(before) :]),
+        lambda *refs: open_kernel(
+            count, chunks, order, moves, unit_moves, *refs[:8], *refs[8 + len(before) :]
+        ),
         out_shape=[
             gathered_shape(x),
-            jax.ShapeDtypeStruct(up.shape, up.dtype),
-            jax.ShapeDtypeStruct(out.shape, out.dtype),
+            jax.ShapeDtypeStruct(up_shape, BF16),
+            jax.ShapeDtypeStruct((count * first.shape[0], first.shape[1]), BF16),
+            jax.ShapeDtypeStruct((gate.shape[0] + out.size // gate.shape[1], gate.shape[1]), BF16),
+            jax.ShapeDtypeStruct((down.shape[0], down.shape[1] + 128), BF16),
         ],
-        in_specs=[pl.BlockSpec(memory_space=pltpu.VMEM)] + [anywhere] * (2 + len(before)),
-        out_specs=[anywhere] * 3,
+        in_specs=[VMEM, VMEM, ANY, ANY, ANY, VMEM, VMEM, VMEM] + [ANY] * len(before),
+        out_specs=[ANY] * 5,
         scratch_shapes=[
             pltpu.VMEM(x.shape, BF16),
+            pltpu.VMEM(up_shape, BF16),
+            pltpu.VMEM((down.shape[0], down.shape[1] + 128), BF16),
             *GATHER_SCRATCH,
             *owners_scratch(1),
-            *TRADE_SCRATCH,
+            pltpu.SemaphoreType.DMA((2, count, chunks)),
+            pltpu.SemaphoreType.DMA((2, count, chunks)),
+            pltpu.SemaphoreType.DMA((3 + len(moves),)),
         ],
         compiler_params=pltpu.CompilerParams(
             collective_id=collective_id,
             has_side_effects=True,
-            vmem_limit_bytes=16 * 1024 * 1024,
+            vmem_limit_bytes=20 * 1024 * 1024,
         ),
         name="open_plane",
-    )(x, up, out, *before)
+    )(x, up, first, gate, out, down, bias, gain, *before)
 
 
 def scatter_stages(
-    terms, finish, sent, own, sib, from_x, from_y, diag_a, diag_b, sems, recvs, earlier=()
+    terms, finish, sent, own, sib, from_x, from_y, diag_a, diag_b, sems, recvs, even=False
 ):
     _, batch, length, width = own.shape
     half = length // 2
@@ -344,8 +454,6 @@
         lax.fori_loop(0, width // tile, body, 0)
 
     def give(j):
-        if earlier:
-            earlier[j].wait_send()
         make(*theirs[j], sent.at[j])
         swaps[j].start()
 
@@ -363,36 +471,36 @@
         swaps[j].wait_recv()
         add(own.at[j], 0, ((own.at[j], 0), (sib.at[j], 0)), length)
 
-    def stage_begin():
-        give(0)
-        make(*mine[0], own.at[0])
-
-    def stage_diag():
+    def send_diag():
         merge(0)
         first_a.start()
         first_b.start()
-        give(1)
         make(*mine[1], own.at[1])
 
-    def stage_x():
+    def send_x():
         merge(1)
         x_lower.start()
-        give(2)
         make(*mine[2], own.at[2])
 
-    def stage_y():
+    def send_y():
         merge(2)
-        y_upper.start()
-        give(3)
+        if not even:
+            y_upper.start()
         make(*mine[3], own.at[3])
 
     def stage_rest():
+        if even:
+            first_a.wait_recv()
+            add(own.at[2], 0, ((own.at[2], 0), (diag_a, 0)), half)
+            y_lower.start()
+            y_upper.start()
         first_b.wait_recv()
         add(own.at[1], half, ((own.at[1], half), (diag_b, 0)), half)
         x_upper.start()
-        first_a.wait_recv()
-        add(own.at[2], 0, ((own.at[2], 0), (diag_a, 0)), half)
-        y_lower.start()
+        if not even:
+            first_a.wait_recv()
+            add(own.at[2], 0, ((own.at[2], 0), (diag_a, 0)), half)
+            y_lower.start()
         merge(3)
 
     def close(start):
@@ -406,10 +514,12 @@
 
         lax.fori_loop(0, half // step, body, 0)
 
-    def stage_end():
+    def close_lower():
         x_lower.wait_recv()
         y_lower.wait_recv()
         close(0)
+
+    def close_upper():
         y_upper.wait_recv()
         x_upper.wait_recv()
         close(half)
@@ -420,8 +530,21 @@
         for copy in swaps:
             copy.wait_send()
 
-    stages = (stage_begin, stage_diag, stage_x, stage_y, stage_rest, stage_end, stage_free)
-    return (to_x, to_y, to_s), stages, swaps
+    stages = (
+        lambda: give(0),
+        lambda: make(*mine[0], own.at[0]),
+        lambda: give(1),
+        send_diag,
+        lambda: give(2),
+        send_x,
+        lambda: give(3),
+        send_y,
+        stage_rest,
+        close_lower,
+        close_upper,
+        stage_free,
+    )
+    return (to_x, to_y, to_s), stages
 
 
 def scatter_scratch(shape):
@@ -451,11 +574,15 @@
         middle[b, at, :] = value
         normed[b, at, :] = normalize(value)[0].astype(BF16)
 
-    targets, stages, _ = scatter_stages(((gated, weight, False),), finish, *refs[-12:-3])
-    _, gather = gather_stages(normed, normed_all, *refs[-3:])
+    targets, stages = scatter_stages(((gated, weight, False),), finish, *refs[-12:-3], True)
+    lower, upper = (gather_stages(normed, normed_all, *refs[-3:], i, 2)[1] for i in (0, 1))
     greet(targets)
-    for stage in stages + gather:
+    for stage in stages[:10] + lower[:1] + stages[10:11] + upper[:1]:
         stage()
+    for pair in zip(lower[1:], upper[1:]):
+        for stage in pair:
+            stage()
+    stages[11]()
 
 
 def plane_mix(gated, weight, x, order, collective_id, *before):
@@ -489,11 +616,15 @@
         grad_middle[b, at, :] = value
         low[b, at, :] = value.astype(BF16)
 
-    targets, stages, _ = scatter_stages(((grad, weight, True),), finish, *refs[-12:-3])
-    _, gather = gather_stages(low, grad_all, *refs[-3:])
+    targets, stages = scatter_stages(((grad, weight, True),), finish, *refs[-12:-3], True)
+    lower, upper = (gather_stages(low, grad_all, *refs[-3:], i, 2)[1] for i in (0, 1))
     greet(targets)
-    for stage in stages + gather:
+    for stage in stages[:10] + lower[:1] + stages[10:11] + upper[:1]:
         stage()
+    for pair in zip(lower[1:], upper[1:]):
+        for stage in pair:
+            stage()
+    stages[11]()
 
 
 def plane_turn(grad, weight, middle, cot, order, collective_id, *before):
@@ -517,66 +648,90 @@
     )(grad, weight, middle, cot, *before)
 
 
-def last_kernel(order, owned, *refs):
-    grad_a, weight_a, grad_b, weight_b, x, grad_middle, active, weight_down, middle = refs[:9]
-    outs, scratch = refs[-22 - owned : -20], refs[-20:]
-
-    def finish_grad(b, at, value):
+def put_back(landed, weight, gain, target, moves):
+    total = 0.0
+    for j, column, place, size in moves:
+        value = landed[j, :, place : place + size].astype(F32)
+        low = weight[:, column : column + size].astype(BF16).astype(F32)
+        total = total + jnp.sum(low * value, axis=-1, keepdims=True)
+        target[:, column : column + size] = gain[...] * value
+    return total
+
+
+def last_kernel(order, moves, *refs):
+    grad_a, weight_a, grad_b, weight_b, x, grad_middle = refs[:6]
+    owned, weights, gains = refs[6:8], refs[8:10], refs[10:12]
+    grad_down = refs[12]
+    scratch = refs[-14:]
+    outs = refs[-20:-14]
+
+    def finish(b, at, value):
         normed, inv = normalize(read_rows(x, b, at, order).astype(F32))
         value = grad_middle[b, at, :] + normalize_back(normed, inv, value)
         write_rows(outs[0], b, at, order, value)
 
-    def finish_out(b, at, value):
-        write_rows(outs[1], b, at, order, (middle[b, at, :] + value).astype(BF16))
-
     terms = ((grad_a, weight_a, True), (grad_b, weight_b, True))
-    _, grads, swaps = scatter_stages(terms, finish_grad, *scratch[:9])
-    _, out, _ = scatter_stages(
-        ((active, weight_down, False),), finish_out, scratch[0], *scratch[9:17], earlier=swaps
-    )
-    targets, owners = owners_stages(refs[9 : 9 + owned], outs[2:], *scratch[17:])
+    _, stages = scatter_stages(terms, finish, *scratch[:9])
+    targets, owners = owners_stages(owned, scratch[9:11], *scratch[11:14])
     greet(targets)
-    for stage in grads[:4] + out[:2]:
+    for stage in stages[:8] + owners[:1] + stages[8:9]:
         stage()
-    grads[4]()
-    out[2]()
-    out[3]()
-    owners[0]()
-    grads[5]()
-    for stage in out[4:]:
+    size = outs[5].shape[1] // max(len(order), 1)
+    for j, i in enumerate(order or (0,)):
+        block = grad_down[:, j * size : (j + 1) * size]
+        outs[5][:, i * size : (i + 1) * size] = block.astype(F32)
+    for stage in stages[9:] + owners[1:]:
         stage()
-    owners[1]()
-
-
-def plane_last(terms, x, grad_middle, summed, owned, order, collective_id, *before):
+    for i in (0, 1):
+        if moves[i]:
+            outs[3 + i][...] = put_back(scratch[9 + i], weights[i], gains[i], outs[1 + i], moves[i])
+        else:
+            outs[1 + i][...] = scratch[9 + i][...]
+            outs[3 + i][...] = jnp.zeros(outs[3 + i].shape, F32)
+
+
+def plane_last(
+    terms, x, grad_middle, owned, weights, gains, grad_down, moves, order, collective_id, *before
+):
     shape = x.shape
+    column = jax.ShapeDtypeStruct(gains[0].shape, F32)
+    plain = jax.ShapeDtypeStruct((grad_down.shape[0], shape[-1]), F32)
     return pl.pallas_call(
-        functools.partial(last_kernel, order, len(owned)),
-        out_shape=[jax.ShapeDtypeStruct(shape, F32), jax.ShapeDtypeStruct(shape, BF16)]
-        + [jax.ShapeDtypeStruct(a.shape, a.dtype) for a in owned],
-        in_specs=[VMEM] * 9 + [ANY] * (len(owned) + len(before)),
-        out_specs=[VMEM] * 2 + [ANY] * len(owned),
+        functools.partial(last_kernel, order, moves),
+        out_shape=[jax.ShapeDtypeStruct(shape, F32)]
+        + [
+            jax.ShapeDtypeStruct(w.shape, F32) if m else jax.ShapeDtypeStruct(o.shape, BF16)
+            for o, w, m in zip(owned, weights, moves)
+        ]
+        + [column, column, plain],
+        in_specs=[VMEM] * 6 + [ANY] * 2 + [VMEM] * 5 + [ANY] * len(before),
+        out_specs=[VMEM] * 6,
         scratch_shapes=scatter_scratch(shape)
-        + scatter_scratch(shape)[1:]
-        + owners_scratch(len(owned)),
+        + [pltpu.VMEM(o.shape, BF16) for o in owned]
+        + owners_scratch(2),
         compiler_params=pltpu.CompilerParams(
             collective_id=collective_id,
             has_side_effects=True,
-            vmem_limit_bytes=60 * 1024 * 1024,
+            vmem_limit_bytes=58 * 1024 * 1024,
         ),
         name="plane_last",
-    )(*terms, x, grad_middle, *summed, *owned, *before)
+    )(*terms, x, grad_middle, *owned, *weights, *gains, grad_down, *before)
 
 
 def scan_kernel(count, forward, cuts, gathers, order, state, coef, *refs):
-    targets, stages = (), ()
     if gathers:
         moved = refs[0]
         total, result, message, landed, send_sem, recv_sem = refs[-11:-5]
         shard, shard_sem = refs[-5:-3]
         targets, stages = gather_stages(shard, result, *refs[-3:])
     else:
-        total, message, landed, send_sem, recv_sem = refs[-5:]
+        left, right, middle = refs[:3]
+        total, result, message, landed, send_sem, recv_sem = refs[-15:-9]
+
+        def finish(b, at, value):
+            write_rows(result, b, at, order, (middle[b, at, :] + value).astype(BF16))
+
+        targets, stages = scatter_stages(((left, right, False),), finish, *refs[-9:])
     here = lax.axis_index("pb")
     place = here if forward else count - 1 - here
     step = 1 if forward else -1
@@ -649,14 +804,16 @@
                 else:
                     copy.start()
         stages[0]()
-    for i in range(1, len(pieces)):
+    count = len(pieces)
+    places = {count // 2: 1, 3 * count // 4: 2} if gathers else {i + 1: i for i in range(8)}
+    if not gathers:
+        places[3 * count // 4] = 8
+    for i in range(1, count):
         emit(i)
-        if gathers and i == len(pieces) // 2:
-            stages[1]()
-        if gathers and i == 3 * len(pieces) // 4:
-            stages[2]()
-    if gathers:
-        stages[3]()
+        if i in places:
+            stages[places[i]]()
+    for stage in stages[max(places.values()) + 1 :]:
+        stage()
 
     @pl.when(has_next)
     def _():
@@ -664,77 +821,150 @@
             hop(i).wait_send()
 
 
-def line_scan(state, coef, count, forward, order, collective_id, *before, gathered=None):
+def line_scan(state, coef, count, forward, order, collective_id, *before, gathered=None, summed=()):
     cuts = 4
     pieces = state.shape[0] * cuts
-    shapes, specs, operands = [jax.ShapeDtypeStruct(state.shape, BF16)], [VMEM], [state, coef]
     scratch = [
         pltpu.VMEM(state.shape, BF16),
         pltpu.VMEM(state.shape, BF16),
         pltpu.SemaphoreType.DMA((pieces,)),
         pltpu.SemaphoreType.DMA((pieces,)),
     ]
-    if gathered is not None:
-        operands.append(gathered)
-        shapes.append(gathered_shape(gathered))
-        specs.append(ANY)
+    gathers = gathered is not None
+    if gathers:
+        operands, specs = (gathered,), [ANY]
+        result, spec = gathered_shape(gathered), ANY
         scratch += [
             pltpu.VMEM(gathered.shape, gathered.dtype),
             pltpu.SemaphoreType.DMA((max(len(order), 1),)),
             *GATHER_SCRATCH,
         ]
-    results = pl.pallas_call(
-        functools.partial(scan_kernel, count, forward, cuts, gathered is not None, order),
-        out_shape=shapes,
-        in_specs=[VMEM, pl.BlockSpec(memory_space=pltpu.SMEM)]
-        + [ANY] * (len(operands) - 2 + len(before)),
-        out_specs=specs,
+    else:
+        operands, specs = summed, [VMEM] * 3
+        result, spec = jax.ShapeDtypeStruct(summed[2].shape, BF16), VMEM
+        scratch += scatter_scratch(summed[2].shape)
+    return pl.pallas_call(
+        functools.partial(scan_kernel, count, forward, cuts, gathers, order),
+        out_shape=[jax.ShapeDtypeStruct(state.shape, BF16), result],
+        in_specs=[VMEM, pl.BlockSpec(memory_space=pltpu.SMEM)] + specs + [ANY] * len(before),
+        out_specs=[VMEM, spec],
         scratch_shapes=scratch,
         compiler_params=pltpu.CompilerParams(
             collective_id=collective_id,
             has_side_effects=True,
-            vmem_limit_bytes=16 * 1024 * 1024,
+            vmem_limit_bytes=48 * 1024 * 1024,
         ),
         name="line_scan",
-    )(*operands, *before)
-    return results if gathered is not None else results[0]
-
-
-def owners_kernel(arrays, line, *refs):
-    trades = 1 if line else 0
-    scratch = refs[-3 - trades :]
-    outs = refs[-3 - trades - arrays - trades : -3 - trades]
-    targets, stages = owners_stages(refs[:arrays], outs[:arrays], *scratch[:3])
+    )(state, coef, *operands, *before)
+
+
+def spread_kernel(line, moves, *refs):
+    weights, gain, out, docs = refs[:4], refs[4], refs[5], refs[6]
+    qkv_mine, gate_mine, out_mine, docs_all, qkv_pack, gate_pack, out_low = refs[-13:-6]
+    scratch = refs[-6:]
+    row, _, other_row, _, _ = plane_ids()
+    targets, stages = owners_stages((qkv_pack, gate_pack), (qkv_mine, gate_mine), *scratch[:3])
+    greet_partner, trade = trade_stages(line, out_low, out_mine, scratch[3])
     barrier = pltpu.get_barrier_semaphore()
     for target in targets:
         pl.semaphore_signal(barrier, inc=1, device_id=target, device_id_type=MESH)
-    greeted = len(targets)
-    if line:
-        greet_partner, trade = trade_stages(line, refs[arrays], outs[arrays], scratch[3])
-        greeted = greeted + greet_partner(barrier)
+    greeted = greet_partner(barrier) + len(targets)
+    for i, blocks in enumerate(moves):
+        for j, column, place, size in blocks:
+            block = weights[i][:, column : column + size].astype(BF16).astype(F32) * gain[...]
+            pack = qkv_pack if i < 3 else gate_pack
+            pack[j, :, place : place + size] = block.astype(BF16)
     pl.semaphore_wait(barrier, greeted)
     stages[0]()
-    if line:
-        trade[0]()
-        trade[1]()
+    give = pltpu.make_async_remote_copy(
+        src_ref=docs,
+        dst_ref=docs_all.at[row],
+        send_sem=scratch[4].at[0],
+        recv_sem=scratch[4].at[1],
+        device_id={"dpl": other_row},
+        device_id_type=MESH,
+    )
+    keep = pltpu.make_async_copy(docs, docs_all.at[row], scratch[4].at[2])
+    give.start()
+    keep.start()
+    out_low[...] = out[...].astype(BF16)
+    trade[0]()
+    trade[1]()
+    give.wait()
+    keep.wait()
     stages[1]()
 
 
-def to_owners(arrays, collective_id, *before, line="", traded=()):
-    count = len(arrays)
-    operands = [*arrays, *traded]
-    anywhere = pl.BlockSpec(memory_space=pl.ANY)
+def plane_spread(weights, gain, out, docs, line, moves, group, collective_id):
+    rows = gain.shape[0]
+    first = sum(w.shape[1] for w in weights[:3]) // group
+    gate = weights[3].shape[1] // group
+    shapes = [
+        jax.ShapeDtypeStruct((group, rows, first), BF16),
+        jax.ShapeDtypeStruct((group, rows, gate), BF16),
+        jax.ShapeDtypeStruct(out.shape, BF16),
+    ]
     return pl.pallas_call(
-        functools.partial(owners_kernel, count, line),
-        out_shape=[jax.ShapeDtypeStruct(a.shape, a.dtype) for a in operands],
-        in_specs=[anywhere] * (len(operands) + len(before)),
-        out_specs=[anywhere] * len(operands),
-        scratch_shapes=owners_scratch(count) + (list(TRADE_SCRATCH) if line else []),
+        functools.partial(spread_kernel, line, moves),
+        out_shape=shapes + [jax.ShapeDtypeStruct((2,) + docs.shape, docs.dtype)],
+        in_specs=[VMEM] * 7,
+        out_specs=[ANY] * 4,
+        scratch_shapes=[pltpu.VMEM(shape.shape, BF16) for shape in shapes]
+        + owners_scratch(2)
+        + list(TRADE_SCRATCH)
+        + [pltpu.SemaphoreType.DMA((3,)), pltpu.SemaphoreType.DMA((1,))],
         compiler_params=pltpu.CompilerParams(
-            collective_id=collective_id, has_side_effects=True
+            collective_id=collective_id,
+            has_side_effects=True,
+            vmem_limit_bytes=20 * 1024 * 1024,
         ),
-        name="to_owners",
-    )(*operands, *before)
+        name="plane_spread",
+    )(*weights, gain, out, docs)
+
+
+def final_kernel(line, order, moves, grad, grad_out, *refs):
+    weights, gain = refs[:3], refs[3]
+    outs, out_out, sums, landed, out_landed = refs[-11:-8], refs[-8], refs[-7], refs[-6], refs[-5]
+    targets, stages = owners_stages((grad,), (landed,), *refs[-4:-1])
+    greet_partner, trade = trade_stages(line, grad_out, out_landed, refs[-1])
+    barrier = pltpu.get_barrier_semaphore()
+    for target in targets:
+        pl.semaphore_signal(barrier, inc=1, device_id=target, device_id_type=MESH)
+    pl.semaphore_wait(barrier, greet_partner(barrier) + len(targets))
+    stages[0]()
+    for stage in trade:
+        stage()
+    size = out_out.shape[1] // max(len(order), 1)
+    for j, i in enumerate(order or (0,)):
+        block = out_landed[:, j * size : (j + 1) * size]
+        out_out[:, i * size : (i + 1) * size] = block.astype(F32)
+    stages[1]()
+    total = 0.0
+    for weight, target, blocks in zip(weights, outs, moves):
+        total = total + put_back(landed, weight, gain, target, blocks)
+    sums[...] = total
+
+
+def plane_final(grad, grad_out, weights, gain, line, order, moves, collective_id, *before):
+    return pl.pallas_call(
+        functools.partial(final_kernel, line, order, moves),
+        out_shape=[jax.ShapeDtypeStruct(w.shape, F32) for w in weights]
+        + [
+            jax.ShapeDtypeStruct(grad_out.shape, F32),
+            jax.ShapeDtypeStruct(gain.shape, F32),
+        ],
+        in_specs=[ANY] * 2 + [VMEM] * 4 + [ANY] * len(before),
+        out_specs=[VMEM] * 5,
+        scratch_shapes=[pltpu.VMEM(grad.shape, BF16), pltpu.VMEM(grad_out.shape, BF16)]
+        + owners_scratch(1)
+        + list(TRADE_SCRATCH),
+        compiler_params=pltpu.CompilerParams(
+            collective_id=collective_id,
+            has_side_effects=True,
+            vmem_limit_bytes=20 * 1024 * 1024,
+        ),
+        name="plane_final",
+    )(grad, grad_out, *weights, gain, *before)
 
 
 def normalize(values):
@@ -838,14 +1068,6 @@
     def to_outer(values):
         return pick(values, [inner.index(i) for i in range(len(inner))])
 
-    def by_head(weight):
-        cut = weight.reshape(rows, H // (n_dpl * heads_pb), n_dpl, heads_pb, -1)
-        return jnp.transpose(cut, (2, 1, 3, 0, 4)).reshape(group, rows, -1)
-
-    def from_head(values):
-        cut = values.reshape(n_dpl, H // (n_dpl * heads_pb), heads_pb, rows, -1)
-        return jnp.transpose(cut, (3, 1, 0, 2, 4)).reshape(rows, -1)
-
     def by_unit(weight):
         cut = weight.reshape(rows, n_dph, n_dpl, n_pb, n_ka, wide_rows)
         return jnp.transpose(cut, (2, 4, 0, 1, 3, 5)).reshape(group, rows, units)
@@ -864,15 +1086,24 @@
 
     gain_one = ln1_gain.astype(BF16).astype(F32)[:, None]
     gain_two = ln2_gain.astype(BF16).astype(F32)[:, None]
-    firsts = [w.astype(BF16) for w in (w_query, w_key, w_value, w_gate)]
-    up_low = w_up.astype(BF16)
-
-    def scaled(weight, gain):
-        return (weight.astype(F32) * gain).astype(BF16)
-
-    query_pack, key_pack, value_pack, gate_pack = (by_head(scaled(w, gain_one)) for w in firsts)
-    qkv_swapped, gate_swapped = to_owners(
-        [jnp.concatenate([query_pack, key_pack, value_pack], axis=-1), gate_pack], 0
+    firsts = (w_query, w_key, w_value, w_gate)
+
+    def head_of(j):
+        r, c = j // n_ka, j % n_ka
+        return (c // heads_pb) * (n_dpl * heads_pb) + r * heads_pb + c % heads_pb
+
+    head_moves = [
+        [(j, head_of(j) * size, place, size) for j in range(group)]
+        for size, place in (
+            (key_width, 0),
+            (key_width, key_width),
+            (value_width, 2 * key_width),
+            (value_width, 0),
+        )
+    ]
+    docs = jnp.pad(doc_lengths, ((0, 8 - batch), (0, 128 - doc_lengths.shape[1])))
+    qkv_swapped, gate_swapped, out_moved, docs_all = plane_spread(
+        firsts, gain_one, w_out, docs, line, head_moves, group, 0
     )
     order = tuple(inner) if chunk % 128 == 0 else ()
     rows_in, rows_cot = inputs, out_cotangent
@@ -893,7 +1124,7 @@
     decay_in = jnp.exp(offsets.astype(F32) * log_gamma)[:, None]
     decay_out = jnp.exp((span - offsets).astype(F32) * log_gamma)[:, None]
     decay_span = jnp.exp(span * log_gamma)
-    lengths = lax.all_gather(doc_lengths, "dpl", axis=0, tiled=True)
+    lengths = docs_all[:, :batch, : doc_lengths.shape[1]].reshape(n_dpl * batch, -1)
     ends = jnp.cumsum(lengths, axis=-1)
     edge = at_pb * span
 
@@ -903,35 +1134,37 @@
     coef_forward = jnp.stack([goes_on(edge), jnp.full((n_dpl * batch,), decay_span)])
     coef_backward = jnp.stack([goes_on(edge + span), jnp.full((n_dpl * batch,), decay_span)])
 
-    down_pack = jnp.concatenate(
-        [
-            to_inner(w_down.astype(BF16)),
-            jnp.broadcast_to(up_bias.astype(BF16)[:, None], (wide_rows, 128)),
-        ],
-        axis=-1,
-    )
-    normed_one_all, up_swapped, out_moved = open_plane(
+    down_in, up_in, unit_moves = w_down, w_up, []
+    if order:
+        moves = [(i * chunk, j * chunk, chunk) for j, i in enumerate(order)]
+        for j in range(group):
+            for q in range(n_dph * n_pb):
+                block = (q // n_pb * n_dpl + j // n_ka) * n_pb + q % n_pb
+                column = (block * n_ka + j % n_ka) * wide_rows
+                unit_moves.append((j, column, q * wide_rows, wide_rows))
+    else:
+        moves = [(i * units, i * units, units) for i in range(width // units)]
+        out_moved, down_in = to_inner(out_moved), to_inner(w_down)
+        up_in = by_unit((w_up.astype(BF16).astype(F32) * gain_two).astype(BF16))
+    normed_one_all, up_swapped, weight_qkv, gate_out, down_pack = open_plane(
         rows_in,
-        by_unit(scaled(up_low, gain_two)),
-        to_inner(w_out.astype(BF16)),
-        line,
+        up_in,
+        qkv_swapped.reshape(group * rows, -1),
+        gate_swapped.reshape(group * rows, -1),
+        out_moved,
+        down_in,
+        up_bias[:, None],
+        gain_two,
+        (group, rows, units),
         order,
+        moves,
+        unit_moves,
+        n_pb,
         1,
-        qkv_swapped,
-        down_pack,
-        coef_forward,
-        coef_backward,
-        *tables_q,
-        *tables_k,
-        decay,
-    )
-    weight_qkv = gather_line(qkv_swapped.reshape(group * rows, -1))
+    )
+    if n_dph > 1:
+        weight_qkv = lax.all_gather(weight_qkv, "dph", axis=0, tiled=True)
     blocks = width // units
-    gate_out = jnp.concatenate(
-        [after(gate_swapped.reshape(group * rows, -1), normed_one_all)]
-        + [out_moved[:, i * units : (i + 1) * units] for i in range(blocks)],
-        axis=0,
-    )
     gate_out = gather_line(gate_out)
     first = mm(normed_one_all, weight_qkv)
     query_pre = first[..., :key_width]
@@ -959,8 +1192,8 @@
         .transpose(1, 0, 3, 2, 4)
         .reshape(value_width, width)
     )
-    weight_up = gather_line(after(up_swapped.reshape(group * rows, -1), weight_out))
-    down_pack = gather_line(after(down_pack, weight_out))
+    weight_up = gather_line(after(up_swapped.reshape(group * rows, -1), gate_out))
+    down_pack = gather_line(after(down_pack, gate_out))
     weight_down = down_pack[:, :width]
     bias_up = down_pack[:, width].astype(F32)
     normed_ret, inv_ret = normalize(retained)
@@ -977,13 +1210,9 @@
         jnp.exp(-0.5 * up_pre * up_pre) * np.float32(1.0 / math.sqrt(2.0 * math.pi))
     )
     grad_up_pre = (mm_back(cot_all, weight_down) * slope).astype(BF16)
-    grad_bias = jnp.sum(grad_up_pre.astype(F32), axis=(0, 1)).astype(BF16)
+    ones = jnp.ones((n_dpl * batch, span, 128), BF16)
     grad_down = jnp.concatenate(
-        [
-            mm_grad(active, cot_all).astype(BF16),
-            jnp.broadcast_to(grad_bias[:, None], (units, 128)),
-        ],
-        axis=-1,
+        [mm_grad(active, cot_all).astype(BF16), mm_grad(grad_up_pre, ones).astype(BF16)], axis=-1
     )
     grad_up = mm_grad(normed_two_all, grad_up_pre).astype(BF16)
     grad_middle, grad_mid_all = plane_turn(
@@ -1003,7 +1232,7 @@
         .reshape(value_width, width)
     )
     grad_gate_w = mm_grad(normed_one_all, grad_gate).astype(BF16)
-    grad_carried = line_scan(
+    grad_carried, output = line_scan(
         grad_state,
         coef_backward,
         n_pb,
@@ -1012,6 +1241,7 @@
         7,
         grad_gate_w,
         grad_out,
+        summed=(active, down_pack, middle),
     )
     grad_gate_w = scatter_line(grad_gate_w)
     grad_out = scatter_line(grad_out)
@@ -1041,47 +1271,50 @@
     grad_qkv_w = mm_grad(normed_one_all, after(grad_qkv, grad_gate_w)).astype(BF16)
     grad_qkv_sum = scatter_line(grad_qkv_w)
     cut = (group, rows, -1)
-    grad_inputs, output, back_up, back_gate = plane_last(
+    grad_inputs, shard_gate, shard_up, sums_gate, sums_up, shard_down = plane_last(
         (grad_qkv, weight_qkv, grad_gate, weight_gate),
         rows_in,
         grad_middle,
-        (active, down_pack, middle),
-        (grad_up.reshape(cut), grad_gate_w.reshape(cut)),
+        (grad_gate_w.reshape(cut), grad_up.reshape(cut)),
+        (w_gate, w_up),
+        (gain_one, gain_two),
+        grad_down,
+        (head_moves[3], unit_moves),
         order,
         8,
         grad_qkv_w,
     )
     if not order:
         output, grad_inputs = to_outer(output), to_outer(grad_inputs)
-
-    shard_down = to_outer(grad_down[:, :width].astype(F32))
+        shard_up = from_unit(shard_up).astype(F32)
+        sums_up = jnp.sum(w_up.astype(BF16).astype(F32) * shard_up, axis=-1, keepdims=True)
+        shard_up = gain_two * shard_up
+
+    shard_query, shard_key, shard_value, shard_out, sums_qkv = plane_final(
+        grad_qkv_sum.reshape(cut),
+        grad_out,
+        firsts[:3],
+        gain_one,
+        line,
+        order,
+        head_moves[:3],
+        9,
+        grad_inputs,
+    )
+    if not order:
+        shard_out, shard_down = to_outer(shard_out), to_outer(shard_down)
     shard_bias = grad_down[:, width].astype(F32)
-    back, shard_out = to_owners(
-        [grad_qkv_sum.reshape(cut)], 9, grad_inputs, line=line, traded=(grad_out,)
-    )
-    shard_out = to_outer(shard_out.astype(F32))
-    shard_up = from_unit(back_up).astype(F32)
-    shard_gate = from_head(back_gate).astype(F32)
-    shard_query = from_head(back[..., :key_width]).astype(F32)
-    shard_key = from_head(back[..., key_width : 2 * key_width]).astype(F32)
-    shard_value = from_head(back[..., 2 * key_width :]).astype(F32)
-    shards = (shard_query, shard_key, shard_value, shard_gate)
-    shard_gain_one = sum(
-        jnp.sum(low.astype(F32) * grad, axis=-1) for low, grad in zip(firsts, shards)
-    )
-    shard_gain_two = jnp.sum(up_low.astype(F32) * shard_up, axis=-1)
-    shard_query, shard_key, shard_value, shard_gate = (gain_one * g for g in shards)
     return (
         output,
         grad_inputs,
-        shard_gain_one,
+        (sums_qkv + sums_gate)[:, 0],
         shard_query,
         shard_key,
         shard_value,
         shard_gate,
         shard_out,
-        shard_gain_two,
-        gain_two * shard_up,
+        sums_up[:, 0],
+        shard_up,
         shard_bias,
         shard_down,
     )

time: 807 us -> 761 us (0.943)
  local copies, waits for them, and re-layouts: 75.8 us -> 57.4 us
  other arithmetic: 44.6 us -> 32.8 us
    convert_element_type x14 -> x0, other arithmetic: 10 us -> none  [the longest x3 2.47 us: scaled(): return (weight.astype(F32) * gain).astype(BF16)]
    convert_element_type x11 -> x0, local copies, waits for them, and re-layouts: 8.97 us -> none  [the longest x2 2.37 us: on_device(): shard_value = from_head(back[..., 2 * key_width:]).astype(F32)]
    pallas_call x2, Pallas kernels: 122 us -> 131 us  [line_scan(): pl.pallas_call(functools.partial(scan_kernel, count, forward, cuts, gathe...]
    dot_general x5 -> x6, matrix products: 58.1 us -> 49.9 us  [mm_grad(): return jnp.einsum('sti,sto->io', left, right, preferred_element_type=F32)]
    all_gather x4 -> x3, waiting for transfers between devices: 28.8 us -> 25.9 us  [gather_line(): return lax.all_gather(values, LINE, axis=0, tiled=True)]
    unnamed x174 -> x138, local copies, waits for them, and re-layouts: 44.2 us -> 44.4 us
  transfers between devices with their start and end apart: 9 -> 8, of which waited for: 2 -> 3; matrix products, arithmetic and copies ran while one was open for 16% -> 15% of each run, Pallas kernels for 57% -> 48%
where the time goes in v3:
time: 761 us; the launch traced here: 753 us
  Pallas kernels  495 us (65%)
  matrix products  122 us (16%)
  local copies, waits for them, and re-layouts  57.4 us (8%)
  other arithmetic  32.8 us (4%)
  waiting for transfers between devices  27.1 us (4%)
  between operations  18.7 us (2%)
    pallas_call x2, Pallas kernels, line_scan(): pl.pallas_call(functools.partial(scan_kernel, count, forward, cuts, gathe...  131 us
    pallas_call x1, Pallas kernels, plane_turn(): pl.pallas_call(functools.partial(turn_kernel, order), out_shape=[jax.Shap...  81.3 us
    pallas_call x1, Pallas kernels, plane_mix(): pl.pallas_call(functools.partial(mix_kernel, order), out_shape=[jax.Shape...  80.9 us
    pallas_call x1, Pallas kernels, open_plane(): pl.pallas_call(lambda *refs: open_kernel(count, chunks, order, moves, uni...  71.8 us
    pallas_call x1, Pallas kernels, plane_last(): pl.pallas_call(functools.partial(last_kernel, order, moves), out_shape=[j...  67.7 us
    dot_general x6, matrix products, mm_grad(): return jnp.einsum('sti,sto->io', left, right, preferred_element_type=F32)  49.9 us
    unnamed x138, local copies, waits for them, and re-layouts  44.4 us
    pallas_call x1, Pallas kernels, plane_spread(): pl.pallas_call(functools.partial(spread_kernel, line, moves), out_shape=s...  32.6 us
  transfers between devices with their start and end apart: 8, of which 3 were waited for; matrix products, arithmetic and copies ran while one was open for 15% of the time, Pallas kernels for 48%

profile of v3, /device:TPU:2, one launch (start us, length us, event | category | flops | bytes accessed | tf_op | source)
XLA Modules:
  0.0 753.2 jit_solution(14710524317559977761)
XLA Ops:
  16.0 32.6 %plane_spread.1 = (bf16[8,64,1024]{2,1,0:T(8,128)(2,1)S(1)}, bf16[8,64,512]{2,1,0:T(8,128)(2,1)S(1)}, bf16[128,2048]{1,0:T(8,128)(2,1)S(1)}, s32[2,8,128]{2,1,0:T(8,128)S(1)}) custom-call(f32[64,2048]{1,0:T(8,128)S(1)} %copy-done.13, f32[64,2048]{1,0:T(8,128)S(1)} %copy-done.15, f32[64,4096]{1,0:T(8,128)S(1)} %copy-done.6, f32[64,4096]{1,0:T(8,128)S(1)} %copy-done.3, ...), custom_call_target="tpu_custom_call" | custom-call | tf_op jit(solution)/shard_map/plane_spread/pallas_call | solution.py:907
  48.7 71.8 %open_plane.1 = (bf16[4,512,2048]{2,1,0:T(8,128)(2,1)S(1)}, bf16[8,64,512]{2,1,0:T(8,128)(2,1)S(1)}, bf16[2048,1024]{1,0:T(8,128)(2,1)S(1)}, bf16[1024,512]{1,0:T(8,128)(2,1)}, bf16[128,2176]{1,0:T(8,128)(2,1)S(1)}) custom-call(bf16[2,128,2048]{2,1,0:T(8,128)(2,1)S(1)} %copy-done, f32[64,4096]{1,0:T(8,128)S(1)} %copy-done.5, bf16[512,1024]{1,0:T(8,128)(2,1)S(1)} %bitcast.91, ...), custom_call_target="tpu_custom_call" | custom-call | tf_op jit(solution)/shard_map/open_plane/pallas_call | solution.py:367
  120.5 2.1 copy-done.8
  124.2 3.3 copy-done.27
  128.1 2.0 fusion.27
  130.1 12.5 %fusion.6 = f32[4,512,1024]{2,1,0:T(8,128)S(1)} fusion(bf16[4,512,2048]{2,1,0:T(8,128)(2,1)} %copy-done.27, bf16[2048,1024]{1,0:T(8,128)(2,1)} %copy-done.8), kind=kOutput, calls=%fused_computation.14 | convolution fusion | flops 8589934592 | bytes 20971520 | tf_op jit(solution)/shard_map/sti,io->sto/dot_general | solution.py:1007
  142.7 2.2 subtract_convert_fusion.1
  146.9 49.1 %line_scan.2 = (bf16[4,256,512]{2,1,0:T(8,128)(2,1)S(1)}, bf16[4,512,2048]{2,1,0:T(8,128)(2,1)}) custom-call(f32[4,256,512]{2,1,0:T(8,128)S(1)} %fusion.18.state, f32[2,4]{1,0:T(2,128)S(1)} %stack.8.coef, bf16[2,128,2048]{2,1,0:T(8,128)(2,1)S(1)} %copy-done.4), custom_call_target="tpu_custom_call" | custom-call | tf_op jit(solution)/shard_map/line_scan/pallas_call | solution.py:846
  196.1 2.1 fusion.11
  201.2 2.0 copy-done.29
  204.3 22.8 %all-gather.4.cloned.1.call-done = bf16[4096,512]{1,0:T(8,128)(2,1)} async-done(((bf16[1024,512]{1,0:T(8,128)(2,1)}), bf16[4096,512]{1,0:T(8,128)(2,1)}) %all-gather.4.cloned.1.call-update) | async-done | bytes 4194320 | tf_op jit(solution)/shard_map/all_gather | solution.py:1080
  227.1 2.5 broadcast_add_fusion
  229.6 2.1 copy-done.37
  233.8 1.9 broadcast_add_fusion.2
  235.8 3.0 multiply_reduce_fusion.1
  239.7 1.6 copy.67
  241.4 2.0 copy.114
  243.3 1.6 slice-done.1
  246.1 7.0 multiply_convert_fusion.4
  253.2 80.9 %plane_mix.1 = (f32[2,128,2048]{2,1,0:T(8,128)S(1)}, bf16[4,512,2048]{2,1,0:T(8,128)(2,1)}) custom-call(bf16[4,512,512]{2,1,0:T(8,128)(2,1)S(1)} %get-tuple-element.97.gated, bf16[512,2048]{1,0:T(8,128)(2,1)} %bitcast.102, bf16[2,128,2048]{2,1,0:T(8,128)(2,1)S(1)} %copy-done), custom_call_target="tpu_custom_call" | custom-call | tf_op jit(solution)/shard_map/plane_mix/pallas_call | solution.py:590
  337.7 3.1 all-gather.8.cloned.1.call-done.weight
  340.9 10.6 %multiply_convert_fusion.3 = (bf16[4,512,512]{2,1,0:T(8,128)(2,1)}, f32[4,512,512]{2,1,0:T(8,128)S(1)}) fusion(f32[512]{0:T(512)S(1)} %convert_reduce_fusion, bf16[4,512,2048]{2,1,0:T(8,128)(2,1)} %get-tuple-element.50, bf16[2048,512]{1,0:T(8,128)(2,1)} %all-gather.8.cloned.1.call-done.weight), kind=kOutput, calls=%fused_computation.23 | convolution fusion | flops 4301258752 | bytes 16779264 | tf_op jit(solution)/shard_map/sti,io->sto/dot_general | solution.py:1007
  351.5 8.3 %fusion.5.grad = bf16[4,512,512]{2,1,0:T(8,128)(2,1)S(1)} fusion(f32[4,512,512]{2,1,0:T(8,128)S(1)} %get-tuple-element.100, bf16[4,512,2048]{2,1,0:T(8,128)(2,1)} %get-tuple-element.47, bf16[512,2176]{1,0:T(8,128)(2,1)S(1)} %copy-done.48, f32[512]{0:T(512)S(1)} %convert_reduce_fusion), kind=kOutput, calls=%fused_computation.7 | convolution fusion | flops 4306501632 | bytes 16779264 | tf_op jit(solution)/shard_map/sto,io->sti/dot_general | solution.py:1011
  361.1 6.2 bitcast_convert_fusion.3.refs_1_
  367.3 2.3 fusion.16
  369.7 8.6 %bitcast_convert_fusion.4 = bf16[512,2048]{1,0:T(8,128)(2,1)S(1)} fusion(bf16[4,512,512]{2,1,0:T(8,128)(2,1)} %get-tuple-element.99.refs_0_, bf16[4,512,2048]{2,1,0:T(8,128)(2,1)} %get-tuple-element.47), kind=kOutput, calls=%fused_computation.13 | convolution fusion | flops 4296015872 | bytes 12582912 | tf_op jit(solution)/shard_map/sti,sto->io/dot_general | solution.py:1015
  378.3 1.5 pad_maximum_fusion.1.refs_0_
  379.9 4.6 reshape.526
  384.5 1.6 copy-done.12
  386.1 81.3 %plane_turn.1 = (f32[2,128,2048]{2,1,0:T(8,128)S(1)}, bf16[4,512,2048]{2,1,0:T(8,128)(2,1)}) custom-call(bf16[4,512,512]{2,1,0:T(8,128)(2,1)S(1)} %copy-done.12, bf16[2048,512]{1,0:T(8,128)(2,1)} %all-gather.8.cloned.1.call-done.weight, f32[2,128,2048]{2,1,0:T(8,128)} %copy-done.1, bf16[2,128,2048]{2,1,0:T(8,128)(2,1)S(1)} %copy-done.4, ...), custom_call_target="tpu_custom_call" | custom-call | tf_op jit(solution)/shard_map/plane_turn/pallas_call | solution.py:632
  472.4 12.3 %fusion.33 = (f32[4,512]{1,0:T(4,128)S(1)}, f32[4,512]{1,0:T(4,128)S(1)}, f32[4,512,512]{2,1,0:T(8,128)}, bf16[4,512,512]{2,1,0:T(8,128)(2,1)S(1)}) fusion(f32[4,512]{1,0:T(4,128)S(1)} %add_rsqrt_fusion, f32[4,512,512]{2,1,0:T(8,128)} %copy-done.29, f32[4,512]{1,0:T(4,128)S(1)} %broadcast_multiply_fusion.2, f32[4,512,512]{2,1,0:T(8,128)} %get-tuple-element.98, ...), kind=kOutput, calls=%fused_computation.100 | convolution fusion | flops 4313837568 | bytes 25198600 | tf_op jit(solution)/shard_map/sto,io->sti/dot_general | solution.py:1011
  486.1 9.4 %bitcast_convert_fusion.2.refs_3_ = bf16[2048,512]{1,0:T(8,128)(2,1)} fusion(bf16[4,512,2048]{2,1,0:T(8,128)(2,1)} %copy-done.27, bf16[4,512,512]{2,1,0:T(8,128)(2,1)S(1)} %get-tuple-element.73.refs_2_), kind=kOutput, calls=%fused_computation.11 | convolution fusion | flops 4296015872 | bytes 12582912 | tf_op jit(solution)/shard_map/sti,sto->io/dot_general | solution.py:1015
  495.8 9.9 %bitcast_convert_fusion.1.refs_4_ = bf16[512,2048]{1,0:T(8,128)(2,1)} fusion(bf16[4,512,512]{2,1,0:T(8,128)(2,1)} %copy-done.10, bf16[4,512,2048]{2,1,0:T(8,128)(2,1)} %get-tuple-element.53), kind=kOutput, calls=%fused_computation.10 | convolution fusion | flops 4296015872 | bytes 12582912 | tf_op jit(solution)/shard_map/sti,sto->io/dot_general | solution.py:1015
  505.8 4.2 multiply_convert_fusion.2
  510.1 3.6 multiply_convert_fusion
  513.7 2.3 fusion.42
  517.6 3.3 fusion.43
  520.9 2.1 multiply_add_fusion.2
  523.0 81.8 %line_scan.3 = (bf16[4,256,512]{2,1,0:T(8,128)(2,1)S(1)}, bf16[2,128,2048]{2,1,0:T(8,128)(2,1)S(1)}) custom-call(f32[4,256,512]{2,1,0:T(8,128)S(1)} %fusion.17.state, f32[2,4]{1,0:T(2,128)S(1)} %stack.9.coef, bf16[4,512,512]{2,1,0:T(8,128)(2,1)} %get-tuple-element.99.refs_0_, bf16[512,2176]{1,0:T(8,128)(2,1)} %all-gather.6.cloned.1.call-done.refs_1_, ...), custom_call_target="tpu_custom_call" | custom-call | tf_op jit(solution)/shard_map/line_scan/pallas_call | solution.py:846
  604.9 2.5 multiply_add_fusion.1
  607.8 2.0 add_convert_fusion
  614.4 13.4 %bitcast_convert_fusion.refs_13_ = bf16[2048,1024]{1,0:T(8,128)(2,1)} fusion(bf16[4,512,2048]{2,1,0:T(8,128)(2,1)} %copy-done.27, bf16[]{:T(256)} %bitcast.30, bf16[4,512,512]{2,1,0:T(8,128)(2,1)S(1)} %copy-done.46, bf16[4,512,128]{2,1,0:T(8,128)(2,1)} %get-tuple-element.85, bf16[4,512,128]{2,1,0:T(8,128)(2,1)} %get-tuple-element.84, ...), kind=kOutput, calls=%fused_computation | convolution fusion | flops 8613003264 | bytes 16777218 | tf_op jit(solution)/shard_map/sti,sto->io/dot_general | solution.py:1015
  627.8 1.4 convert_reduce_fusion.1
  629.2 3.6 pad_maximum_fusion.refs_0_
  632.8 67.7 %plane_last.1 = (f32[2,128,2048]{2,1,0:T(8,128)}, f32[64,4096]{1,0:T(8,128)}, f32[64,4096]{1,0:T(8,128)}, f32[64,1]{1,0:T(8,128)}, f32[64,1]{1,0:T(8,128)}, /*index=5*/f32[128,2048]{1,0:T(8,128)}) custom-call(bf16[4,512,1024]{2,1,0:T(8,128)(2,1)} %pad_maximum_fusion.refs_0_, bf16[2048,1024]{1,0:T(8,128)(2,1)} %copy-done.8, bf16[4,512,512]{2,1,0:T(8,128)(2,1)} %copy-done.51, ...), custom_call_target="tpu_custom_call" | custom-call | tf_op jit(solution)/shard_map/plane_last/pallas_call | solution.py:699
  700.5 1.4 reduce.2
  703.0 1.6 copy-done.2
  706.8 29.7 %plane_final.1 = (f32[64,2048]{1,0:T(8,128)S(1)}, f32[64,2048]{1,0:T(8,128)S(1)}, f32[64,4096]{1,0:T(8,128)S(1)}, f32[128,2048]{1,0:T(8,128)S(1)}, f32[64,1]{1,0:T(8,128)S(1)}) custom-call(bf16[8,64,1024]{2,1,0:T(8,128)(2,1)S(1)} %bitcast.90, bf16[128,2048]{1,0:T(8,128)(2,1)S(1)} %copy-done.25, f32[64,2048]{1,0:T(8,128)S(1)} %copy-done.14, ...), custom_call_target="tpu_custom_call" | custom-call | tf_op jit(solution)/shard_map/plane_final/pallas_call | solution.py:949
  (195 shorter events, 49.1 us)
Async XLA Ops:
  7.2 41.5 %copy-start = (bf16[2,128,2048]{2,1,0:T(8,128)(2,1)S(1)}, bf16[2,128,2048]{2,1,0:T(8,128)(2,1)}, u32[]{:S(2)}) copy-start(bf16[2,128,2048]{2,1,0:T(8,128)(2,1)} %refs_4_.1) | copy-start | bytes 3145732
  7.2 219.9 %all-gather.4.cloned.1.call-start = ((), (), s32[]{:S(2)}) async-start(), calls=%async_computation.5 | async-start | bytes 5242880 | tf_op jit(solution)/shard_map/all_gather | solution.py:1080
  8.7 111.8 %copy-start.22 = (f32[64,1]{1,0:T(8,128)}, f32[64,1]{1,0:T(8,128)S(1)}, u32[]{:S(2)}) copy-start(f32[64,1]{1,0:T(8,128)S(1)} %copy.57.refs_4_.refs_10_.refs_3_) | copy-start | bytes 772
  8.8 111.7 %copy-start.26 = (f32[64,1]{1,0:T(8,128)}, f32[64,1]{1,0:T(8,128)S(1)}, u32[]{:S(2)}) copy-start(f32[64,1]{1,0:T(8,128)S(1)} %copy.59.refs_7_.refs_11_) | copy-start | bytes 772
  16.0 32.6 %copy-start.5 = (f32[64,4096]{1,0:T(8,128)S(1)}, f32[64,4096]{1,0:T(8,128)}, u32[]{:S(2)}) copy-start(f32[64,4096]{1,0:T(8,128)} %refs_9_.1) | copy-start | bytes 3145732
  16.0 32.6 %copy-start.18 = (f32[128,2048]{1,0:T(8,128)S(1)}, f32[128,2048]{1,0:T(8,128)}, u32[]{:S(2)}) copy-start(f32[128,2048]{1,0:T(8,128)} %refs_5_.3) | copy-start | bytes 3145732
  120.5 2.1 copy-start.8
  124.2 3.3 copy-start.27
  127.5 209.2 %all-gather.6.cloned.1.call-start = ((), (), s32[]{:S(2)}) async-start(), calls=%async_computation.6 | async-start | bytes 2785280 | tf_op jit(solution)/shard_map/all_gather | solution.py:1080
  130.1 12.6 %copy-start.49 = (f32[512,128]{1,0:T(8,128)}, f32[512,128]{1,0:T(8,128)S(1)}, u32[]{:S(2)}) copy-start(f32[512,128]{1,0:T(8,128)S(1)} %get-tuple-element.88) | copy-start | bytes 786436
  142.6 56.4 %copy-start.28 = (f32[4,512,1024]{2,1,0:T(8,128)}, f32[4,512,1024]{2,1,0:T(8,128)S(1)}, u32[]{:S(2)}) copy-start(f32[4,512,1024]{2,1,0:T(8,128)S(1)} %fusion.6) | copy-start | bytes 25165828
  144.9 53.3 %copy-start.39 = (bf16[4,512,128]{2,1,0:T(8,128)(2,1)}, bf16[4,512,128]{2,1,0:T(8,128)(2,1)S(1)}, u32[]{:S(2)}) copy-start(bf16[4,512,128]{2,1,0:T(8,128)(2,1)S(1)} %get-tuple-element.74) | copy-start | bytes 1572868
  144.9 53.3 %copy-start.41 = (bf16[4,512,128]{2,1,0:T(8,128)(2,1)}, bf16[4,512,128]{2,1,0:T(8,128)(2,1)S(1)}, u32[]{:S(2)}) copy-start(bf16[4,512,128]{2,1,0:T(8,128)(2,1)S(1)} %get-tuple-element.75) | copy-start | bytes 1572868
  196.1 2.1 copy-start.43
  198.2 2.1 copy-start.31
  227.1 5.8 copy-start.21
  229.6 2.1 copy-start.37
  233.8 107.1 %all-gather.8.cloned.1.call-start = ((), (), s32[]{:S(2)}) async-start(), calls=%async_computation.7 | async-start | bytes 2621440 | tf_op jit(solution)/shard_map/all_gather | solution.py:1080
  235.7 233.0 %reduce-scatter.6.cloned.1.call-start = ((), (), s32[]{:S(2)}) async-start(), calls=%async_computation.8 | async-start | bytes 2621440 | tf_op jit(solution)/shard_map/reduce_scatter | solution.py:1083
  235.8 3.5 copy-start.38
  239.2 4.1 slice-start
  239.7 3.6 copy-start.45
  239.7 5.2 slice-start.1
  239.7 6.4 copy-start.30
  241.4 11.8 %copy-start.35 = (bf16[1,4,128,4,512]{4,3,2,1,0:T(4,128)(2,1)}, bf16[1,4,128,4,512]{4,3,2,1,0:T(4,128)(2,1)S(1)}, u32[]{:S(2)}) copy-start(bf16[1,4,128,4,512]{4,3,2,1,0:T(4,128)(2,1)S(1)} %copy.67) | copy-start | bytes 6291460
  340.8 10.6 %copy-start.48 = (bf16[512,2176]{1,0:T(8,128)(2,1)S(1)}, bf16[512,2176]{1,0:T(8,128)(2,1)}, u32[]{:S(2)}) copy-start(bf16[512,2176]{1,0:T(8,128)(2,1)} %all-gather.6.cloned.1.call-done.refs_1_) | copy-start | bytes 6684676
  340.9 20.2 %slice-start.4 = ((s8[8388608]{0:T(1024)(128)(4,1)}), s8[4194304]{0:T(1024)(128)(4,1)S(1)}, s32[]{:S(2)}) async-start(s8[8388608]{0:T(1024)(128)(4,1)} %bitcast.109), calls=%async_computation.17 | async-start | bytes 8388608
  351.5 9.6 %slice-start.5 = ((s8[8388608]{0:T(1024)(128)(4,1)}), s8[4194304]{0:T(1024)(128)(4,1)S(1)}, s32[]{:S(2)}) async-start(s8[8388608]{0:T(1024)(128)(4,1)} %bitcast.109), calls=%async_computation.18 | async-start | bytes 8388608
  367.3 103.3 %reduce-scatter.8.cloned.1.call-start = ((), (), s32[]{:S(2)}) async-start(), calls=%async_computation.9 | async-start | bytes 2785280 | tf_op jit(solution)/shard_map/reduce_scatter | solution.py:1083
  379.8 232.7 %reduce-scatter.10.cloned.1.call-start = ((), (), s32[]{:S(2)}) async-start(), calls=%async_computation.10 | async-start | bytes 2621440 | tf_op jit(solution)/shard_map/reduce_scatter | solution.py:1083
  495.5 206.4 %reduce-scatter.14.cloned.1.call-start = ((), (), s32[]{:S(2)}) async-start(), calls=%async_computation.12 | async-start | bytes 2621440 | tf_op jit(solution)/shard_map/reduce_scatter | solution.py:1083
  505.7 197.2 %reduce-scatter.12.cloned.1.call-start = ((), (), s32[]{:S(2)}) async-start(), calls=%async_computation.11 | async-start | bytes 5242880 | tf_op jit(solution)/shard_map/reduce_scatter | solution.py:1083
  505.8 4.2 copy-start.44
  510.1 3.6 copy-start.32
  513.7 2.3 copy-start.40
  513.7 2.3 copy-start.42
  520.9 84.0 %slice-start.2 = ((s8[8388608]{0:T(1024)(128)(4,1)}), s8[4194304]{0:T(1024)(128)(4,1)S(1)}, s32[]{:S(2)}) async-start(s8[8388608]{0:T(1024)(128)(4,1)} %bitcast.95), calls=%async_computation.15 | async-start | bytes 8388608
  523.0 81.9 %slice-start.3 = ((s8[8388608]{0:T(1024)(128)(4,1)}), s8[4194304]{0:T(1024)(128)(4,1)S(1)}, s32[]{:S(2)}) async-start(s8[8388608]{0:T(1024)(128)(4,1)} %bitcast.95), calls=%async_computation.16 | async-start | bytes 8388608
  604.9 2.9 copy-start.36
  610.1 4.3 copy-start.46
  632.8 70.2 %copy-start.7 = (f32[64,4096]{1,0:T(8,128)S(1)}, f32[64,4096]{1,0:T(8,128)}, u32[]{:S(2)}) copy-start(f32[64,4096]{1,0:T(8,128)} %refs_2_.3) | copy-start | bytes 3145732
  632.8 70.2 %copy-start.14 = (f32[64,2048]{1,0:T(8,128)S(1)}, f32[64,2048]{1,0:T(8,128)}, u32[]{:S(2)}) copy-start(f32[64,2048]{1,0:T(8,128)} %refs_0_.7) | copy-start | bytes 1572868
  632.8 70.2 %copy-start.16 = (f32[64,2048]{1,0:T(8,128)S(1)}, f32[64,2048]{1,0:T(8,128)}, u32[]{:S(2)}) copy-start(f32[64,2048]{1,0:T(8,128)} %refs_1_.5) | copy-start | bytes 1572868
  632.8 70.2 %copy-start.23 = (f32[64,1]{1,0:T(8,128)S(1)}, f32[64,1]{1,0:T(8,128)}, u32[]{:S(2)}) copy-start(f32[64,1]{1,0:T(8,128)} %copy-done.22) | copy-start | bytes 772
  700.5 36.0 %copy-start.57 = (f32[64,1]{1,0:T(8,128)S(1)}, f32[64,1]{1,0:T(8,128)}, u32[]{:S(2)}) copy-start(f32[64,1]{1,0:T(8,128)} %get-tuple-element.59) | copy-start | bytes 772
  738.1 3.9 copy-start.55
  739.4 4.5 copy-start.54
  741.0 3.9 copy-start.53
  (24 other events, 34.0 us)
Sparse Core Ops, SparseCore 0:
  127.6 99.4 all-gather.3
  233.9 59.9 all-gather.5
  296.0 44.7 all-gather.7
  367.4 51.8 reduce-scatter.5
  421.6 45.2 reduce-scatter.7
  495.7 58.9 reduce-scatter.9
  557.0 54.1 reduce-scatter.13
  627.9 74.9 reduce-scatter.11

commit v4 on v3

--- a/solution.py
+++ b/solution.py
@@ -160,14 +160,14 @@
     copies = []
     for a in range(len(sources)):
         copies.append(
-            pltpu.make_async_copy(sources[a].at[me], targets[a].at[me], keep_sem.at[a])
+            pltpu.make_async_copy(sources[a].at[me], targets[a](me), keep_sem.at[a])
         )
         for i in (6, 5, 4, 3, 2, 1, 0):
             r, c = peers[i]
             copies.append(
                 pltpu.make_async_remote_copy(
                     src_ref=sources[a].at[r * 4 + c],
-                    dst_ref=targets[a].at[me],
+                    dst_ref=targets[a](me),
                     send_sem=send_sem.at[a, i],
                     recv_sem=recv_sem.at[a, i],
                     device_id={"dpl": r, "ka": c},
@@ -184,6 +184,10 @@
             copy.wait()
 
     return [{"dpl": r, "ka": c} for r, c in peers], (begin, end)
+
+
+def blocks_of(ref):
+    return lambda j: ref.at[j]
 
 
 def owners_scratch(count):
@@ -243,17 +247,16 @@
 TRADE_SCRATCH = (pltpu.SemaphoreType.DMA((3,)),)
 
 
-def line_gather_stages(count, chunks, block, full, send_sem, recv_sem):
+def line_gather_stages(count, chunks, full, send_sem, recv_sem):
     here = lax.axis_index("pb")
-    rows = block.shape[0]
+    rows = full.shape[0] // count
     size = rows // chunks
 
     def hop(up, distance, c):
         owner = here - distance if up else here + distance
         place = full.at[pl.ds(owner * rows + c * size, size)]
-        source = block.at[pl.ds(c * size, size)] if distance == 0 else place
         return pltpu.make_async_remote_copy(
-            src_ref=source,
+            src_ref=place,
             dst_ref=place,
             send_sem=send_sem.at[int(up), distance, c],
             recv_sem=recv_sem.at[int(up), distance, c],
@@ -295,15 +298,39 @@
     return step, finish
 
 
-def open_kernel(
-    count, chunks, order, moves, unit_moves, x, up, first, gate, out, down, bias, gain, *refs
-):
-    normed_all, up_mine, first_all, gate_out, down_pack, normed, up_low, down_low = refs[:8]
-    sems = refs[8:]
-    targets, owners = owners_stages((up_low if unit_moves else up,), (up_mine,), *sems[3:6])
+def open_kernel(count, chunks, line, order, moves, unit_moves, head_moves, *refs):
+    weights, gain_one, out, docs, x, up, down, bias, gain_two = refs[:4], *refs[4:12]
+    normed_all, up_mine, first_all, gate_out, down_pack, docs_all = refs[-28:-22]
+    qkv_pack, gate_pack, out_low, out_mine, normed, up_low, down_low, bias_low = refs[-22:-14]
+    sems = refs[-14:]
+    row, _, other_row, _, _ = plane_ids()
+    here = lax.axis_index("pb")
+    group, rows, _ = qkv_pack.shape
+
+    def first_block(j):
+        return first_all.at[pl.ds(here * (group * rows) + j * rows, rows)]
+
+    def gate_block(j):
+        return gate_out.at[pl.ds(j * rows, rows)]
+
     _, gather = gather_stages(normed, normed_all, *sems[:3])
-    step, finish = line_gather_stages(count, chunks, first, first_all, *sems[6:8])
-    here = lax.axis_index("pb")
+    targets, first = owners_stages((qkv_pack,), (first_block,), *sems[3:6])
+    _, second = owners_stages((gate_pack,), (gate_block,), *sems[6:9])
+    _, third = owners_stages(
+        (up_low if unit_moves else up,),
+        (blocks_of(up_mine),),
+        sems[9].at[pl.ds(0, 1)],
+        sems[10].at[pl.ds(0, 1)],
+        sems[10].at[pl.ds(1, 1)],
+    )
+    greet_partner, trade = trade_stages(line, out_low, out_mine, sems[9].at[pl.ds(1, 3)])
+    step, finish = line_gather_stages(count, chunks, first_all, *sems[11:13])
+
+    def pack(i, target):
+        for j, column, place, size in head_moves[i]:
+            block = weights[i][:, column : column + size].astype(BF16).astype(F32)
+            target[j, :, place : place + size] = (block * gain_one[...]).astype(BF16)
+
     barrier = pltpu.get_barrier_semaphore()
     for target in targets:
         pl.semaphore_signal(barrier, inc=1, device_id=target, device_id_type=MESH)
@@ -317,34 +344,49 @@
         pl.semaphore_signal(barrier, inc=1, device_id={"pb": here + 1}, device_id_type=MESH)
 
     ends = (here > 0).astype(jnp.int32) + (here < count - 1).astype(jnp.int32)
-    pl.semaphore_wait(barrier, len(targets) + ends)
+    greeted = greet_partner(barrier) + len(targets) + ends
+    for i in (0, 1, 2):
+        pack(i, qkv_pack)
+    pl.semaphore_wait(barrier, greeted)
+    first[0]()
+    give = pltpu.make_async_remote_copy(
+        src_ref=docs,
+        dst_ref=docs_all.at[row],
+        send_sem=sems[9].at[4],
+        recv_sem=sems[9].at[5],
+        device_id={"dpl": other_row},
+        device_id_type=MESH,
+    )
+    keep = pltpu.make_async_copy(docs, docs_all.at[row], sems[9].at[6])
+    give.start()
+    keep.start()
+    out_low[...] = out[...].astype(BF16)
+    trade[0]()
+    first[1]()
     for c in range(chunks):
         step(0, c)
     normalize_rows(x, normed, order)
     gather[0]()
+    pack(3, gate_pack)
+    second[0]()
     for j, source, target, size in unit_moves:
-        block = up[:, source : source + size].astype(BF16).astype(F32) * gain[...]
+        block = up[:, source : source + size].astype(BF16).astype(F32) * gain_two[...]
         up_low[j, :, target : target + size] = block.astype(BF16)
-    owners[0]()
-    height, lanes, wide = gate.shape[0], gate.shape[1], out.shape[0]
+    third[0]()
+    lanes, wide = gate_out.shape[1], out.shape[0]
     for source, target, size in moves:
         down_low[:, target : target + size] = down[:, source : source + size].astype(BF16)
-    down_low[:, down.shape[1] :] = jnp.broadcast_to(bias[...], (wide, 128)).astype(BF16)
-    pairs = [
-        (first, first_all.at[pl.ds(here * first.shape[0], first.shape[0])]),
-        (gate, gate_out.at[pl.ds(0, height)]),
-        (down_low, down_pack),
-    ]
+    bias_low[...] = jnp.zeros(bias_low.shape, BF16)
+    bias_low[0:1, 0:wide] = bias[...].astype(BF16)
+    trade[1]()
+    edge = gate_out.shape[0] - bias_low.shape[0]
+    pairs = [(down_low, down_pack), (bias_low, gate_out.at[pl.ds(edge, bias_low.shape[0])])]
     for source, target, size in moves:
+        place = pl.ds(group * rows + target // lanes * wide, wide)
         pairs.append(
-            (
-                out.at[:, pl.ds(source, size)],
-                gate_out.at[
-                    pl.ds(height + target // lanes * wide, wide), pl.ds(target % lanes, size)
-                ],
-            )
+            (out_mine.at[:, pl.ds(source, size)], gate_out.at[place, pl.ds(target % lanes, size)])
         )
-    copies = [pltpu.make_async_copy(a, b, sems[8].at[i]) for i, (a, b) in enumerate(pairs)]
+    copies = [pltpu.make_async_copy(a, b, sems[13].at[i]) for i, (a, b) in enumerate(pairs)]
     for copy in copies:
         copy.start()
     for c in range(chunks):
@@ -355,45 +397,63 @@
             step(distance, c)
             if distance == 2 and c == chunks // 2:
                 gather[2]()
+    give.wait()
+    keep.wait()
     for copy in copies:
         copy.wait()
+    second[1]()
     gather[3]()
-    owners[1]()
+    third[1]()
     finish()
 
 
-def open_plane(x, up, first, gate, out, down, bias, gain, up_shape, order, moves, unit_moves, count, collective_id, *before):
+def open_plane(
+    weights, gain_one, out, docs, x, up, down, bias, gain_two, line, order, moves, unit_moves, head_moves, units, count, collective_id
+):
     chunks = 4
+    group = len(head_moves[0])
+    rows = gain_one.shape[0]
+    first = sum(w.shape[1] for w in weights[:3]) // group
+    edge = 16
     return pl.pallas_call(
-        lambda *refs: open_kernel(
-            count, chunks, order, moves, unit_moves, *refs[:8], *refs[8 + len(before) :]
+        functools.partial(
+            open_kernel, count, chunks, line, order, moves, unit_moves, head_moves
         ),
         out_shape=[
             gathered_shape(x),
-            jax.ShapeDtypeStruct(up_shape, BF16),
-            jax.ShapeDtypeStruct((count * first.shape[0], first.shape[1]), BF16),
-            jax.ShapeDtypeStruct((gate.shape[0] + out.size // gate.shape[1], gate.shape[1]), BF16),
-            jax.ShapeDtypeStruct((down.shape[0], down.shape[1] + 128), BF16),
+            jax.ShapeDtypeStruct((group, rows, units), BF16),
+            jax.ShapeDtypeStruct((count * group * rows, first), BF16),
+            jax.ShapeDtypeStruct((group * rows + out.size // units + edge, units), BF16),
+            jax.ShapeDtypeStruct(down.shape, BF16),
+            jax.ShapeDtypeStruct((2,) + docs.shape, docs.dtype),
         ],
-        in_specs=[VMEM, VMEM, ANY, ANY, ANY, VMEM, VMEM, VMEM] + [ANY] * len(before),
-        out_specs=[ANY] * 5,
+        in_specs=[VMEM] * 12,
+        out_specs=[ANY] * 6,
         scratch_shapes=[
+            pltpu.VMEM((group, rows, first), BF16),
+            pltpu.VMEM((group, rows, units), BF16),
+            pltpu.VMEM(out.shape, BF16),
+            pltpu.VMEM(out.shape, BF16),
             pltpu.VMEM(x.shape, BF16),
-            pltpu.VMEM(up_shape, BF16),
-            pltpu.VMEM((down.shape[0], down.shape[1] + 128), BF16),
+            pltpu.VMEM((group, rows, units), BF16),
+            pltpu.VMEM(down.shape, BF16),
+            pltpu.VMEM((edge, units), BF16),
             *GATHER_SCRATCH,
             *owners_scratch(1),
+            *owners_scratch(1),
+            pltpu.SemaphoreType.DMA((7,)),
+            pltpu.SemaphoreType.DMA((2, 7)),
             pltpu.SemaphoreType.DMA((2, count, chunks)),
             pltpu.SemaphoreType.DMA((2, count, chunks)),
-            pltpu.SemaphoreType.DMA((3 + len(moves),)),
+            pltpu.SemaphoreType.DMA((2 + len(moves),)),
         ],
         compiler_params=pltpu.CompilerParams(
             collective_id=collective_id,
             has_side_effects=True,
-            vmem_limit_bytes=20 * 1024 * 1024,
+            vmem_limit_bytes=32 * 1024 * 1024,
         ),
         name="open_plane",
-    )(x, up, first, gate, out, down, bias, gain, *before)
+    )(*weights, gain_one, out, docs, x, up, down, bias, gain_two)
 
 
 def scatter_stages(
@@ -422,7 +482,11 @@
             device_id_type=MESH,
         )
 
-    swaps = [hop(sent.at[j], sib.at[j], j, to_s) for j in range(4)]
+    swaps = [hop(sent.at[j], sib.at[j], j, to_s) for j in range(1, 4)]
+    heads = [
+        hop(sent.at[0, :, part, :], sib.at[0, :, part, :], i, to_s)
+        for part, i in ((lower, 0), (upper, 10))
+    ]
     first_a = hop(own.at[0, :, lower, :], diag_a, 4, to_x)
     first_b = hop(own.at[0, :, upper, :], diag_b, 5, to_y)
     x_lower = hop(own.at[1, :, lower, :], from_x.at[:, lower, :], 6, to_x)
@@ -430,13 +494,13 @@
     x_upper = hop(own.at[1, :, upper, :], from_x.at[:, upper, :], 8, to_x)
     y_lower = hop(own.at[2, :, lower, :], from_y.at[:, lower, :], 9, to_y)
 
-    def make(r, c, out):
+    def make(r, c, out, start=0, size=length):
         def body(n, carry):
             columns = pl.ds(pl.multiple_of(n * tile, tile), tile)
             value = 0.0
             for left, right, flipped in terms:
-                block = left[pl.ds(r * batch, batch), pl.ds(c * length, length), :]
-                block = block.reshape(batch * length, left.shape[2])
+                block = left[pl.ds(r * batch, batch), pl.ds(c * length + start, size), :]
+                block = block.reshape(batch * size, left.shape[2])
                 if flipped:
                     value = value + lax.dot_general(
                         block,
@@ -448,14 +512,25 @@
                     value = value + jnp.dot(
                         block, right[:, columns], preferred_element_type=F32
                     )
-            out[:, :, columns] = value.reshape(batch, length, tile).astype(BF16)
+            out[:, pl.ds(start, size), columns] = value.reshape(batch, size, tile).astype(BF16)
             return carry
 
         lax.fori_loop(0, width // tile, body, 0)
 
     def give(j):
         make(*theirs[j], sent.at[j])
-        swaps[j].start()
+        swaps[j - 1].start()
+
+    def give_head(i):
+        make(*theirs[0], sent.at[0], i * half, half)
+        heads[i].start()
+
+    def own_head(i):
+        make(*mine[0], own.at[0], i * half, half)
+
+    def merge_head(i):
+        heads[i].wait_recv()
+        add(own.at[0], i * half, ((own.at[0], i * half), (sib.at[0], i * half)), half)
 
     def add(out_ref, out_start, parts, size):
         def body(i, carry):
@@ -468,12 +543,21 @@
         lax.fori_loop(0, size // step, body, 0)
 
     def merge(j):
-        swaps[j].wait_recv()
+        swaps[j - 1].wait_recv()
         add(own.at[j], 0, ((own.at[j], 0), (sib.at[j], 0)), length)
 
+    def open_heads():
+        give_head(0)
+        own_head(0)
+        give_head(1)
+
+    def send_head():
+        merge_head(0)
+        first_a.start()
+        own_head(1)
+
     def send_diag():
-        merge(0)
-        first_a.start()
+        merge_head(1)
         first_b.start()
         make(*mine[1], own.at[1])
 
@@ -527,12 +611,12 @@
             copy.wait_send()
 
     def stage_free():
-        for copy in swaps:
+        for copy in heads + swaps:
             copy.wait_send()
 
     stages = (
-        lambda: give(0),
-        lambda: make(*mine[0], own.at[0]),
+        open_heads,
+        send_head,
         lambda: give(1),
         send_diag,
         lambda: give(2),
@@ -557,8 +641,8 @@
         pltpu.VMEM(shape, BF16),
         pltpu.VMEM((batch, length // 2, width), BF16),
         pltpu.VMEM((batch, length // 2, width), BF16),
-        pltpu.SemaphoreType.DMA((10,)),
-        pltpu.SemaphoreType.DMA((10,)),
+        pltpu.SemaphoreType.DMA((11,)),
+        pltpu.SemaphoreType.DMA((11,)),
     ]
 
 
@@ -566,8 +650,18 @@
 ANY = pl.BlockSpec(memory_space=pl.ANY)
 
 
-def mix_kernel(order, gated, weight, x, *refs):
-    middle, normed_all, normed = refs[-15:-12]
+def mix_kernel(order, places, gated, x, gate_out, *refs):
+    middle, normed_all, weight, normed, load_sem = refs[-17:-12]
+    loads = [
+        pltpu.make_async_copy(
+            gate_out.at[pl.ds(source, rows)],
+            weight.at[pl.ds(row, rows), pl.ds(column, gate_out.shape[1])],
+            load_sem.at[i],
+        )
+        for i, (source, row, column, rows) in enumerate(places)
+    ]
+    for load in loads:
+        load.start()
 
     def finish(b, at, value):
         value = value + read_rows(x, b, at, order).astype(F32)
@@ -577,6 +671,8 @@
     targets, stages = scatter_stages(((gated, weight, False),), finish, *refs[-12:-3], True)
     lower, upper = (gather_stages(normed, normed_all, *refs[-3:], i, 2)[1] for i in (0, 1))
     greet(targets)
+    for load in loads:
+        load.wait()
     for stage in stages[:10] + lower[:1] + stages[10:11] + upper[:1]:
         stage()
     for pair in zip(lower[1:], upper[1:]):
@@ -585,15 +681,20 @@
     stages[11]()
 
 
-def plane_mix(gated, weight, x, order, collective_id, *before):
+def plane_mix(gated, x, gate_out, places, order, collective_id, *before):
     shape = x.shape
     return pl.pallas_call(
-        functools.partial(mix_kernel, order),
-        out_shape=[jax.ShapeDtypeStruct(shape, F32), gathered_shape(x)],
-        in_specs=[VMEM] * 3 + [ANY] * len(before),
-        out_specs=[VMEM, ANY],
+        functools.partial(mix_kernel, order, places),
+        out_shape=[
+            jax.ShapeDtypeStruct(shape, F32),
+            gathered_shape(x),
+            jax.ShapeDtypeStruct((gated.shape[2], shape[2]), BF16),
+        ],
+        in_specs=[VMEM] * 2 + [ANY] * (1 + len(before)),
+        out_specs=[VMEM, ANY, VMEM],
         scratch_shapes=[
             pltpu.VMEM(shape, BF16),
+            pltpu.SemaphoreType.DMA((len(places),)),
             *scatter_scratch(shape),
             *GATHER_SCRATCH,
         ],
@@ -603,7 +704,7 @@
             vmem_limit_bytes=48 * 1024 * 1024,
         ),
         name="plane_mix",
-    )(gated, weight, x, *before)
+    )(gated, x, gate_out, *before)
 
 
 def turn_kernel(order, grad, weight, middle, cot, *refs):
@@ -659,9 +760,9 @@
 
 
 def last_kernel(order, moves, *refs):
-    grad_a, weight_a, grad_b, weight_b, x, grad_middle = refs[:6]
-    owned, weights, gains = refs[6:8], refs[8:10], refs[10:12]
-    grad_down = refs[12]
+    parts, weight_a, grad_b, weight_b, x, grad_middle = refs[:3], *refs[3:8]
+    owned, weights, gains = refs[8:10], refs[10:12], refs[12:14]
+    grad_down = refs[14]
     scratch = refs[-14:]
     outs = refs[-20:-14]
 
@@ -670,11 +771,15 @@
         value = grad_middle[b, at, :] + normalize_back(normed, inv, value)
         write_rows(outs[0], b, at, order, value)
 
-    terms = ((grad_a, weight_a, True), (grad_b, weight_b, True))
+    terms, place = [(grad_b, weight_b, True)], 0
+    for part in parts:
+        columns = pl.ds(place, part.shape[2])
+        terms.append((part, weight_a.at[:, columns], True))
+        place += part.shape[2]
     _, stages = scatter_stages(terms, finish, *scratch[:9])
-    targets, owners = owners_stages(owned, scratch[9:11], *scratch[11:14])
+    targets, owners = owners_stages(owned, [blocks_of(ref) for ref in scratch[9:11]], *scratch[11:14])
     greet(targets)
-    for stage in stages[:8] + owners[:1] + stages[8:9]:
+    for stage in owners[:1] + stages[:9]:
         stage()
     size = outs[5].shape[1] // max(len(order), 1)
     for j, i in enumerate(order or (0,)):
@@ -704,7 +809,7 @@
             for o, w, m in zip(owned, weights, moves)
         ]
         + [column, column, plain],
-        in_specs=[VMEM] * 6 + [ANY] * 2 + [VMEM] * 5 + [ANY] * len(before),
+        in_specs=[VMEM] * 8 + [ANY] * 2 + [VMEM] * 5 + [ANY] * len(before),
         out_specs=[VMEM] * 6,
         scratch_shapes=scatter_scratch(shape)
         + [pltpu.VMEM(o.shape, BF16) for o in owned]
@@ -726,7 +831,31 @@
         targets, stages = gather_stages(shard, result, *refs[-3:])
     else:
         left, right, middle = refs[:3]
-        total, result, message, landed, send_sem, recv_sem = refs[-15:-9]
+        query, key, value, grad, scores, carried = refs[3:9]
+        decay, decay_in, decay_out, cos_q, sin_q, cos_k, sin_k = refs[9:16]
+        total, result, out_q, out_k, out_v = refs[-20:-15]
+        sum_k, sum_v, message, landed, send_sem, recv_sem = refs[-15:-9]
+        scale = query.shape[2] ** (-0.5)
+
+        def dot(a, b, contract):
+            return lax.dot_general(
+                a, b, ((contract[:1], contract[1:]), ((), ())), preferred_element_type=F32
+            )
+
+        def within(s):
+            low = (dot(grad[s], value[s], (1, 1)) * decay[...]).astype(BF16)
+            part = dot(low, key[s], (1, 0))
+            part = part + decay_in[...] * dot(grad[s], carried[s], (1, 1))
+            part = turn_back(part, (cos_q[...], sin_q[...]))
+            out_q[s] = (part * scale).astype(BF16)
+            sum_k[s] = dot(low, query[s], (0, 0))
+            sum_v[s] = dot(scores[s], grad[s], (0, 0))
+
+        def across(s):
+            part = sum_k[s] + decay_out[...] * dot(value[s], total[s], (1, 1))
+            out_k[s] = turn_back(part, (cos_k[...], sin_k[...])).astype(BF16)
+            part = sum_v[s] + decay_out[...] * dot(key[s], total[s], (1, 0))
+            out_v[s] = part.astype(BF16)
 
         def finish(b, at, value):
             write_rows(result, b, at, order, (middle[b, at, :] + value).astype(BF16))
@@ -805,15 +934,24 @@
                     copy.start()
         stages[0]()
     count = len(pieces)
-    places = {count // 2: 1, 3 * count // 4: 2} if gathers else {i + 1: i for i in range(8)}
-    if not gathers:
-        places[3 * count // 4] = 8
+    if gathers:
+        jobs = {count // 2: stages[1:2], 3 * count // 4: stages[2:3]}
+        rest = stages[3:]
+    else:
+        jobs = {i + 1: [stage] for i, stage in enumerate(stages[:8])}
+        seqs = range(state.shape[0])
+        inner = [functools.partial(within, s) for s in seqs]
+        outer = [functools.partial(across, s) for s in seqs]
+        late = [*inner[:3], stages[8], *inner[3:]]
+        for i, job in enumerate(late):
+            jobs.setdefault(min(9 + i, count - 1), []).append(job)
+        rest = [*outer[:-1], *stages[9:], *outer[-1:]]
     for i in range(1, count):
         emit(i)
-        if i in places:
-            stages[places[i]]()
-    for stage in stages[max(places.values()) + 1 :]:
-        stage()
+        for job in jobs.get(i, ()):
+            job()
+    for job in rest:
+        job()
 
     @pl.when(has_next)
     def _():
@@ -821,7 +959,7 @@
             hop(i).wait_send()
 
 
-def line_scan(state, coef, count, forward, order, collective_id, *before, gathered=None, summed=()):
+def line_scan(state, coef, count, forward, order, collective_id, *before, gathered=None, summed=(), local=()):
     cuts = 4
     pieces = state.shape[0] * cuts
     scratch = [
@@ -831,101 +969,43 @@
         pltpu.SemaphoreType.DMA((pieces,)),
     ]
     gathers = gathered is not None
+    shapes = [jax.ShapeDtypeStruct(state.shape, BF16)]
     if gathers:
         operands, specs = (gathered,), [ANY]
-        result, spec = gathered_shape(gathered), ANY
+        shapes.append(gathered_shape(gathered))
+        outs = [VMEM, ANY]
         scratch += [
             pltpu.VMEM(gathered.shape, gathered.dtype),
             pltpu.SemaphoreType.DMA((max(len(order), 1),)),
             *GATHER_SCRATCH,
         ]
     else:
-        operands, specs = summed, [VMEM] * 3
-        result, spec = jax.ShapeDtypeStruct(summed[2].shape, BF16), VMEM
+        operands = (*summed, *local)
+        specs = [VMEM] * len(operands)
+        shapes.append(jax.ShapeDtypeStruct(summed[2].shape, BF16))
+        shapes += [jax.ShapeDtypeStruct(local[i].shape, BF16) for i in range(3)]
+        outs = [VMEM] * 5
+        scratch = [pltpu.VMEM(local[i].shape, F32) for i in (1, 2)] + scratch
         scratch += scatter_scratch(summed[2].shape)
     return pl.pallas_call(
         functools.partial(scan_kernel, count, forward, cuts, gathers, order),
-        out_shape=[jax.ShapeDtypeStruct(state.shape, BF16), result],
+        out_shape=shapes,
         in_specs=[VMEM, pl.BlockSpec(memory_space=pltpu.SMEM)] + specs + [ANY] * len(before),
-        out_specs=[VMEM, spec],
+        out_specs=outs,
         scratch_shapes=scratch,
         compiler_params=pltpu.CompilerParams(
             collective_id=collective_id,
             has_side_effects=True,
-            vmem_limit_bytes=48 * 1024 * 1024,
+            vmem_limit_bytes=(16 if gathers else 58) * 1024 * 1024,
         ),
         name="line_scan",
     )(state, coef, *operands, *before)
 
 
-def spread_kernel(line, moves, *refs):
-    weights, gain, out, docs = refs[:4], refs[4], refs[5], refs[6]
-    qkv_mine, gate_mine, out_mine, docs_all, qkv_pack, gate_pack, out_low = refs[-13:-6]
-    scratch = refs[-6:]
-    row, _, other_row, _, _ = plane_ids()
-    targets, stages = owners_stages((qkv_pack, gate_pack), (qkv_mine, gate_mine), *scratch[:3])
-    greet_partner, trade = trade_stages(line, out_low, out_mine, scratch[3])
-    barrier = pltpu.get_barrier_semaphore()
-    for target in targets:
-        pl.semaphore_signal(barrier, inc=1, device_id=target, device_id_type=MESH)
-    greeted = greet_partner(barrier) + len(targets)
-    for i, blocks in enumerate(moves):
-        for j, column, place, size in blocks:
-            block = weights[i][:, column : column + size].astype(BF16).astype(F32) * gain[...]
-            pack = qkv_pack if i < 3 else gate_pack
-            pack[j, :, place : place + size] = block.astype(BF16)
-    pl.semaphore_wait(barrier, greeted)
-    stages[0]()
-    give = pltpu.make_async_remote_copy(
-        src_ref=docs,
-        dst_ref=docs_all.at[row],
-        send_sem=scratch[4].at[0],
-        recv_sem=scratch[4].at[1],
-        device_id={"dpl": other_row},
-        device_id_type=MESH,
-    )
-    keep = pltpu.make_async_copy(docs, docs_all.at[row], scratch[4].at[2])
-    give.start()
-    keep.start()
-    out_low[...] = out[...].astype(BF16)
-    trade[0]()
-    trade[1]()
-    give.wait()
-    keep.wait()
-    stages[1]()
-
-
-def plane_spread(weights, gain, out, docs, line, moves, group, collective_id):
-    rows = gain.shape[0]
-    first = sum(w.shape[1] for w in weights[:3]) // group
-    gate = weights[3].shape[1] // group
-    shapes = [
-        jax.ShapeDtypeStruct((group, rows, first), BF16),
-        jax.ShapeDtypeStruct((group, rows, gate), BF16),
-        jax.ShapeDtypeStruct(out.shape, BF16),
-    ]
-    return pl.pallas_call(
-        functools.partial(spread_kernel, line, moves),
-        out_shape=shapes + [jax.ShapeDtypeStruct((2,) + docs.shape, docs.dtype)],
-        in_specs=[VMEM] * 7,
-        out_specs=[ANY] * 4,
-        scratch_shapes=[pltpu.VMEM(shape.shape, BF16) for shape in shapes]
-        + owners_scratch(2)
-        + list(TRADE_SCRATCH)
-        + [pltpu.SemaphoreType.DMA((3,)), pltpu.SemaphoreType.DMA((1,))],
-        compiler_params=pltpu.CompilerParams(
-            collective_id=collective_id,
-            has_side_effects=True,
-            vmem_limit_bytes=20 * 1024 * 1024,
-        ),
-        name="plane_spread",
-    )(*weights, gain, out, docs)
-
-
 def final_kernel(line, order, moves, grad, grad_out, *refs):
     weights, gain = refs[:3], refs[3]
     outs, out_out, sums, landed, out_landed = refs[-11:-8], refs[-8], refs[-7], refs[-6], refs[-5]
-    targets, stages = owners_stages((grad,), (landed,), *refs[-4:-1])
+    targets, stages = owners_stages((grad,), (blocks_of(landed),), *refs[-4:-1])
     greet_partner, trade = trade_stages(line, grad_out, out_landed, refs[-1])
     barrier = pltpu.get_barrier_semaphore()
     for target in targets:
@@ -1102,13 +1182,41 @@
         )
     ]
     docs = jnp.pad(doc_lengths, ((0, 8 - batch), (0, 128 - doc_lengths.shape[1])))
-    qkv_swapped, gate_swapped, out_moved, docs_all = plane_spread(
-        firsts, gain_one, w_out, docs, line, head_moves, group, 0
-    )
     order = tuple(inner) if chunk % 128 == 0 else ()
     rows_in, rows_cot = inputs, out_cotangent
     if not order:
         rows_in, rows_cot = to_inner(inputs), to_inner(out_cotangent)
+    out_in, down_in, up_in, unit_moves = w_out, w_down, w_up, []
+    if order:
+        moves = [(i * chunk, j * chunk, chunk) for j, i in enumerate(order)]
+        for j in range(group):
+            for q in range(n_dph * n_pb):
+                block = (q // n_pb * n_dpl + j // n_ka) * n_pb + q % n_pb
+                column = (block * n_ka + j % n_ka) * wide_rows
+                unit_moves.append((j, column, q * wide_rows, wide_rows))
+    else:
+        moves = [(i * units, i * units, units) for i in range(width // units)]
+        out_in, down_in = to_inner(w_out), to_inner(w_down)
+        up_in = by_unit((w_up.astype(BF16).astype(F32) * gain_two).astype(BF16))
+    normed_one_all, up_swapped, weight_qkv, gate_out, down_pack, docs_all = open_plane(
+        firsts,
+        gain_one,
+        out_in,
+        docs,
+        rows_in,
+        up_in,
+        down_in,
+        up_bias[None, :],
+        gain_two,
+        line,
+        order,
+        moves,
+        unit_moves,
+        head_moves,
+        units,
+        n_pb,
+        0,
+    )
     head = (
         (at_ka // heads_pb) * (n_dpl * heads_pb) + at_dpl * heads_pb + at_ka % heads_pb
     ).astype(F32)
@@ -1134,34 +1242,6 @@
     coef_forward = jnp.stack([goes_on(edge), jnp.full((n_dpl * batch,), decay_span)])
     coef_backward = jnp.stack([goes_on(edge + span), jnp.full((n_dpl * batch,), decay_span)])
 
-    down_in, up_in, unit_moves = w_down, w_up, []
-    if order:
-        moves = [(i * chunk, j * chunk, chunk) for j, i in enumerate(order)]
-        for j in range(group):
-            for q in range(n_dph * n_pb):
-                block = (q // n_pb * n_dpl + j // n_ka) * n_pb + q % n_pb
-                column = (block * n_ka + j % n_ka) * wide_rows
-                unit_moves.append((j, column, q * wide_rows, wide_rows))
-    else:
-        moves = [(i * units, i * units, units) for i in range(width // units)]
-        out_moved, down_in = to_inner(out_moved), to_inner(w_down)
-        up_in = by_unit((w_up.astype(BF16).astype(F32) * gain_two).astype(BF16))
-    normed_one_all, up_swapped, weight_qkv, gate_out, down_pack = open_plane(
-        rows_in,
-        up_in,
-        qkv_swapped.reshape(group * rows, -1),
-        gate_swapped.reshape(group * rows, -1),
-        out_moved,
-        down_in,
-        up_bias[:, None],
-        gain_two,
-        (group, rows, units),
-        order,
-        moves,
-        unit_moves,
-        n_pb,
-        1,
-    )
     if n_dph > 1:
         weight_qkv = lax.all_gather(weight_qkv, "dph", axis=0, tiled=True)
     blocks = width // units
@@ -1184,24 +1264,26 @@
     retained = retained + decay_in * jnp.einsum(
         "snd,sde->sne", query, carried, preferred_element_type=F32
     )
-    gate_out = after(gate_out, retained).reshape(n_dph * n_pb, -1, units)
-    weight_gate = gate_out[:, : group * rows].reshape(width, units)
-    weight_out = (
-        gate_out[:, group * rows :]
-        .reshape(-1, n_pb // heads_pb, blocks, wide_rows, units)
-        .transpose(1, 0, 3, 2, 4)
-        .reshape(value_width, width)
-    )
-    weight_up = gather_line(after(up_swapped.reshape(group * rows, -1), gate_out))
-    down_pack = gather_line(after(down_pack, gate_out))
-    weight_down = down_pack[:, :width]
-    bias_up = down_pack[:, width].astype(F32)
     normed_ret, inv_ret = normalize(retained)
+    stride = gate_out.shape[0] // (n_dph * n_pb)
+    spread = n_pb // heads_pb
+    out_places = []
+    for q in range(n_dph * n_pb):
+        row = (q % spread * (n_dph * n_pb // spread) + q // spread) * wide_rows
+        for i in range(blocks):
+            source = q * stride + group * rows + i * wide_rows
+            out_places.append((source, row, i * units, wide_rows))
+    cut_out = gate_out.reshape(n_dph * n_pb, stride, units)
+    bias_up = cut_out[:, stride - 16, :wide_rows].reshape(units).astype(F32)
+    weight_up = gather_line(after(up_swapped.reshape(group * rows, -1), gate_out, inv_ret))
+    weight_gate = after(cut_out[:, : group * rows].reshape(width, units), inv_ret)
     gate = mm(normed_one_all, weight_gate)
-    opened = jax.nn.sigmoid(gate)
-    silu = gate * opened
-    gated = (silu * normed_ret).astype(BF16)
-    middle, normed_two_all = plane_mix(gated, weight_out, rows_in, order, 3)
+    gated = (gate * jax.nn.sigmoid(gate) * normed_ret).astype(BF16)
+    weight_down = gather_line(after(down_pack, gated))
+    gate_low = gate.astype(BF16)
+    middle, normed_two_all, weight_out = plane_mix(
+        gated, rows_in, gate_out, out_places, order, 3, value, query, key, scores, decay_in, decay_out
+    )
     up_pre = mm(normed_two_all, weight_up) + bias_up
     bell = 0.5 * (1.0 + lax.erf(up_pre * np.float32(math.sqrt(0.5))))
     active = (up_pre * bell).astype(BF16)
@@ -1220,19 +1302,22 @@
     )
     grad_down = scatter_line(grad_down)
     grad_up = scatter_line(grad_up)
-    grad_gated = after(mm_back(grad_mid_all, weight_out), grad_up, grad_down)
+    grad_gated = after(mm_back(grad_mid_all, weight_out), grad_up)
+    gate_again = gate_low.astype(F32)
+    opened = jax.nn.sigmoid(gate_again)
+    silu = gate_again * opened
     grad_gate = (grad_gated * normed_ret * (opened + silu * (1.0 - opened))).astype(BF16)
     grad_ret = normalize_back(normed_ret, inv_ret, grad_gated * silu).astype(BF16)
     query_in = (query.astype(F32) * decay_in).astype(BF16)
     grad_state = jnp.einsum("snd,sne->sde", query_in, grad_ret, preferred_element_type=F32)
-    grad_out = mm_grad(gated, grad_mid_all).astype(BF16)
+    grad_out = after(mm_grad(gated, grad_mid_all), grad_down).astype(BF16)
     grad_out = (
         grad_out.reshape(n_pb // heads_pb, -1, wide_rows, width)
         .swapaxes(0, 1)
         .reshape(value_width, width)
     )
     grad_gate_w = mm_grad(normed_one_all, grad_gate).astype(BF16)
-    grad_carried, output = line_scan(
+    _, output, *grad_parts = line_scan(
         grad_state,
         coef_backward,
         n_pb,
@@ -1241,38 +1326,29 @@
         7,
         grad_gate_w,
         grad_out,
-        summed=(active, down_pack, middle),
+        summed=(active, weight_down, middle),
+        local=(
+            query,
+            key,
+            value,
+            grad_ret,
+            scores,
+            carried,
+            decay,
+            decay_in,
+            decay_out,
+            *tables_q,
+            *tables_k,
+        ),
     )
     grad_gate_w = scatter_line(grad_gate_w)
     grad_out = scatter_line(grad_out)
-    grad_scores = (
-        jnp.einsum("sne,sme->snm", grad_ret, value, preferred_element_type=F32) * decay
-    ).astype(BF16)
-    grad_query = jnp.einsum("snm,smd->snd", grad_scores, key, preferred_element_type=F32)
-    grad_query = grad_query + decay_in * jnp.einsum(
-        "sne,sde->snd", grad_ret, carried, preferred_element_type=F32
-    )
-    grad_key = jnp.einsum("snm,snd->smd", grad_scores, query, preferred_element_type=F32)
-    grad_key = grad_key + decay_out * jnp.einsum(
-        "sme,sde->smd", value, grad_carried, preferred_element_type=F32
-    )
-    grad_value = jnp.einsum("snm,sne->sme", scores, grad_ret, preferred_element_type=F32)
-    grad_value = grad_value + decay_out * jnp.einsum(
-        "smd,sde->sme", key, grad_carried, preferred_element_type=F32
-    )
-    grad_qkv = jnp.concatenate(
-        [
-            (turn_back(grad_query, tables_q) * scale).astype(BF16),
-            turn_back(grad_key, tables_k).astype(BF16),
-            grad_value.astype(BF16),
-        ],
-        axis=-1,
-    )
+    grad_qkv = jnp.concatenate(grad_parts, axis=-1)
     grad_qkv_w = mm_grad(normed_one_all, after(grad_qkv, grad_gate_w)).astype(BF16)
     grad_qkv_sum = scatter_line(grad_qkv_w)
     cut = (group, rows, -1)
     grad_inputs, shard_gate, shard_up, sums_gate, sums_up, shard_down = plane_last(
-        (grad_qkv, weight_qkv, grad_gate, weight_gate),
+        (*grad_parts, weight_qkv, grad_gate, weight_gate),
         rows_in,
         grad_middle,
         (grad_gate_w.reshape(cut), grad_up.reshape(cut)),
@@ -1285,7 +1361,7 @@
         grad_qkv_w,
     )
     if not order:
-        output, grad_inputs = to_outer(output), to_outer(grad_inputs)
+        output, grad_inputs, shard_down = (to_outer(a) for a in (output, grad_inputs, shard_down))
         shard_up = from_unit(shard_up).astype(F32)
         sums_up = jnp.sum(w_up.astype(BF16).astype(F32) * shard_up, axis=-1, keepdims=True)
         shard_up = gain_two * shard_up
@@ -1302,7 +1378,7 @@
         grad_inputs,
     )
     if not order:
-        shard_out, shard_down = to_outer(shard_out), to_outer(shard_down)
+        shard_out = to_outer(shard_out)
     shard_bias = grad_down[:, width].astype(F32)
     return (
         output,

time: 761 us -> 729 us (0.958)
  other arithmetic: 32.8 us -> 19.3 us
  matrix products: 122 us -> 109 us
  Pallas kernels: 495 us -> 486 us
  waiting for transfers between devices: 27.1 us -> 35.6 us
    dot_general x7 -> x0, matrix products: 16.5 us -> none  [the longest x1 3.61 us: on_device(): jnp.einsum('sne,sme->snm', grad_ret, value, preferred_element_type=F32)]
    reduce_scatter x5, waiting for transfers between devices: 1.06 us -> 10.8 us  [scatter_line(): return lax.psum_scatter(values, LINE, scatter_dimension=0, tiled=True)]
    pallas_call x3 -> x2, Pallas kernels: 185 us -> 176 us  [the longest x1 92.9 us: open_plane(): pl.pallas_call(functools.partial(open_kernel, count, chunks, line, order,...]
    unnamed x138 -> x117, local copies, waits for them, and re-layouts: 44.4 us -> 40.4 us
  transfers between devices with their start and end apart: 8 -> 8, of which waited for: 3 -> 2; matrix products, arithmetic and copies ran while one was open for 15% -> 17% of each run, Pallas kernels for 48% -> 50%
where the time goes in v4:
time: 729 us; the launch traced here: 721 us
  Pallas kernels  486 us (67%)
  matrix products  109 us (15%)
  local copies, waits for them, and re-layouts  51.3 us (7%)
  waiting for transfers between devices  35.6 us (5%)
  other arithmetic  19.3 us (3%)
  between operations  19.2 us (3%)
    pallas_call x2, Pallas kernels, line_scan(): pl.pallas_call(functools.partial(scan_kernel, count, forward, cuts, gathe...  136 us
    pallas_call x1, Pallas kernels, open_plane(): pl.pallas_call(functools.partial(open_kernel, count, chunks, line, order,...  92.9 us
    pallas_call x1, Pallas kernels, plane_mix(): pl.pallas_call(functools.partial(mix_kernel, order, places), out_shape=[j...  82.6 us
    pallas_call x1, Pallas kernels, plane_turn(): pl.pallas_call(functools.partial(turn_kernel, order), out_shape=[jax.Shap...  81.7 us
    pallas_call x1, Pallas kernels, plane_last(): pl.pallas_call(functools.partial(last_kernel, order, moves), out_shape=[j...  62.7 us
    dot_general x6, matrix products, mm_grad(): return jnp.einsum('sti,sto->io', left, right, preferred_element_type=F32)  47.8 us
    unnamed x117, local copies, waits for them, and re-layouts  40.4 us
    dot_general x3, matrix products, mm(): return jnp.einsum('sti,io->sto', left, right, preferred_element_type=F32)  33.3 us
  transfers between devices with their start and end apart: 8, of which 2 were waited for; matrix products, arithmetic and copies ran while one was open for 17% of the time, Pallas kernels for 50%

profile of v4, /device:TPU:2, one launch (start us, length us, event | category | flops | bytes accessed | tf_op | source)
XLA Modules:
  0.0 721.0 jit_solution(12206191799020244459)
XLA Ops:
  9.4 1.2 copy-done.1
  10.7 1.2 copy-done.6
  11.9 1.2 copy-done.7
  13.1 1.2 copy-done.11
  16.4 1.2 copy-done.23
  17.6 1.2 copy-done.24
  19.5 92.9 %open_plane.1 = (bf16[4,512,2048]{2,1,0:T(8,128)(2,1)S(1)}, bf16[8,64,512]{2,1,0:T(8,128)(2,1)S(1)}, bf16[2048,1024]{1,0:T(8,128)(2,1)S(1)}, bf16[1040,512]{1,0:...) custom-call(f32[64,2048]{1,0:T(8,128)S(1)} %copy-done.19, f32[64,2048]{1,0:T(8,128)S(1)} %copy-done.21, ...), custom_call_target="tpu_custom_call" | custom-call | tf_op jit(solution)/shard_map/open_plane/pallas_call | solution.py:418
  112.4 1.9 copy-done.13
  114.4 3.3 copy-done.31
  119.4 12.8 %fusion.14 = f32[4,512,1024]{2,1,0:T(8,128)S(1)} fusion(bf16[4,512,2048]{2,1,0:T(8,128)(2,1)} %copy-done.31, bf16[2048,1024]{1,0:T(8,128)(2,1)} %copy-done.13), kind=kOutput, calls=%fused_computation.24 | convolution fusion | flops 8589934592 | bytes 20971520 | tf_op jit(solution)/shard_map/sti,io->sto/dot_general | solution.py:1087
  134.9 51.1 %line_scan.2 = (bf16[4,256,512]{2,1,0:T(8,128)(2,1)S(1)}, bf16[4,512,2048]{2,1,0:T(8,128)(2,1)S(1)}) custom-call(f32[4,256,512]{2,1,0:T(8,128)S(1)} %fusion.25.state, f32[2,4]{1,0:T(2,128)S(1)} %stack.8.coef, bf16[2,128,2048]{2,1,0:T(8,128)(2,1)S(1)} %copy-done.9), custom_call_target="tpu_custom_call" | custom-call | tf_op jit(solution)/shard_map/line_scan/pallas_call | solution.py:990
  188.2 1.4 copy-done.32
  189.6 1.3 fusion.42
  191.9 2.1 copy-done.33
  196.0 24.7 %all-gather.4.cloned.1.call-done.gate_out = bf16[4160,512]{1,0:T(8,128)(2,1)} async-done(((bf16[1040,512]{1,0:T(8,128)(2,1)}), bf16[4160,512]{1,0:T(8,128)(2,1)}) %all-gather.4.cloned.1.call-update) | async-done | bytes 4259856 | tf_op jit(solution)/shard_map/all_gather | solution.py:1160
  220.7 1.2 slice.76
  223.4 1.9 slice_add_fusion
  226.2 8.6 %multiply_convert_fusion.3 = (bf16[4,512,512]{2,1,0:T(8,128)(2,1)S(1)}, bf16[4,512,512]{2,1,0:T(8,128)(2,1)}) fusion(f32[4,512,512]{2,1,0:T(8,128)S(1)} %copy-done.34, f32[4,512]{1,0:T(4,128)S(1)} %get-tuple-element.81, f32[4,512]{1,0:T(4,128)S(1)} %broadcast_multiply_fusion.2, bf16[4,512,2048]{2,1,0:T(8,128)(2,1)} %copy-done.31, ...), kind=kOutput, calls=%fused_computation.31 | convolution fusion | flops 4304404480 | bytes 18890752 | tf_op jit(solution)/shard_map/sti,io->sto/dot_general | solution.py:1087
  237.3 3.8 slice.94.refs_0_.refs_5_
  241.2 1.4 pad_maximum_fusion.1.refs_2_.refs_4_
  242.7 82.6 %plane_mix.1 = (f32[2,128,2048]{2,1,0:T(8,128)S(1)}, bf16[4,512,2048]{2,1,0:T(8,128)(2,1)}, bf16[512,2048]{1,0:T(8,128)(2,1)}) custom-call(bf16[4,512,512]{2,1,0:T(8,128)(2,1)} %copy-done.45, bf16[2,128,2048]{2,1,0:T(8,128)(2,1)S(1)} %copy-done.2, bf16[4160,512]{1,0:T(8,128)(2,1)} %all-gather.4.cloned.1.call-done.gate_out, ...), custom_call_target="tpu_custom_call" | custom-call | tf_op jit(solution)/shard_map/plane_mix/pallas_call | solution.py:686
  325.4 1.3 copy-done.4
  327.4 11.9 %multiply_convert_fusion.2 = (bf16[4,512,512]{2,1,0:T(8,128)(2,1)}, f32[4,512,512]{2,1,0:T(8,128)}) fusion(f32[512]{0:T(512)S(1)} %bitcast.93, bf16[4,512,2048]{2,1,0:T(8,128)(2,1)} %get-tuple-element.47, bf16[2048,512]{1,0:T(8,128)(2,1)} %all-gather.8.cloned.1.call-done.weight), kind=kOutput, calls=%fused_computation.29 | convolution fusion | flops 4301258752 | bytes 16779264 | tf_op jit(solution)/shard_map/sti,io->sto/dot_general | solution.py:1087
  339.2 9.6 %fusion.8.grad = bf16[4,512,512]{2,1,0:T(8,128)(2,1)S(1)} fusion(f32[4,512,512]{2,1,0:T(8,128)} %get-tuple-element.93, bf16[4,512,2048]{2,1,0:T(8,128)(2,1)} %copy-done.32, bf16[512,2048]{1,0:T(8,128)(2,1)} %all-gather.6.cloned.1.call-done.refs_1_, f32[512]{0:T(512)S(1)} %bitcast.94), kind=kOutput, calls=%fused_computation.12 | convolution fusion | flops 4306501632 | bytes 16779264 | tf_op jit(solution)/shard_map/sto,io->sti/dot_general | solution.py:1091
  348.8 5.7 bitcast_convert_fusion.2.refs_1_
  355.8 8.6 %bitcast_convert_fusion.3 = bf16[512,2048]{1,0:T(8,128)(2,1)S(1)} fusion(bf16[4,512,512]{2,1,0:T(8,128)(2,1)} %get-tuple-element.92.refs_0_, bf16[4,512,2048]{2,1,0:T(8,128)(2,1)} %copy-done.32), kind=kOutput, calls=%fused_computation.23 | convolution fusion | flops 4296015872 | bytes 12582912 | tf_op jit(solution)/shard_map/sti,sto->io/dot_general | solution.py:1095
  364.4 1.6 pad_maximum_fusion.refs_0_
  366.1 1.6 copy-done.18
  367.6 81.7 %plane_turn.1 = (f32[2,128,2048]{2,1,0:T(8,128)S(1)}, bf16[4,512,2048]{2,1,0:T(8,128)(2,1)}) custom-call(bf16[4,512,512]{2,1,0:T(8,128)(2,1)S(1)} %copy-done.18, bf16[2048,512]{1,0:T(8,128)(2,1)} %all-gather.8.cloned.1.call-done.weight, f32[2,128,2048]{2,1,0:T(8,128)} %copy-done.4, bf16[2,128,2048]{2,1,0:T(8,128)(2,1)S(1)} %copy-done.10, ...), custom_call_target="tpu_custom_call" | custom-call | tf_op jit(solution)/shard_map/plane_turn/pallas_call | solution.py:733
  449.4 1.4 copy-done.16
  450.7 1.2 slice.78
  452.6 12.2 %fusion.39 = (f32[4,512]{1,0:T(4,128)S(1)}, f32[4,512]{1,0:T(4,128)S(1)}, f32[4,512,512]{2,1,0:T(8,128)}, bf16[4,512,512]{2,1,0:T(8,128)(2,1)S(1)}) fusion(f32[4,512]{1,0:T(4,128)S(1)} %get-tuple-element.81, f32[4,512,512]{2,1,0:T(8,128)} %copy-done.33, f32[4,512]{1,0:T(4,128)S(1)} %broadcast_multiply_fusion.2, bf16[4,512,512]{2,1,0:T(8,128)(2,1)} %get-tuple-element.91, ...), kind=kOutput, calls=%fused_computation.99 | convolution fusion | flops 4313837568 | bytes 23101444 | tf_op jit(solution)/shard_map/sto,io->sti/dot_general | solution.py:1091
  464.7 1.3 copy-done.47
  466.1 9.6 %bitcast_convert_fusion.1.refs_16_ = bf16[2048,512]{1,0:T(8,128)(2,1)} fusion(bf16[4,512,2048]{2,1,0:T(8,128)(2,1)} %copy-done.31, bf16[4,512,512]{2,1,0:T(8,128)(2,1)S(1)} %get-tuple-element.73.refs_4_), kind=kOutput, calls=%fused_computation.21 | convolution fusion | flops 4296015872 | bytes 12582912 | tf_op jit(solution)/shard_map/sti,sto->io/dot_general | solution.py:1095
  475.8 1.1 slice.79
  477.6 9.1 %fusion.13.refs_17_ = bf16[512,2048]{1,0:T(8,128)(2,1)} fusion(bf16[4,512,512]{2,1,0:T(8,128)(2,1)S(1)} %copy-done.46, bf16[4,512,2048]{2,1,0:T(8,128)(2,1)} %get-tuple-element.50, f32[]{:T(128)} %bitcast.25), kind=kOutput, calls=%fused_computation.20 | convolution fusion | flops 4297064448 | bytes 12582916 | tf_op jit(solution)/shard_map/sti,sto->io/dot_general | solution.py:1095
  487.3 4.1 multiply_convert_fusion.1.refs_6_
  491.5 2.2 fusion.24.state
  493.7 85.0 %line_scan.3 = (bf16[4,256,512]{2,1,0:T(8,128)(2,1)}, bf16[2,128,2048]{2,1,0:T(8,128)(2,1)}, bf16[4,512,256]{2,1,0:T(8,128)(2,1)}, bf16[4,512,256]{2,1,0:T(8,128)(2,1)}, bf16[4,512,512]{2,1,0:T(8,128)(2,1)}) custom-call(f32[4,256,512]{2,1,0:T(8,128)} %fusion.24.state, f32[2,4]{1,0:T(2,128)} %stack.9.coef, bf16[4,512,512]{2,1,0:T(8,128)(2,1)} %get-tuple-element.92.refs_0_, ...), custom_call_target="tpu_custom_call" | custom-call | tf_op jit(solution)/shard_map/line_scan/pallas_call | solution.py:990
  580.5 14.1 %bitcast_convert_fusion.refs_15_ = bf16[2048,1024]{1,0:T(8,128)(2,1)} fusion(bf16[4,512,2048]{2,1,0:T(8,128)(2,1)} %copy-done.31, bf16[4,512,512]{2,1,0:T(8,128)(2,1)} %get-tuple-element.55.refs_2_, bf16[4,512,256]{2,1,0:T(8,128)(2,1)} %get-tuple-element.54.refs_1_, bf16[4,512,256]{2,1,0:T(8,128)(2,1)} %get-tuple-element.53.refs_0_, bf16[]{:T(256)} %bitcast.30), kind=kOutput, calls=%fused_computation | convolution fusion | flops 8608808960 | bytes 16777218 | tf_op jit(solution)/shard_map/sti,sto->io/dot_general | solution.py:1095
  594.6 1.4 convert_reduce_fusion
  596.0 62.7 %plane_last.1 = (f32[2,128,2048]{2,1,0:T(8,128)}, f32[64,4096]{1,0:T(8,128)}, f32[64,4096]{1,0:T(8,128)}, f32[64,1]{1,0:T(8,128)}, f32[64,1]{1,0:T(8,128)}, /*index=5*/f32[128,2048]{1,0:T(8,128)}) custom-call(bf16[4,512,256]{2,1,0:T(8,128)(2,1)} %get-tuple-element.53.refs_0_, bf16[4,512,256]{2,1,0:T(8,128)(2,1)} %get-tuple-element.54.refs_1_, ...), custom_call_target="tpu_custom_call" | custom-call | tf_op jit(solution)/shard_map/plane_last/pallas_call | solution.py:804
  658.8 1.4 reduce.1
  660.2 10.8 %reduce-scatter.12.cloned.1.call-done = bf16[512,1024]{1,0:T(8,128)(2,1)} async-done(((bf16[2048,1024]{1,0:T(8,128)(2,1)}), bf16[512,1024]{1,0:T(8,128)(2,1)}) %reduce-scatter.12.cloned.1.call-update) | async-done | bytes 1048592 | tf_op jit(solution)/shard_map/reduce_scatter | solution.py:1163
  671.0 1.6 copy-done.5
  672.6 1.2 copy-done.25
  674.8 29.7 %plane_final.1 = (f32[64,2048]{1,0:T(8,128)S(1)}, f32[64,2048]{1,0:T(8,128)S(1)}, f32[64,4096]{1,0:T(8,128)S(1)}, f32[128,2048]{1,0:T(8,128)S(1)}, f32[64,1]{1,0:T(8,128)S(1)}) custom-call(bf16[8,64,1024]{2,1,0:T(8,128)(2,1)S(1)} %bitcast.83, bf16[128,2048]{1,0:T(8,128)(2,1)S(1)} %copy-done.28, f32[64,2048]{1,0:T(8,128)S(1)} %copy-done.20, ...), custom_call_target="tpu_custom_call" | custom-call | tf_op jit(solution)/shard_map/plane_final/pallas_call | solution.py:1029
  706.1 1.3 copy.119
  (160 shorter events, 30.2 us)
Async XLA Ops:
  7.2 213.5 %all-gather.4.cloned.1.call-start = ((), (), s32[]{:S(2)}) async-start(), calls=%async_computation.5 | async-start | bytes 5324800 | tf_op jit(solution)/shard_map/all_gather | solution.py:1160
  8.6 109.1 %copy-start.26 = (f32[64,1]{1,0:T(8,128)}, f32[64,1]{1,0:T(8,128)S(1)}, u32[]{:S(2)}) copy-start(f32[64,1]{1,0:T(8,128)S(1)} %copy.68.refs_4_.refs_12_.refs_3_) | copy-start | bytes 772
  8.7 109.0 %copy-start.29 = (f32[64,1]{1,0:T(8,128)}, f32[64,1]{1,0:T(8,128)S(1)}, u32[]{:S(2)}) copy-start(f32[64,1]{1,0:T(8,128)S(1)} %copy.69.refs_11_.refs_13_) | copy-start | bytes 772
  112.4 2.0 copy-start.13
  114.4 3.3 copy-start.31
  117.7 209.7 %all-gather.8.cloned.1.call-start = ((), (), s32[]{:S(2)}) async-start(), calls=%async_computation.7 | async-start | bytes 2621440 | tf_op jit(solution)/shard_map/all_gather | solution.py:1160
  119.4 12.9 %copy-start.41 = (f32[512,128]{1,0:T(8,128)}, f32[512,128]{1,0:T(8,128)S(1)}, u32[]{:S(2)}) copy-start(f32[512,128]{1,0:T(8,128)S(1)} %get-tuple-element.82.refs_14_) | copy-start | bytes 786436
  119.4 12.9 %copy-start.42 = (f32[512,128]{1,0:T(8,128)}, f32[512,128]{1,0:T(8,128)S(1)}, u32[]{:S(2)}) copy-start(f32[512,128]{1,0:T(8,128)S(1)} %get-tuple-element.83.refs_15_) | copy-start | bytes 786436
  119.4 12.9 %copy-start.43 = (f32[512,128]{1,0:T(8,128)}, f32[512,128]{1,0:T(8,128)S(1)}, u32[]{:S(2)}) copy-start(f32[512,128]{1,0:T(8,128)S(1)} %get-tuple-element.86.refs_13_) | copy-start | bytes 786436
  119.4 12.9 %copy-start.44 = (f32[512,128]{1,0:T(8,128)}, f32[512,128]{1,0:T(8,128)S(1)}, u32[]{:S(2)}) copy-start(f32[512,128]{1,0:T(8,128)S(1)} %get-tuple-element.87.refs_12_) | copy-start | bytes 786436
  132.3 55.9 %copy-start.36 = (f32[4,512,1024]{2,1,0:T(8,128)}, f32[4,512,1024]{2,1,0:T(8,128)S(1)}, u32[]{:S(2)}) copy-start(f32[4,512,1024]{2,1,0:T(8,128)S(1)} %fusion.14) | copy-start | bytes 25165828
  132.9 53.5 %copy-start.40 = (bf16[4,512,128]{2,1,0:T(8,128)(2,1)}, bf16[4,512,128]{2,1,0:T(8,128)(2,1)S(1)}, u32[]{:S(2)}) copy-start(bf16[4,512,128]{2,1,0:T(8,128)(2,1)S(1)} %get-tuple-element.75) | copy-start | bytes 1572868
  132.9 2.0 copy-start.9
  186.0 3.6 copy-start.32
  186.0 5.1 copy-start.8
  187.4 304.1 %copy-start = (bf16[4,512,256]{2,1,0:T(8,128)(2,1)}, bf16[4,512,256]{2,1,0:T(8,128)(2,1)S(1)}, u32[]{:S(2)}) copy-start(bf16[4,512,256]{2,1,0:T(8,128)(2,1)S(1)} %fusion.16.refs_1_.refs_3_) | copy-start | bytes 3145732
  189.6 1.5 copy-start.35
  191.9 2.1 copy-start.33
  223.4 115.8 %all-gather.6.cloned.1.call-start = ((), (), s32[]{:S(2)}) async-start(), calls=%async_computation.6 | async-start | bytes 2621440 | tf_op jit(solution)/shard_map/all_gather | solution.py:1160
  223.4 2.8 copy-start.34
  225.3 9.6 %copy-start.39 = (bf16[4,512,512]{2,1,0:T(8,128)(2,1)}, bf16[4,512,512]{2,1,0:T(8,128)(2,1)S(1)}, u32[]{:S(2)}) copy-start(bf16[4,512,512]{2,1,0:T(8,128)(2,1)S(1)} %slice_add_fusion) | copy-start | bytes 6291460
  234.9 1.3 copy-start.45
  236.2 6.4 copy-start.2
  237.1 213.7 %reduce-scatter.6.cloned.1.call-start = ((), (), s32[]{:S(2)}) async-start(), calls=%async_computation.8 | async-start | bytes 2621440 | tf_op jit(solution)/shard_map/reduce_scatter | solution.py:1163
  241.2 84.1 %copy-start.14 = (f32[512,1]{1,0:T(8,128)}, f32[512,1]{1,0:T(8,128)S(1)}, u32[]{:S(2)}) copy-start(f32[512,1]{1,0:T(8,128)S(1)} %get-tuple-element.98.refs_5_.refs_11_) | copy-start | bytes 6148
  241.2 84.1 %copy-start.15 = (f32[512,1]{1,0:T(8,128)}, f32[512,1]{1,0:T(8,128)S(1)}, u32[]{:S(2)}) copy-start(f32[512,1]{1,0:T(8,128)S(1)} %get-tuple-element.99.refs_4_.refs_10_) | copy-start | bytes 6148
  242.6 82.7 %copy-start.3 = (bf16[4,512,256]{2,1,0:T(8,128)(2,1)}, bf16[4,512,256]{2,1,0:T(8,128)(2,1)S(1)}, u32[]{:S(2)}) copy-start(bf16[4,512,256]{2,1,0:T(8,128)(2,1)S(1)} %pad_maximum_fusion.1.refs_2_.refs_4_) | copy-start | bytes 3145732
  339.2 9.6 %copy-start.53 = (bf16[4,512,2048]{2,1,0:T(8,128)(2,1)S(1)}, bf16[4,512,2048]{2,1,0:T(8,128)(2,1)}, u32[]{:S(2)}) copy-start(bf16[4,512,2048]{2,1,0:T(8,128)(2,1)} %get-tuple-element.47) | copy-start | bytes 25165828
  348.8 6.2 copy-start.17
  354.6 121.2 %reduce-scatter.8.cloned.1.call-start = ((), (), s32[]{:S(2)}) async-start(), calls=%async_computation.9 | async-start | bytes 2785280 | tf_op jit(solution)/shard_map/reduce_scatter | solution.py:1163
  364.4 1.7 copy-start.10
  366.0 212.8 %reduce-scatter.10.cloned.1.call-start = ((), (), s32[]{:S(2)}) async-start(), calls=%async_computation.10 | async-start | bytes 2621440 | tf_op jit(solution)/shard_map/reduce_scatter | solution.py:1163
  366.1 1.6 copy-start.18
  449.4 1.4 copy-start.16
  466.1 11.5 %copy-start.46 = (bf16[4,512,512]{2,1,0:T(8,128)(2,1)S(1)}, bf16[4,512,512]{2,1,0:T(8,128)(2,1)}, u32[]{:S(2)}) copy-start(bf16[4,512,512]{2,1,0:T(8,128)(2,1)} %copy-done.45) | copy-start | bytes 6291460
  475.7 184.5 %reduce-scatter.14.cloned.1.call-start = ((), (), s32[]{:S(2)}) async-start(), calls=%async_computation.12 | async-start | bytes 2621440 | tf_op jit(solution)/shard_map/reduce_scatter | solution.py:1163
  486.7 184.2 %reduce-scatter.12.cloned.1.call-start = ((), (), s32[]{:S(2)}) async-start(), calls=%async_computation.11 | async-start | bytes 5242880 | tf_op jit(solution)/shard_map/reduce_scatter | solution.py:1163
  491.5 2.2 copy-start.37
  596.0 74.9 %copy-start.12 = (f32[64,4096]{1,0:T(8,128)S(1)}, f32[64,4096]{1,0:T(8,128)}, u32[]{:S(2)}) copy-start(f32[64,4096]{1,0:T(8,128)} %refs_2_.3) | copy-start | bytes 3145732
  596.0 74.9 %copy-start.20 = (f32[64,2048]{1,0:T(8,128)S(1)}, f32[64,2048]{1,0:T(8,128)}, u32[]{:S(2)}) copy-start(f32[64,2048]{1,0:T(8,128)} %refs_0_.5) | copy-start | bytes 1572868
  596.0 74.9 %copy-start.22 = (f32[64,2048]{1,0:T(8,128)S(1)}, f32[64,2048]{1,0:T(8,128)}, u32[]{:S(2)}) copy-start(f32[64,2048]{1,0:T(8,128)} %refs_1_.3) | copy-start | bytes 1572868
  596.0 74.9 %copy-start.27 = (f32[64,1]{1,0:T(8,128)S(1)}, f32[64,1]{1,0:T(8,128)}, u32[]{:S(2)}) copy-start(f32[64,1]{1,0:T(8,128)} %copy-done.26) | copy-start | bytes 772
  596.0 109.1 %copy-start.48 = (bf16[2,128,2048]{2,1,0:T(8,128)(2,1)S(1)}, bf16[2,128,2048]{2,1,0:T(8,128)(2,1)}, u32[]{:S(2)}) copy-start(bf16[2,128,2048]{2,1,0:T(8,128)(2,1)} %get-tuple-element.114) | copy-start | bytes 3145732
  658.8 45.7 %copy-start.52 = (f32[64,1]{1,0:T(8,128)S(1)}, f32[64,1]{1,0:T(8,128)}, u32[]{:S(2)}) copy-start(f32[64,1]{1,0:T(8,128)} %get-tuple-element.59) | copy-start | bytes 772
  671.0 1.6 copy-start.5
  706.1 3.9 copy-start.51
  707.4 4.5 copy-start.50
  709.0 3.9 copy-start.49
  (14 other events, 16.2 us)
Sparse Core Ops, SparseCore 0:
  117.8 102.8 all-gather.3
  223.5 56.8 all-gather.7
  282.5 44.6 all-gather.5
  354.7 54.7 reduce-scatter.5
  411.7 45.3 reduce-scatter.7
  475.8 67.2 reduce-scatter.9
  545.4 48.2 reduce-scatter.13
  596.1 74.8 reduce-scatter.11

commit v5 on v4

--- a/solution.py
+++ b/solution.py
@@ -183,7 +183,23 @@
         for copy in copies:
             copy.wait()
 
-    return [{"dpl": r, "ka": c} for r, c in peers], (begin, end)
+    def arrive(r, c, across_rows):
+        away = lax.rem(col - c + 4, 4)
+        pltpu.make_async_remote_copy(
+            src_ref=sources[0].at[me],
+            dst_ref=targets[0](r * 4 + c),
+            send_sem=send_sem.at[0, 0],
+            recv_sem=recv_sem.at[0, away + 3 if across_rows else away - 1],
+            device_id={"dpl": other_row, "ka": col},
+            device_id_type=MESH,
+        ).wait_recv()
+
+    def leave():
+        for copy in copies[1:]:
+            copy.wait_send()
+
+    near = (copies[0].wait, arrive, leave) if len(sources) == 1 else None
+    return [{"dpl": r, "ka": c} for r, c in peers], (begin, end, near)
 
 
 def blocks_of(ref):
@@ -362,9 +378,22 @@
     keep.start()
     out_low[...] = out[...].astype(BF16)
     trade[0]()
-    first[1]()
-    for c in range(chunks):
-        step(0, c)
+    _, col, _, across, sibling = plane_ids()
+    across_s = lax.rem(sibling + 2, 4)
+    kept, arrive, leave = first[2]
+    kept()
+    arrive(row, sibling, False)
+    nearest = [row * 2 + col // 2]
+    step(0, nearest[0])
+    for r, c, d, far in (
+        (row, across, across_s, False),
+        (other_row, col, sibling, True),
+        (other_row, across, across_s, True),
+    ):
+        arrive(r, c, far)
+        arrive(r, d, far)
+        nearest.append(r * 2 + c // 2)
+        step(0, nearest[-1])
     normalize_rows(x, normed, order)
     gather[0]()
     pack(3, gate_pack)
@@ -389,14 +418,15 @@
     copies = [pltpu.make_async_copy(a, b, sems[13].at[i]) for i, (a, b) in enumerate(pairs)]
     for copy in copies:
         copy.start()
-    for c in range(chunks):
+    for c in nearest:
         step(1, c)
     gather[1]()
     for distance in range(2, count):
-        for c in range(chunks):
+        for i, c in enumerate(nearest):
             step(distance, c)
-            if distance == 2 and c == chunks // 2:
+            if distance == 2 and i == chunks // 2:
                 gather[2]()
+    leave()
     give.wait()
     keep.wait()
     for copy in copies:
@@ -785,7 +815,7 @@
     for j, i in enumerate(order or (0,)):
         block = grad_down[:, j * size : (j + 1) * size]
         outs[5][:, i * size : (i + 1) * size] = block.astype(F32)
-    for stage in stages[9:] + owners[1:]:
+    for stage in stages[9:] + owners[1:2]:
         stage()
     for i in (0, 1):
         if moves[i]:
@@ -1256,7 +1286,7 @@
     key_out = (key.astype(F32) * decay_out).astype(BF16)
     state = jnp.einsum("smd,sme->sde", key_out, value, preferred_element_type=F32)
     carried, cot_all = line_scan(
-        state, coef_forward, n_pb, True, order, 2, gathered=rows_cot
+        state, coef_forward, n_pb, True, order, 2, value, query, key, gathered=rows_cot
     )
     raw = jnp.einsum("snd,smd->snm", query, key, preferred_element_type=F32)
     scores = (raw * decay).astype(BF16)
@@ -1282,7 +1312,7 @@
     weight_down = gather_line(after(down_pack, gated))
     gate_low = gate.astype(BF16)
     middle, normed_two_all, weight_out = plane_mix(
-        gated, rows_in, gate_out, out_places, order, 3, value, query, key, scores, decay_in, decay_out
+        gated, rows_in, gate_out, out_places, order, 3, scores, decay_in, decay_out
     )
     up_pre = mm(normed_two_all, weight_up) + bias_up
     bell = 0.5 * (1.0 + lax.erf(up_pre * np.float32(math.sqrt(0.5))))

time: 729 us -> 719 us (0.986)
  Pallas kernels: 486 us -> 478 us
  transfers between devices with their start and end apart: 8 -> 8, of which waited for: 2 -> 2; matrix products, arithmetic and copies ran while one was open for 17% -> 16% of each run, Pallas kernels for 50% -> 51%
where the time goes in v5:
time: 719 us; the launch traced here: 711 us
  Pallas kernels  478 us (66%)
  matrix products  109 us (15%)
  local copies, waits for them, and re-layouts  50.4 us (7%)
  waiting for transfers between devices  36.3 us (5%)
  between operations  19 us (3%)
  other arithmetic  18.1 us (3%)
    pallas_call x2, Pallas kernels, line_scan(): pl.pallas_call(functools.partial(scan_kernel, count, forward, cuts, gathe...  135 us
    pallas_call x1, Pallas kernels, open_plane(): pl.pallas_call(functools.partial(open_kernel, count, chunks, line, order,...  87.3 us
    pallas_call x1, Pallas kernels, plane_turn(): pl.pallas_call(functools.partial(turn_kernel, order), out_shape=[jax.Shap...  81.7 us
    pallas_call x1, Pallas kernels, plane_mix(): pl.pallas_call(functools.partial(mix_kernel, order, places), out_shape=[j...  81.2 us
    pallas_call x1, Pallas kernels, plane_last(): pl.pallas_call(functools.partial(last_kernel, order, moves), out_shape=[j...  62.7 us
    dot_general x6, matrix products, mm_grad(): return jnp.einsum('sti,sto->io', left, right, preferred_element_type=F32)  47.8 us
    unnamed x117, local copies, waits for them, and re-layouts  43 us
    dot_general x3, matrix products, mm(): return jnp.einsum('sti,io->sto', left, right, preferred_element_type=F32)  33 us
  transfers between devices with their start and end apart: 8, of which 2 were waited for; matrix products, arithmetic and copies ran while one was open for 16% of the time, Pallas kernels for 51%

profile of v5, /device:TPU:2, one launch (start us, length us, event | category | flops | bytes accessed | tf_op | source)
XLA Modules:
  0.0 710.8 jit_solution(9276925018695867239)
XLA Ops:
  9.4 1.2 copy-done.2
  10.7 1.2 copy-done.7
  11.9 1.2 copy-done.8
  13.1 1.2 copy-done.12
  16.4 1.2 copy-done.24
  17.6 1.2 copy-done.25
  19.5 87.3 %open_plane.1 = (bf16[4,512,2048]{2,1,0:T(8,128)(2,1)S(1)}, bf16[8,64,512]{2,1,0:T(8,128)(2,1)S(1)}, bf16[2048,1024]{1,0:T(8,128)(2,1)S(1)}, bf16[1040,512]{1,0:...) custom-call(f32[64,2048]{1,0:T(8,128)S(1)} %copy-done.20, f32[64,2048]{1,0:T(8,128)S(1)} %copy-done.22, ...), custom_call_target="tpu_custom_call" | custom-call | tf_op jit(solution)/shard_map/open_plane/pallas_call | solution.py:448
  106.8 1.9 copy-done.14
  108.8 3.3 copy-done.32
  112.5 12.5 %fusion.14 = f32[4,512,1024]{2,1,0:T(8,128)S(1)} fusion(bf16[4,512,2048]{2,1,0:T(8,128)(2,1)} %copy-done.32, bf16[2048,1024]{1,0:T(8,128)(2,1)} %copy-done.14), kind=kOutput, calls=%fused_computation.24 | convolution fusion | flops 8589934592 | bytes 20971520 | tf_op jit(solution)/shard_map/sti,io->sto/dot_general | solution.py:1117
  129.8 50.7 %line_scan.2 = (bf16[4,256,512]{2,1,0:T(8,128)(2,1)S(1)}, bf16[4,512,2048]{2,1,0:T(8,128)(2,1)S(1)}) custom-call(f32[4,256,512]{2,1,0:T(8,128)S(1)} %fusion.25.state, f32[2,4]{1,0:T(2,128)S(1)} %stack.8.coef, bf16[2,128,2048]{2,1,0:T(8,128)(2,1)S(1)} %copy-done.10, bf16[4,512,512]{2,1,0:T(8,128)(2,1)S(1)} %slice.94.refs_1_.refs_5_, ...), custom_call_target="tpu_custom_call" | custom-call | tf_op jit(solution)/shard_map/line_scan/pallas_call | solution.py:1020
  181.6 1.3 fusion.42
  182.8 1.9 copy-done.33
  186.1 2.1 copy-done.35
  190.1 25.1 %all-gather.4.cloned.1.call-done.gate_out = bf16[4160,512]{1,0:T(8,128)(2,1)} async-done(((bf16[1040,512]{1,0:T(8,128)(2,1)}), bf16[4160,512]{1,0:T(8,128)(2,1)}) %all-gather.4.cloned.1.call-update) | async-done | bytes 4259856 | tf_op jit(solution)/shard_map/all_gather | solution.py:1190
  215.2 1.2 slice.76
  218.0 1.9 slice_add_fusion
  220.8 8.7 %multiply_convert_fusion.3 = (bf16[4,512,512]{2,1,0:T(8,128)(2,1)S(1)}, bf16[4,512,512]{2,1,0:T(8,128)(2,1)}) fusion(f32[4,512,512]{2,1,0:T(8,128)S(1)} %copy-done.36, f32[4,512]{1,0:T(4,128)S(1)} %get-tuple-element.81, f32[4,512]{1,0:T(4,128)S(1)} %broadcast_multiply_fusion.2, bf16[4,512,2048]{2,1,0:T(8,128)(2,1)} %copy-done.32, ...), kind=kOutput, calls=%fused_computation.31 | convolution fusion | flops 4304404480 | bytes 18890752 | tf_op jit(solution)/shard_map/sti,io->sto/dot_general | solution.py:1117
  229.6 1.3 copy-done.46
  233.3 81.2 %plane_mix.1 = (f32[2,128,2048]{2,1,0:T(8,128)S(1)}, bf16[4,512,2048]{2,1,0:T(8,128)(2,1)}, bf16[512,2048]{1,0:T(8,128)(2,1)S(1)}) custom-call(bf16[4,512,512]{2,1,0:T(8,128)(2,1)} %copy-done.46, bf16[2,128,2048]{2,1,0:T(8,128)(2,1)S(1)} %copy-done.3, bf16[4160,512]{1,0:T(8,128)(2,1)} %all-gather.4.cloned.1.call-done.gate_out, ...), custom_call_target="tpu_custom_call" | custom-call | tf_op jit(solution)/shard_map/plane_mix/pallas_call | solution.py:716
  314.5 1.3 copy-done.5
  315.8 1.3 copy-done.34
  317.8 11.8 %multiply_convert_fusion.2 = (bf16[4,512,512]{2,1,0:T(8,128)(2,1)}, f32[4,512,512]{2,1,0:T(8,128)}) fusion(f32[512]{0:T(512)S(1)} %bitcast.93, bf16[4,512,2048]{2,1,0:T(8,128)(2,1)} %get-tuple-element.47, bf16[2048,512]{1,0:T(8,128)(2,1)} %all-gather.8.cloned.1.call-done.weight), kind=kOutput, calls=%fused_computation.29 | convolution fusion | flops 4301258752 | bytes 16779264 | tf_op jit(solution)/shard_map/sti,io->sto/dot_general | solution.py:1117
  329.7 9.6 %fusion.8.grad = bf16[4,512,512]{2,1,0:T(8,128)(2,1)S(1)} fusion(f32[4,512,512]{2,1,0:T(8,128)} %get-tuple-element.93, bf16[4,512,2048]{2,1,0:T(8,128)(2,1)} %copy-done.33, bf16[512,2048]{1,0:T(8,128)(2,1)} %all-gather.6.cloned.1.call-done.refs_1_, f32[512]{0:T(512)S(1)} %bitcast.94), kind=kOutput, calls=%fused_computation.12 | convolution fusion | flops 4306501632 | bytes 16779264 | tf_op jit(solution)/shard_map/sto,io->sti/dot_general | solution.py:1121
  339.3 5.7 bitcast_convert_fusion.2.refs_1_
  346.0 8.6 %bitcast_convert_fusion.3 = bf16[512,2048]{1,0:T(8,128)(2,1)S(1)} fusion(bf16[4,512,512]{2,1,0:T(8,128)(2,1)} %get-tuple-element.92.refs_0_, bf16[4,512,2048]{2,1,0:T(8,128)(2,1)} %copy-done.33), kind=kOutput, calls=%fused_computation.23 | convolution fusion | flops 4296015872 | bytes 12582912 | tf_op jit(solution)/shard_map/sti,sto->io/dot_general | solution.py:1125
  354.6 1.6 pad_maximum_fusion.refs_0_
  356.3 1.6 copy-done.19
  357.9 81.7 %plane_turn.1 = (f32[2,128,2048]{2,1,0:T(8,128)S(1)}, bf16[4,512,2048]{2,1,0:T(8,128)(2,1)}) custom-call(bf16[4,512,512]{2,1,0:T(8,128)(2,1)S(1)} %copy-done.19, bf16[2048,512]{1,0:T(8,128)(2,1)} %all-gather.8.cloned.1.call-done.weight, f32[2,128,2048]{2,1,0:T(8,128)} %copy-done.5, bf16[2,128,2048]{2,1,0:T(8,128)(2,1)S(1)} %copy-done.11, ...), custom_call_target="tpu_custom_call" | custom-call | tf_op jit(solution)/shard_map/plane_turn/pallas_call | solution.py:763
  439.6 1.4 copy-done.17
  441.0 1.2 slice.78
  442.8 12.2 %fusion.39 = (f32[4,512]{1,0:T(4,128)S(1)}, f32[4,512]{1,0:T(4,128)S(1)}, f32[4,512,512]{2,1,0:T(8,128)}, bf16[4,512,512]{2,1,0:T(8,128)(2,1)S(1)}) fusion(f32[4,512]{1,0:T(4,128)S(1)} %get-tuple-element.81, f32[4,512,512]{2,1,0:T(8,128)} %copy-done.35, f32[4,512]{1,0:T(4,128)S(1)} %broadcast_multiply_fusion.2, bf16[4,512,512]{2,1,0:T(8,128)(2,1)} %get-tuple-element.91, ...), kind=kOutput, calls=%fused_computation.99 | convolution fusion | flops 4313837568 | bytes 23101444 | tf_op jit(solution)/shard_map/sto,io->sti/dot_general | solution.py:1121
  455.0 1.3 copy-done.45
  456.3 9.6 %bitcast_convert_fusion.1.refs_16_ = bf16[2048,512]{1,0:T(8,128)(2,1)} fusion(bf16[4,512,2048]{2,1,0:T(8,128)(2,1)} %copy-done.32, bf16[4,512,512]{2,1,0:T(8,128)(2,1)S(1)} %get-tuple-element.73.refs_4_), kind=kOutput, calls=%fused_computation.21 | convolution fusion | flops 4296015872 | bytes 12582912 | tf_op jit(solution)/shard_map/sti,sto->io/dot_general | solution.py:1125
  466.0 1.1 slice.79
  467.8 9.1 %fusion.13.refs_17_ = bf16[512,2048]{1,0:T(8,128)(2,1)} fusion(bf16[4,512,512]{2,1,0:T(8,128)(2,1)S(1)} %copy-done.47, bf16[4,512,2048]{2,1,0:T(8,128)(2,1)} %get-tuple-element.50, f32[]{:T(128)} %bitcast.25), kind=kOutput, calls=%fused_computation.20 | convolution fusion | flops 4297064448 | bytes 12582916 | tf_op jit(solution)/shard_map/sti,sto->io/dot_general | solution.py:1125
  477.6 4.1 multiply_convert_fusion.1.refs_6_
  481.8 2.2 fusion.24.state
  484.0 84.4 %line_scan.3 = (bf16[4,256,512]{2,1,0:T(8,128)(2,1)}, bf16[2,128,2048]{2,1,0:T(8,128)(2,1)}, bf16[4,512,256]{2,1,0:T(8,128)(2,1)}, bf16[4,512,256]{2,1,0:T(8,128)(2,1)}, bf16[4,512,512]{2,1,0:T(8,128)(2,1)}) custom-call(f32[4,256,512]{2,1,0:T(8,128)} %fusion.24.state, f32[2,4]{1,0:T(2,128)} %stack.9.coef, bf16[4,512,512]{2,1,0:T(8,128)(2,1)} %get-tuple-element.92.refs_0_, ...), custom_call_target="tpu_custom_call" | custom-call | tf_op jit(solution)/shard_map/line_scan/pallas_call | solution.py:1020
  570.2 14.1 %bitcast_convert_fusion.refs_15_ = bf16[2048,1024]{1,0:T(8,128)(2,1)} fusion(bf16[4,512,2048]{2,1,0:T(8,128)(2,1)} %copy-done.32, bf16[4,512,512]{2,1,0:T(8,128)(2,1)} %get-tuple-element.55.refs_2_, bf16[4,512,256]{2,1,0:T(8,128)(2,1)} %get-tuple-element.54.refs_1_, bf16[4,512,256]{2,1,0:T(8,128)(2,1)} %get-tuple-element.53.refs_0_, bf16[]{:T(256)} %bitcast.30), kind=kOutput, calls=%fused_computation | convolution fusion | flops 8608808960 | bytes 16777218 | tf_op jit(solution)/shard_map/sti,sto->io/dot_general | solution.py:1125
  584.3 1.4 convert_reduce_fusion
  585.7 62.7 %plane_last.1 = (f32[2,128,2048]{2,1,0:T(8,128)}, f32[64,4096]{1,0:T(8,128)}, f32[64,4096]{1,0:T(8,128)}, f32[64,1]{1,0:T(8,128)}, f32[64,1]{1,0:T(8,128)}, /*index=5*/f32[128,2048]{1,0:T(8,128)}) custom-call(bf16[4,512,256]{2,1,0:T(8,128)(2,1)} %get-tuple-element.53.refs_0_, bf16[4,512,256]{2,1,0:T(8,128)(2,1)} %get-tuple-element.54.refs_1_, ...), custom_call_target="tpu_custom_call" | custom-call | tf_op jit(solution)/shard_map/plane_last/pallas_call | solution.py:834
  648.4 1.4 reduce.1
  649.8 11.0 %reduce-scatter.12.cloned.1.call-done = bf16[512,1024]{1,0:T(8,128)(2,1)} async-done(((bf16[2048,1024]{1,0:T(8,128)(2,1)}), bf16[512,1024]{1,0:T(8,128)(2,1)}) %reduce-scatter.12.cloned.1.call-update) | async-done | bytes 1048592 | tf_op jit(solution)/shard_map/reduce_scatter | solution.py:1193
  660.8 1.6 copy-done.6
  662.4 1.2 copy-done.26
  664.7 29.7 %plane_final.1 = (f32[64,2048]{1,0:T(8,128)S(1)}, f32[64,2048]{1,0:T(8,128)S(1)}, f32[64,4096]{1,0:T(8,128)S(1)}, f32[128,2048]{1,0:T(8,128)S(1)}, f32[64,1]{1,0:T(8,128)S(1)}) custom-call(bf16[8,64,1024]{2,1,0:T(8,128)(2,1)S(1)} %bitcast.83, bf16[128,2048]{1,0:T(8,128)(2,1)S(1)} %copy-done.29, f32[64,2048]{1,0:T(8,128)S(1)} %copy-done.21, ...), custom_call_target="tpu_custom_call" | custom-call | tf_op jit(solution)/shard_map/plane_final/pallas_call | solution.py:1059
  696.0 1.3 copy.119
  (160 shorter events, 29.9 us)
Async XLA Ops:
  7.2 208.1 %all-gather.4.cloned.1.call-start = ((), (), s32[]{:S(2)}) async-start(), calls=%async_computation.5 | async-start | bytes 5324800 | tf_op jit(solution)/shard_map/all_gather | solution.py:1190
  8.6 103.4 %copy-start.27 = (f32[64,1]{1,0:T(8,128)}, f32[64,1]{1,0:T(8,128)S(1)}, u32[]{:S(2)}) copy-start(f32[64,1]{1,0:T(8,128)S(1)} %copy.68.refs_4_.refs_12_.refs_3_) | copy-start | bytes 772
  8.7 103.4 %copy-start.30 = (f32[64,1]{1,0:T(8,128)}, f32[64,1]{1,0:T(8,128)S(1)}, u32[]{:S(2)}) copy-start(f32[64,1]{1,0:T(8,128)S(1)} %copy.69.refs_11_.refs_13_) | copy-start | bytes 772
  9.4 1.2 copy-start.2
  106.8 2.0 copy-start.14
  108.7 3.3 copy-start.32
  112.1 205.7 %all-gather.8.cloned.1.call-start = ((), (), s32[]{:S(2)}) async-start(), calls=%async_computation.7 | async-start | bytes 2621440 | tf_op jit(solution)/shard_map/all_gather | solution.py:1190
  125.3 3.7 copy-start.1
  127.8 353.9 %copy-start = (bf16[4,512,256]{2,1,0:T(8,128)(2,1)}, bf16[4,512,256]{2,1,0:T(8,128)(2,1)S(1)}, u32[]{:S(2)}) copy-start(bf16[4,512,256]{2,1,0:T(8,128)(2,1)S(1)} %fusion.16.refs_2_.refs_3_) | copy-start | bytes 3145732
  128.0 52.5 %copy-start.4 = (bf16[4,512,256]{2,1,0:T(8,128)(2,1)}, bf16[4,512,256]{2,1,0:T(8,128)(2,1)S(1)}, u32[]{:S(2)}) copy-start(bf16[4,512,256]{2,1,0:T(8,128)(2,1)S(1)} %pad_maximum_fusion.1.refs_3_.refs_4_) | copy-start | bytes 3145732
  128.0 1.8 copy-start.10
  180.5 4.2 copy-start.33
  180.5 4.7 copy-start.9
  180.8 4.0 copy-start.39
  181.6 3.2 copy-start.37
  186.1 2.1 copy-start.35
  217.9 111.7 %all-gather.6.cloned.1.call-start = ((), (), s32[]{:S(2)}) async-start(), calls=%async_computation.6 | async-start | bytes 2621440 | tf_op jit(solution)/shard_map/all_gather | solution.py:1190
  218.0 2.8 copy-start.36
  219.9 9.7 %copy-start.40 = (bf16[4,512,512]{2,1,0:T(8,128)(2,1)}, bf16[4,512,512]{2,1,0:T(8,128)(2,1)S(1)}, u32[]{:S(2)}) copy-start(bf16[4,512,512]{2,1,0:T(8,128)(2,1)S(1)} %slice_add_fusion) | copy-start | bytes 6291460
  220.8 12.4 %copy-start.3 = (bf16[2,128,2048]{2,1,0:T(8,128)(2,1)S(1)}, bf16[2,128,2048]{2,1,0:T(8,128)(2,1)}, u32[]{:S(2)}) copy-start(bf16[2,128,2048]{2,1,0:T(8,128)(2,1)} %refs_6_.1) | copy-start | bytes 3145732
  229.6 1.3 copy-start.46
  232.9 208.1 %reduce-scatter.6.cloned.1.call-start = ((), (), s32[]{:S(2)}) async-start(), calls=%async_computation.8 | async-start | bytes 2621440 | tf_op jit(solution)/shard_map/reduce_scatter | solution.py:1193
  233.2 81.2 %copy-start.15 = (f32[512,1]{1,0:T(8,128)}, f32[512,1]{1,0:T(8,128)S(1)}, u32[]{:S(2)}) copy-start(f32[512,1]{1,0:T(8,128)S(1)} %get-tuple-element.98.refs_2_.refs_11_) | copy-start | bytes 6148
  233.2 81.2 %copy-start.16 = (f32[512,1]{1,0:T(8,128)}, f32[512,1]{1,0:T(8,128)S(1)}, u32[]{:S(2)}) copy-start(f32[512,1]{1,0:T(8,128)S(1)} %get-tuple-element.99.refs_1_.refs_10_) | copy-start | bytes 6148
  314.4 1.3 copy-start.5
  315.8 1.3 copy-start.34
  329.7 9.6 %copy-start.53 = (bf16[4,512,2048]{2,1,0:T(8,128)(2,1)S(1)}, bf16[4,512,2048]{2,1,0:T(8,128)(2,1)}, u32[]{:S(2)}) copy-start(bf16[4,512,2048]{2,1,0:T(8,128)(2,1)} %get-tuple-element.47) | copy-start | bytes 25165828
  339.2 6.0 copy-start.18
  345.0 121.0 %reduce-scatter.8.cloned.1.call-start = ((), (), s32[]{:S(2)}) async-start(), calls=%async_computation.9 | async-start | bytes 2785280 | tf_op jit(solution)/shard_map/reduce_scatter | solution.py:1193
  354.6 1.7 copy-start.11
  356.2 212.1 %reduce-scatter.10.cloned.1.call-start = ((), (), s32[]{:S(2)}) async-start(), calls=%async_computation.10 | async-start | bytes 2621440 | tf_op jit(solution)/shard_map/reduce_scatter | solution.py:1193
  356.3 1.6 copy-start.19
  439.6 1.4 copy-start.17
  455.0 1.3 copy-start.45
  456.3 11.5 %copy-start.47 = (bf16[4,512,512]{2,1,0:T(8,128)(2,1)S(1)}, bf16[4,512,512]{2,1,0:T(8,128)(2,1)}, u32[]{:S(2)}) copy-start(bf16[4,512,512]{2,1,0:T(8,128)(2,1)} %copy-done.46) | copy-start | bytes 6291460
  465.9 183.9 %reduce-scatter.14.cloned.1.call-start = ((), (), s32[]{:S(2)}) async-start(), calls=%async_computation.12 | async-start | bytes 2621440 | tf_op jit(solution)/shard_map/reduce_scatter | solution.py:1193
  477.0 183.9 %reduce-scatter.12.cloned.1.call-start = ((), (), s32[]{:S(2)}) async-start(), calls=%async_computation.11 | async-start | bytes 5242880 | tf_op jit(solution)/shard_map/reduce_scatter | solution.py:1193
  481.7 2.2 copy-start.38
  585.7 75.1 %copy-start.13 = (f32[64,4096]{1,0:T(8,128)S(1)}, f32[64,4096]{1,0:T(8,128)}, u32[]{:S(2)}) copy-start(f32[64,4096]{1,0:T(8,128)} %refs_2_.3) | copy-start | bytes 3145732
  585.7 75.1 %copy-start.21 = (f32[64,2048]{1,0:T(8,128)S(1)}, f32[64,2048]{1,0:T(8,128)}, u32[]{:S(2)}) copy-start(f32[64,2048]{1,0:T(8,128)} %refs_0_.5) | copy-start | bytes 1572868
  585.7 75.2 %copy-start.23 = (f32[64,2048]{1,0:T(8,128)S(1)}, f32[64,2048]{1,0:T(8,128)}, u32[]{:S(2)}) copy-start(f32[64,2048]{1,0:T(8,128)} %refs_1_.3) | copy-start | bytes 1572868
  585.7 75.2 %copy-start.28 = (f32[64,1]{1,0:T(8,128)S(1)}, f32[64,1]{1,0:T(8,128)}, u32[]{:S(2)}) copy-start(f32[64,1]{1,0:T(8,128)} %copy-done.27) | copy-start | bytes 772
  585.7 109.3 %copy-start.48 = (bf16[2,128,2048]{2,1,0:T(8,128)(2,1)S(1)}, bf16[2,128,2048]{2,1,0:T(8,128)(2,1)}, u32[]{:S(2)}) copy-start(bf16[2,128,2048]{2,1,0:T(8,128)(2,1)} %get-tuple-element.114) | copy-start | bytes 3145732
  648.4 46.0 %copy-start.52 = (f32[64,1]{1,0:T(8,128)S(1)}, f32[64,1]{1,0:T(8,128)}, u32[]{:S(2)}) copy-start(f32[64,1]{1,0:T(8,128)} %get-tuple-element.59) | copy-start | bytes 772
  660.8 1.6 copy-start.6
  696.0 3.9 copy-start.51
  697.3 4.5 copy-start.50
  698.9 3.9 copy-start.49
  (14 other events, 14.6 us)
Sparse Core Ops, SparseCore 0:
  112.2 102.9 all-gather.3
  218.1 56.3 all-gather.7
  276.6 44.6 all-gather.5
  345.1 54.2 reduce-scatter.5
  401.7 45.3 reduce-scatter.7
  466.1 66.7 reduce-scatter.9
  535.2 48.2 reduce-scatter.13
  585.9 74.8 reduce-scatter.11

commit v6 on v5

--- a/solution.py
+++ b/solution.py
@@ -315,7 +315,17 @@
 
 
 def open_kernel(count, chunks, line, order, moves, unit_moves, head_moves, *refs):
-    weights, gain_one, out, docs, x, up, down, bias, gain_two = refs[:4], *refs[4:12]
+    gain_one, docs, bias, gain_two = refs[4], refs[6], refs[10], refs[11]
+    fetched = [i for i in range(10) if i not in (4, 6)]
+    held, fetch_sem = refs[-9:-1], refs[-1]
+    fetches = [
+        pltpu.make_async_copy(refs[i], ref, fetch_sem.at[n])
+        for n, (i, ref) in enumerate(zip(fetched, held))
+    ]
+    for copy in fetches:
+        copy.start()
+    refs = refs[:-9]
+    weights, out, x, up, down = held[:4], *held[4:]
     normed_all, up_mine, first_all, gate_out, down_pack, docs_all = refs[-28:-22]
     qkv_pack, gate_pack, out_low, out_mine, normed, up_low, down_low, bias_low = refs[-22:-14]
     sems = refs[-14:]
@@ -362,6 +372,7 @@
     ends = (here > 0).astype(jnp.int32) + (here < count - 1).astype(jnp.int32)
     greeted = greet_partner(barrier) + len(targets) + ends
     for i in (0, 1, 2):
+        fetches[i].wait()
         pack(i, qkv_pack)
     pl.semaphore_wait(barrier, greeted)
     first[0]()
@@ -376,6 +387,8 @@
     keep = pltpu.make_async_copy(docs, docs_all.at[row], sems[9].at[6])
     give.start()
     keep.start()
+    for copy in fetches[3:]:
+        copy.wait()
     out_low[...] = out[...].astype(BF16)
     trade[0]()
     _, col, _, across, sibling = plane_ids()
@@ -457,7 +470,7 @@
             jax.ShapeDtypeStruct(down.shape, BF16),
             jax.ShapeDtypeStruct((2,) + docs.shape, docs.dtype),
         ],
-        in_specs=[VMEM] * 12,
+        in_specs=[ANY] * 4 + [VMEM, ANY, VMEM, ANY, ANY, ANY, VMEM, VMEM],
         out_specs=[ANY] * 6,
         scratch_shapes=[
             pltpu.VMEM((group, rows, first), BF16),
@@ -476,11 +489,13 @@
             pltpu.SemaphoreType.DMA((2, count, chunks)),
             pltpu.SemaphoreType.DMA((2, count, chunks)),
             pltpu.SemaphoreType.DMA((2 + len(moves),)),
+            *[pltpu.VMEM(a.shape, a.dtype) for a in (*weights, out, x, up, down)],
+            pltpu.SemaphoreType.DMA((8,)),
         ],
         compiler_params=pltpu.CompilerParams(
             collective_id=collective_id,
             has_side_effects=True,
-            vmem_limit_bytes=32 * 1024 * 1024,
+            vmem_limit_bytes=60 * 1024 * 1024,
         ),
         name="open_plane",
     )(*weights, gain_one, out, docs, x, up, down, bias, gain_two)
@@ -1032,32 +1047,60 @@
     )(state, coef, *operands, *before)
 
 
-def final_kernel(line, order, moves, grad, grad_out, *refs):
+def final_kernel(line, order, heads_pb, moves, grad, grad_out, *refs):
     weights, gain = refs[:3], refs[3]
     outs, out_out, sums, landed, out_landed = refs[-11:-8], refs[-8], refs[-7], refs[-6], refs[-5]
     targets, stages = owners_stages((grad,), (blocks_of(landed),), *refs[-4:-1])
     greet_partner, trade = trade_stages(line, grad_out, out_landed, refs[-1])
+    row, col, other_row, across, sibling = plane_ids()
+    across_s = lax.rem(sibling + 2, 4)
     barrier = pltpu.get_barrier_semaphore()
     for target in targets:
         pl.semaphore_signal(barrier, inc=1, device_id=target, device_id_type=MESH)
     pl.semaphore_wait(barrier, greet_partner(barrier) + len(targets))
     stages[0]()
-    for stage in trade:
-        stage()
+    trade[0]()
+    kept, arrive, leave = stages[2]
+
+    def place(r, c):
+        head = (c // heads_pb) * (2 * heads_pb) + r * heads_pb + lax.rem(c, heads_pb)
+        total = 0.0
+        for weight, target, blocks in zip(weights, outs, moves):
+            _, _, start, size = blocks[0]
+            columns = pl.ds(pl.multiple_of(head * size, size), size)
+            value = landed[r * 4 + c, :, start : start + size].astype(F32)
+            low = weight[:, columns].astype(BF16).astype(F32)
+            target[:, columns] = gain[...] * value
+            total = total + jnp.sum(low * value, axis=-1, keepdims=True)
+        return total
+
+    kept()
+    total = place(row, col)
+    for r, c, far in (
+        (row, sibling, False),
+        (row, across, False),
+        (other_row, col, True),
+        (row, across_s, False),
+        (other_row, sibling, True),
+        (other_row, across, True),
+        (other_row, across_s, True),
+    ):
+        arrive(r, c, far)
+        total = total + place(r, c)
+    sums[...] = total
+    trade[1]()
     size = out_out.shape[1] // max(len(order), 1)
     for j, i in enumerate(order or (0,)):
         block = out_landed[:, j * size : (j + 1) * size]
         out_out[:, i * size : (i + 1) * size] = block.astype(F32)
-    stages[1]()
-    total = 0.0
-    for weight, target, blocks in zip(weights, outs, moves):
-        total = total + put_back(landed, weight, gain, target, blocks)
-    sums[...] = total
-
-
-def plane_final(grad, grad_out, weights, gain, line, order, moves, collective_id, *before):
+    leave()
+
+
+def plane_final(
+    grad, grad_out, weights, gain, line, order, heads_pb, moves, collective_id, *before
+):
     return pl.pallas_call(
-        functools.partial(final_kernel, line, order, moves),
+        functools.partial(final_kernel, line, order, heads_pb, moves),
         out_shape=[jax.ShapeDtypeStruct(w.shape, F32) for w in weights]
         + [
             jax.ShapeDtypeStruct(grad_out.shape, F32),
@@ -1396,6 +1439,10 @@
         sums_up = jnp.sum(w_up.astype(BF16).astype(F32) * shard_up, axis=-1, keepdims=True)
         shard_up = gain_two * shard_up
 
+    output, grad_inputs, shard_gate, shard_up, shard_down = (
+        after(a, sums_gate) for a in (output, grad_inputs, shard_gate, shard_up, shard_down)
+    )
+
     shard_query, shard_key, shard_value, shard_out, sums_qkv = plane_final(
         grad_qkv_sum.reshape(cut),
         grad_out,
@@ -1403,9 +1450,10 @@
         gain_one,
         line,
         order,
+        heads_pb,
         head_moves[:3],
         9,
-        grad_inputs,
+        sums_gate,
     )
     if not order:
         shard_out = to_outer(shard_out)

time: 719 us -> 700 us (0.974)
  local copies, waits for them, and re-layouts: 50.4 us -> 32 us
  waiting for transfers between devices: 36.3 us -> 26.4 us
    unnamed x117 -> x88, local copies, waits for them, and re-layouts: 43 us -> 20.7 us
    reduce_scatter x5, waiting for transfers between devices: 11 us -> 2.13 us  [scatter_line(): return lax.psum_scatter(values, LINE, scatter_dimension=0, tiled=True)]
  transfers between devices with their start and end apart: 8 -> 8, of which waited for: 2 -> 2; matrix products, arithmetic and copies ran while one was open for 16% -> 18% of each run, Pallas kernels for 51% -> 52%
where the time goes in v6:
time: 700 us; the launch traced here: 692 us
  Pallas kernels  480 us (69%)
  matrix products  109 us (16%)
  local copies, waits for them, and re-layouts  32 us (5%)
  waiting for transfers between devices  26.4 us (4%)
  other arithmetic  25.1 us (4%)
  between operations  19.7 us (3%)
    pallas_call x2, Pallas kernels, line_scan(): pl.pallas_call(functools.partial(scan_kernel, count, forward, cuts, gathe...  137 us
    pallas_call x1, Pallas kernels, open_plane(): pl.pallas_call(functools.partial(open_kernel, count, chunks, line, order,...  88.5 us
    pallas_call x1, Pallas kernels, plane_turn(): pl.pallas_call(functools.partial(turn_kernel, order), out_shape=[jax.Shap...  81.7 us
    pallas_call x1, Pallas kernels, plane_mix(): pl.pallas_call(functools.partial(mix_kernel, order, places), out_shape=[j...  81.1 us
    pallas_call x1, Pallas kernels, plane_last(): pl.pallas_call(functools.partial(last_kernel, order, moves), out_shape=[j...  62.6 us
    dot_general x6, matrix products, mm_grad(): return jnp.einsum('sti,sto->io', left, right, preferred_element_type=F32)  47.8 us
    dot_general x3, matrix products, mm(): return jnp.einsum('sti,io->sto', left, right, preferred_element_type=F32)  33 us
    pallas_call x1, Pallas kernels, plane_final(): pl.pallas_call(functools.partial(final_kernel, line, order, heads_pb, mov...  29.1 us
  transfers between devices with their start and end apart: 8, of which 2 were waited for; matrix products, arithmetic and copies ran while one was open for 18% of the time, Pallas kernels for 52%

profile of v6, /device:TPU:2, one launch (start us, length us, event | category | flops | bytes accessed | tf_op | source)
XLA Modules:
  0.0 692.3 jit_solution(15094608804937874918)
XLA Ops:
  9.9 1.3 pad.6.refs_6_
  11.2 88.5 %open_plane.1 = (bf16[4,512,2048]{2,1,0:T(8,128)(2,1)}, bf16[8,64,512]{2,1,0:T(8,128)(2,1)}, bf16[2048,1024]{1,0:T(8,128)(2,1)}, bf16[1040,512]{1,0:T(8,128)(2,1...) custom-call(f32[64,2048]{1,0:T(8,128)} %refs_0_.5, f32[64,2048]{1,0:T(8,128)} %refs_1_.3, f32[64,4096]{1,0:T(8,128)} %refs_2_.3, ...), custom_call_target="tpu_custom_call" | custom-call | tf_op jit(solution)/shard_map/open_plane/pallas_call | solution.py:461
  100.9 12.5 %fusion.14 = f32[4,512,1024]{2,1,0:T(8,128)S(1)} fusion(bf16[4,512,2048]{2,1,0:T(8,128)(2,1)} %get-tuple-element.40, bf16[2048,1024]{1,0:T(8,128)(2,1)} %get-tuple-element.41.refs_3_), kind=kOutput, calls=%fused_computation.24 | convolution fusion | flops 8589934592 | bytes 20971520 | tf_op jit(solution)/shard_map/sti,io->sto/dot_general | solution.py:1160
  113.9 1.1 fusion.29
  118.1 51.7 %line_scan.2 = (bf16[4,256,512]{2,1,0:T(8,128)(2,1)S(1)}, bf16[4,512,2048]{2,1,0:T(8,128)(2,1)S(1)}) custom-call(f32[4,256,512]{2,1,0:T(8,128)S(1)} %fusion.25.state, f32[2,4]{1,0:T(2,128)S(1)} %stack.8.coef, bf16[2,128,2048]{2,1,0:T(8,128)(2,1)S(1)} %copy-done.7, bf16[4,512,512]{2,1,0:T(8,128)(2,1)S(1)} %slice.102.refs_1_.refs_5_, ...), custom_call_target="tpu_custom_call" | custom-call | tf_op jit(solution)/shard_map/line_scan/pallas_call | solution.py:1035
  170.0 1.1 copy-done.26
  172.0 1.3 fusion.42
  175.4 2.0 copy-done.22
  179.4 24.2 %all-gather.4.cloned.1.call-done.gate_out = bf16[4160,512]{1,0:T(8,128)(2,1)} async-done(((bf16[1040,512]{1,0:T(8,128)(2,1)}), bf16[4160,512]{1,0:T(8,128)(2,1)}) %all-gather.4.cloned.1.call-update) | async-done | bytes 4259856 | tf_op jit(solution)/shard_map/all_gather | solution.py:1233
  203.6 1.2 slice.84
  206.4 1.9 slice_add_fusion
  209.2 8.8 %multiply_convert_fusion.3 = (bf16[4,512,512]{2,1,0:T(8,128)(2,1)S(1)}, bf16[4,512,512]{2,1,0:T(8,128)(2,1)}) fusion(f32[4,512,512]{2,1,0:T(8,128)S(1)} %copy-done.23, f32[4,512]{1,0:T(4,128)S(1)} %get-tuple-element.81, f32[4,512]{1,0:T(4,128)S(1)} %broadcast_multiply_fusion.2, bf16[4,512,2048]{2,1,0:T(8,128)(2,1)} %get-tuple-element.40, ...), kind=kOutput, calls=%fused_computation.31 | convolution fusion | flops 4304404480 | bytes 18890752 | tf_op jit(solution)/shard_map/sti,io->sto/dot_general | solution.py:1160
  217.9 1.3 copy-done.32
  221.7 81.1 %plane_mix.1 = (f32[2,128,2048]{2,1,0:T(8,128)S(1)}, bf16[4,512,2048]{2,1,0:T(8,128)(2,1)}, bf16[512,2048]{1,0:T(8,128)(2,1)S(1)}) custom-call(bf16[4,512,512]{2,1,0:T(8,128)(2,1)} %copy-done.32, bf16[2,128,2048]{2,1,0:T(8,128)(2,1)S(1)} %copy-done.2, bf16[4160,512]{1,0:T(8,128)(2,1)} %all-gather.4.cloned.1.call-done.gate_out, ...), custom_call_target="tpu_custom_call" | custom-call | tf_op jit(solution)/shard_map/plane_mix/pallas_call | solution.py:731
  302.8 1.4 copy-done.4
  304.2 1.3 copy-done.21
  306.2 11.7 %multiply_convert_fusion.2 = (bf16[4,512,512]{2,1,0:T(8,128)(2,1)}, f32[4,512,512]{2,1,0:T(8,128)}) fusion(f32[512]{0:T(512)S(1)} %bitcast.93, bf16[4,512,2048]{2,1,0:T(8,128)(2,1)} %get-tuple-element.47, bf16[2048,512]{1,0:T(8,128)(2,1)} %all-gather.8.cloned.1.call-done.weight), kind=kOutput, calls=%fused_computation.29 | convolution fusion | flops 4301258752 | bytes 16779264 | tf_op jit(solution)/shard_map/sti,io->sto/dot_general | solution.py:1160
  317.9 9.6 %fusion.8.grad = bf16[4,512,512]{2,1,0:T(8,128)(2,1)S(1)} fusion(f32[4,512,512]{2,1,0:T(8,128)} %get-tuple-element.93, bf16[4,512,2048]{2,1,0:T(8,128)(2,1)} %copy-done.20, bf16[512,2048]{1,0:T(8,128)(2,1)} %all-gather.6.cloned.1.call-done.refs_1_, f32[512]{0:T(512)S(1)} %bitcast.94), kind=kOutput, calls=%fused_computation.12 | convolution fusion | flops 4306501632 | bytes 16779264 | tf_op jit(solution)/shard_map/sto,io->sti/dot_general | solution.py:1164
  327.5 5.7 bitcast_convert_fusion.2.refs_1_
  334.3 8.6 %bitcast_convert_fusion.3 = bf16[512,2048]{1,0:T(8,128)(2,1)S(1)} fusion(bf16[4,512,512]{2,1,0:T(8,128)(2,1)} %get-tuple-element.92.refs_0_, bf16[4,512,2048]{2,1,0:T(8,128)(2,1)} %copy-done.20), kind=kOutput, calls=%fused_computation.23 | convolution fusion | flops 4296015872 | bytes 12582912 | tf_op jit(solution)/shard_map/sti,sto->io/dot_general | solution.py:1168
  342.9 1.6 pad_maximum_fusion.refs_0_
  344.6 1.6 copy-done.15
  346.2 81.7 %plane_turn.1 = (f32[2,128,2048]{2,1,0:T(8,128)S(1)}, bf16[4,512,2048]{2,1,0:T(8,128)(2,1)}) custom-call(bf16[4,512,512]{2,1,0:T(8,128)(2,1)S(1)} %copy-done.15, bf16[2048,512]{1,0:T(8,128)(2,1)} %all-gather.8.cloned.1.call-done.weight, f32[2,128,2048]{2,1,0:T(8,128)} %copy-done.4, bf16[2,128,2048]{2,1,0:T(8,128)(2,1)S(1)} %copy-done.8, ...), custom_call_target="tpu_custom_call" | custom-call | tf_op jit(solution)/shard_map/plane_turn/pallas_call | solution.py:778
  427.9 1.4 copy-done.11
  429.3 1.2 slice.86
  431.2 12.2 %fusion.39 = (f32[4,512]{1,0:T(4,128)S(1)}, f32[4,512]{1,0:T(4,128)S(1)}, f32[4,512,512]{2,1,0:T(8,128)}, bf16[4,512,512]{2,1,0:T(8,128)(2,1)S(1)}) fusion(f32[4,512]{1,0:T(4,128)S(1)} %get-tuple-element.81, f32[4,512,512]{2,1,0:T(8,128)} %copy-done.22, f32[4,512]{1,0:T(4,128)S(1)} %broadcast_multiply_fusion.2, ...), kind=kOutput, calls=%fused_computation.104 | convolution fusion | flops 4313837568 | bytes 23101444 | tf_op jit(solution)/shard_map/sto,io->sti/dot_general | solution.py:1164
  443.4 1.3 copy-done.34
  444.7 9.6 %bitcast_convert_fusion.1.refs_16_ = bf16[2048,512]{1,0:T(8,128)(2,1)} fusion(bf16[4,512,2048]{2,1,0:T(8,128)(2,1)} %get-tuple-element.40, bf16[4,512,512]{2,1,0:T(8,128)(2,1)S(1)} %get-tuple-element.73.refs_4_), kind=kOutput, calls=%fused_computation.21 | convolution fusion | flops 4296015872 | bytes 12582912 | tf_op jit(solution)/shard_map/sti,sto->io/dot_general | solution.py:1168
  454.4 1.2 slice.87
  456.3 9.2 %fusion.13.refs_17_ = bf16[512,2048]{1,0:T(8,128)(2,1)} fusion(bf16[4,512,512]{2,1,0:T(8,128)(2,1)S(1)} %copy-done.33, bf16[4,512,2048]{2,1,0:T(8,128)(2,1)} %get-tuple-element.50, f32[]{:T(128)} %bitcast.25), kind=kOutput, calls=%fused_computation.20 | convolution fusion | flops 4297064448 | bytes 12582916 | tf_op jit(solution)/shard_map/sti,sto->io/dot_general | solution.py:1168
  466.1 4.1 multiply_convert_fusion.1.refs_6_
  470.2 2.2 fusion.24.state
  472.5 84.9 %line_scan.3 = (bf16[4,256,512]{2,1,0:T(8,128)(2,1)}, bf16[2,128,2048]{2,1,0:T(8,128)(2,1)}, bf16[4,512,256]{2,1,0:T(8,128)(2,1)}, bf16[4,512,256]{2,1,0:T(8,128)(2,1)}, bf16[4,512,512]{2,1,0:T(8,128)(2,1)}) custom-call(f32[4,256,512]{2,1,0:T(8,128)} %fusion.24.state, f32[2,4]{1,0:T(2,128)} %stack.9.coef, bf16[4,512,512]{2,1,0:T(8,128)(2,1)} %get-tuple-element.92.refs_0_, ...), custom_call_target="tpu_custom_call" | custom-call | tf_op jit(solution)/shard_map/line_scan/pallas_call | solution.py:1035
  557.4 1.2 slice.88
  559.3 14.0 %bitcast_convert_fusion.refs_15_ = bf16[2048,1024]{1,0:T(8,128)(2,1)} fusion(bf16[4,512,2048]{2,1,0:T(8,128)(2,1)} %get-tuple-element.40, bf16[4,512,512]{2,1,0:T(8,128)(2,1)} %get-tuple-element.55.refs_2_, bf16[4,512,256]{2,1,0:T(8,128)(2,1)} %get-tuple-element.54.refs_1_, bf16[4,512,256]{2,1,0:T(8,128)(2,1)} %get-tuple-element.53.refs_0_, bf16[]{:T(256)} %bitcast.30), kind=kOutput, calls=%fused_computation | convolution fusion | flops 8608808960 | bytes 16777218 | tf_op jit(solution)/shard_map/sti,sto->io/dot_general | solution.py:1168
  573.3 1.4 convert_reduce_fusion
  574.7 62.6 %plane_last.1 = (f32[2,128,2048]{2,1,0:T(8,128)}, f32[64,4096]{1,0:T(8,128)}, f32[64,4096]{1,0:T(8,128)}, f32[64,1]{1,0:T(8,128)}, f32[64,1]{1,0:T(8,128)}, /*index=5*/f32[128,2048]{1,0:T(8,128)}) custom-call(bf16[4,512,256]{2,1,0:T(8,128)(2,1)} %get-tuple-element.53.refs_0_, bf16[4,512,256]{2,1,0:T(8,128)(2,1)} %get-tuple-element.54.refs_1_, ...), custom_call_target="tpu_custom_call" | custom-call | tf_op jit(solution)/shard_map/plane_last/pallas_call | solution.py:849
  637.3 1.2 slice.74
  639.2 1.4 reduce.1
  640.6 2.4 broadcast_add_fusion.1
  643.0 1.0 broadcast_add_fusion.4
  644.1 1.5 broadcast_add_fusion
  645.6 1.0 broadcast_add_fusion.3
  646.6 1.0 broadcast_add_fusion.2
  647.7 2.1 reduce-scatter.12.cloned.1.call-done
  649.8 1.2 copy-done.16
  651.0 1.0 copy-done.18
  652.0 29.1 %plane_final.1 = (f32[64,2048]{1,0:T(8,128)S(1)}, f32[64,2048]{1,0:T(8,128)S(1)}, f32[64,4096]{1,0:T(8,128)S(1)}, f32[128,2048]{1,0:T(8,128)S(1)}, f32[64,1]{1,0:T(8,128)S(1)}) custom-call(bf16[8,64,1024]{2,1,0:T(8,128)(2,1)S(1)} %bitcast.84, bf16[128,2048]{1,0:T(8,128)(2,1)S(1)} %copy-done.18, f32[64,2048]{1,0:T(8,128)S(1)} %copy-done.12, ...), custom_call_target="tpu_custom_call" | custom-call | tf_op jit(solution)/shard_map/plane_final/pallas_call | solution.py:1102
  (137 shorter events, 21.9 us)
Async XLA Ops:
  7.2 196.4 %all-gather.4.cloned.1.call-start = ((), (), s32[]{:S(2)}) async-start(), calls=%async_computation.5 | async-start | bytes 5324800 | tf_op jit(solution)/shard_map/all_gather | solution.py:1233
  99.8 206.4 %all-gather.8.cloned.1.call-start = ((), (), s32[]{:S(2)}) async-start(), calls=%async_computation.7 | async-start | bytes 2621440 | tf_op jit(solution)/shard_map/all_gather | solution.py:1233
  113.7 3.6 copy-start.1
  115.0 0.9 copy-start.30
  115.0 0.9 copy-start.31
  116.1 354.1 %copy-start = (bf16[4,512,256]{2,1,0:T(8,128)(2,1)}, bf16[4,512,256]{2,1,0:T(8,128)(2,1)S(1)}, u32[]{:S(2)}) copy-start(bf16[4,512,256]{2,1,0:T(8,128)(2,1)S(1)} %fusion.16.refs_2_.refs_3_) | copy-start | bytes 3145732
  116.3 53.5 %copy-start.3 = (bf16[4,512,256]{2,1,0:T(8,128)(2,1)}, bf16[4,512,256]{2,1,0:T(8,128)(2,1)S(1)}, u32[]{:S(2)}) copy-start(bf16[4,512,256]{2,1,0:T(8,128)(2,1)S(1)} %pad_maximum_fusion.1.refs_3_.refs_4_) | copy-start | bytes 3145732
  116.3 1.8 copy-start.7
  169.8 4.2 copy-start.20
  169.8 4.7 copy-start.6
  170.0 1.2 copy-start.26
  172.0 2.0 copy-start.24
  175.4 2.1 copy-start.22
  175.4 30.0 %copy-start.39 = (bf16[8,64,512]{2,1,0:T(8,128)(2,1)S(1)}, bf16[8,64,512]{2,1,0:T(8,128)(2,1)}, u32[]{:S(2)}) copy-start(bf16[8,64,512]{2,1,0:T(8,128)(2,1)} %get-tuple-element.48) | copy-start | bytes 1572868
  206.3 111.6 %all-gather.6.cloned.1.call-start = ((), (), s32[]{:S(2)}) async-start(), calls=%async_computation.6 | async-start | bytes 2621440 | tf_op jit(solution)/shard_map/all_gather | solution.py:1233
  206.3 2.8 copy-start.23
  208.2 9.7 %copy-start.27 = (bf16[4,512,512]{2,1,0:T(8,128)(2,1)}, bf16[4,512,512]{2,1,0:T(8,128)(2,1)S(1)}, u32[]{:S(2)}) copy-start(bf16[4,512,512]{2,1,0:T(8,128)(2,1)S(1)} %slice_add_fusion) | copy-start | bytes 6291460
  209.2 11.3 %copy-start.40 = (bf16[128,2048]{1,0:T(8,128)(2,1)S(1)}, bf16[128,2048]{1,0:T(8,128)(2,1)}, u32[]{:S(2)}) copy-start(bf16[128,2048]{1,0:T(8,128)(2,1)} %get-tuple-element.45) | copy-start | bytes 1572868
  209.2 12.5 %copy-start.2 = (bf16[2,128,2048]{2,1,0:T(8,128)(2,1)S(1)}, bf16[2,128,2048]{2,1,0:T(8,128)(2,1)}, u32[]{:S(2)}) copy-start(bf16[2,128,2048]{2,1,0:T(8,128)(2,1)} %refs_6_.1) | copy-start | bytes 3145732
  217.9 1.3 copy-start.32
  221.3 208.0 %reduce-scatter.6.cloned.1.call-start = ((), (), s32[]{:S(2)}) async-start(), calls=%async_computation.8 | async-start | bytes 2621440 | tf_op jit(solution)/shard_map/reduce_scatter | solution.py:1236
  221.6 81.2 %copy-start.9 = (f32[512,1]{1,0:T(8,128)}, f32[512,1]{1,0:T(8,128)S(1)}, u32[]{:S(2)}) copy-start(f32[512,1]{1,0:T(8,128)S(1)} %get-tuple-element.98.refs_2_.refs_11_) | copy-start | bytes 6148
  221.6 81.2 %copy-start.10 = (f32[512,1]{1,0:T(8,128)}, f32[512,1]{1,0:T(8,128)S(1)}, u32[]{:S(2)}) copy-start(f32[512,1]{1,0:T(8,128)S(1)} %get-tuple-element.99.refs_1_.refs_10_) | copy-start | bytes 6148
  302.8 1.4 copy-start.4
  304.2 1.3 copy-start.21
  317.9 9.6 %copy-start.41 = (bf16[4,512,2048]{2,1,0:T(8,128)(2,1)S(1)}, bf16[4,512,2048]{2,1,0:T(8,128)(2,1)}, u32[]{:S(2)}) copy-start(bf16[4,512,2048]{2,1,0:T(8,128)(2,1)} %get-tuple-element.47) | copy-start | bytes 25165828
  327.5 6.0 copy-start.14
  333.3 121.1 %reduce-scatter.8.cloned.1.call-start = ((), (), s32[]{:S(2)}) async-start(), calls=%async_computation.9 | async-start | bytes 2785280 | tf_op jit(solution)/shard_map/reduce_scatter | solution.py:1236
  342.9 1.7 copy-start.8
  344.5 212.9 %reduce-scatter.10.cloned.1.call-start = ((), (), s32[]{:S(2)}) async-start(), calls=%async_computation.10 | async-start | bytes 2621440 | tf_op jit(solution)/shard_map/reduce_scatter | solution.py:1236
  344.6 1.6 copy-start.15
  427.9 1.4 copy-start.11
  443.4 1.3 copy-start.34
  444.7 11.5 %copy-start.33 = (bf16[4,512,512]{2,1,0:T(8,128)(2,1)S(1)}, bf16[4,512,512]{2,1,0:T(8,128)(2,1)}, u32[]{:S(2)}) copy-start(bf16[4,512,512]{2,1,0:T(8,128)(2,1)} %copy-done.32) | copy-start | bytes 6291460
  454.3 193.3 %reduce-scatter.14.cloned.1.call-start = ((), (), s32[]{:S(2)}) async-start(), calls=%async_computation.12 | async-start | bytes 2621440 | tf_op jit(solution)/shard_map/reduce_scatter | solution.py:1236
  465.4 184.3 %reduce-scatter.12.cloned.1.call-start = ((), (), s32[]{:S(2)}) async-start(), calls=%async_computation.11 | async-start | bytes 5242880 | tf_op jit(solution)/shard_map/reduce_scatter | solution.py:1236
  470.2 2.2 copy-start.25
  574.7 68.3 %copy-start.36 = (bf16[2,128,2048]{2,1,0:T(8,128)(2,1)S(1)}, bf16[2,128,2048]{2,1,0:T(8,128)(2,1)}, u32[]{:S(2)}) copy-start(bf16[2,128,2048]{2,1,0:T(8,128)(2,1)} %get-tuple-element.52) | copy-start | bytes 3145732
  640.6 3.5 copy-start.35
  640.6 5.0 copy-start.38
  643.0 3.6 copy-start.37
  644.1 5.7 copy-start.5
  644.1 5.7 copy-start.12
  644.1 5.7 copy-start.13
  644.1 5.7 copy-start.17
  644.1 5.7 copy-start.19
  649.8 1.2 copy-start.16
  651.0 1.0 copy-start.18
  (2 other events, 1.5 us)
Sparse Core Ops, SparseCore 0:
  99.9 103.6 all-gather.3
  206.4 56.9 all-gather.7
  265.5 44.9 all-gather.5
  333.4 54.7 reduce-scatter.5
  390.5 45.3 reduce-scatter.7
  454.5 67.2 reduce-scatter.9
  524.0 48.3 reduce-scatter.13
  574.8 74.9 reduce-scatter.11

commit v7 on v6

--- a/solution.py
+++ b/solution.py
@@ -989,7 +989,7 @@
         outer = [functools.partial(across, s) for s in seqs]
         late = [*inner[:3], stages[8], *inner[3:]]
         for i, job in enumerate(late):
-            jobs.setdefault(min(9 + i, count - 1), []).append(job)
+            jobs.setdefault(min(7 + 2 * i, count - 1), []).append(job)
         rest = [*outer[:-1], *stages[9:], *outer[-1:]]
     for i in range(1, count):
         emit(i)

time: 700 us -> 700 us (level)
  no operation moved by 1% of the time
where the time goes in v7:
time: 700 us; the launch traced here: 692 us
  Pallas kernels  481 us (69%)
  matrix products  109 us (16%)
  local copies, waits for them, and re-layouts  32 us (5%)
  waiting for transfers between devices  25.5 us (4%)
  other arithmetic  25.1 us (4%)
  between operations  19.7 us (3%)
    pallas_call x2, Pallas kernels, line_scan(): pl.pallas_call(functools.partial(scan_kernel, count, forward, cuts, gathe...  138 us
    pallas_call x1, Pallas kernels, open_plane(): pl.pallas_call(functools.partial(open_kernel, count, chunks, line, order,...  88.5 us
    pallas_call x1, Pallas kernels, plane_turn(): pl.pallas_call(functools.partial(turn_kernel, order), out_shape=[jax.Shap...  81.7 us
    pallas_call x1, Pallas kernels, plane_mix(): pl.pallas_call(functools.partial(mix_kernel, order, places), out_shape=[j...  81.1 us
    pallas_call x1, Pallas kernels, plane_last(): pl.pallas_call(functools.partial(last_kernel, order, moves), out_shape=[j...  62.6 us
    dot_general x6, matrix products, mm_grad(): return jnp.einsum('sti,sto->io', left, right, preferred_element_type=F32)  47.8 us
    dot_general x3, matrix products, mm(): return jnp.einsum('sti,io->sto', left, right, preferred_element_type=F32)  33 us
    pallas_call x1, Pallas kernels, plane_final(): pl.pallas_call(functools.partial(final_kernel, line, order, heads_pb, mov...  29.1 us
  transfers between devices with their start and end apart: 8, of which 2 were waited for; matrix products, arithmetic and copies ran while one was open for 18% of the time, Pallas kernels for 52%

profile of v7, /device:TPU:2, one launch (start us, length us, event | category | flops | bytes accessed | tf_op | source)
XLA Modules:
  0.0 692.3 jit_solution(152212403513986641)
XLA Ops:
  9.9 1.3 pad.6.refs_6_
  11.2 88.5 %open_plane.1 = (bf16[4,512,2048]{2,1,0:T(8,128)(2,1)}, bf16[8,64,512]{2,1,0:T(8,128)(2,1)}, bf16[2048,1024]{1,0:T(8,128)(2,1)}, bf16[1040,512]{1,0:T(8,128)(2,1...) custom-call(f32[64,2048]{1,0:T(8,128)} %refs_0_.5, f32[64,2048]{1,0:T(8,128)} %refs_1_.3, f32[64,4096]{1,0:T(8,128)} %refs_2_.3, ...), custom_call_target="tpu_custom_call" | custom-call | tf_op jit(solution)/shard_map/open_plane/pallas_call | solution.py:461
  100.9 12.5 %fusion.14 = f32[4,512,1024]{2,1,0:T(8,128)S(1)} fusion(bf16[4,512,2048]{2,1,0:T(8,128)(2,1)} %get-tuple-element.40, bf16[2048,1024]{1,0:T(8,128)(2,1)} %get-tuple-element.41.refs_3_), kind=kOutput, calls=%fused_computation.24 | convolution fusion | flops 8589934592 | bytes 20971520 | tf_op jit(solution)/shard_map/sti,io->sto/dot_general | solution.py:1160
  113.9 1.1 fusion.29
  118.1 51.7 %line_scan.2 = (bf16[4,256,512]{2,1,0:T(8,128)(2,1)S(1)}, bf16[4,512,2048]{2,1,0:T(8,128)(2,1)S(1)}) custom-call(f32[4,256,512]{2,1,0:T(8,128)S(1)} %fusion.25.state, f32[2,4]{1,0:T(2,128)S(1)} %stack.8.coef, bf16[2,128,2048]{2,1,0:T(8,128)(2,1)S(1)} %copy-done.7, bf16[4,512,512]{2,1,0:T(8,128)(2,1)S(1)} %slice.102.refs_1_.refs_5_, ...), custom_call_target="tpu_custom_call" | custom-call | tf_op jit(solution)/shard_map/line_scan/pallas_call | solution.py:1035
  170.0 1.1 copy-done.26
  172.0 1.3 fusion.42
  175.4 2.0 copy-done.22
  179.4 24.2 %all-gather.4.cloned.1.call-done.gate_out = bf16[4160,512]{1,0:T(8,128)(2,1)} async-done(((bf16[1040,512]{1,0:T(8,128)(2,1)}), bf16[4160,512]{1,0:T(8,128)(2,1)}) %all-gather.4.cloned.1.call-update) | async-done | bytes 4259856 | tf_op jit(solution)/shard_map/all_gather | solution.py:1233
  203.6 1.2 slice.84
  206.4 1.9 slice_add_fusion
  209.2 8.8 %multiply_convert_fusion.3 = (bf16[4,512,512]{2,1,0:T(8,128)(2,1)S(1)}, bf16[4,512,512]{2,1,0:T(8,128)(2,1)}) fusion(f32[4,512,512]{2,1,0:T(8,128)S(1)} %copy-done.23, f32[4,512]{1,0:T(4,128)S(1)} %get-tuple-element.81, f32[4,512]{1,0:T(4,128)S(1)} %broadcast_multiply_fusion.2, bf16[4,512,2048]{2,1,0:T(8,128)(2,1)} %get-tuple-element.40, ...), kind=kOutput, calls=%fused_computation.31 | convolution fusion | flops 4304404480 | bytes 18890752 | tf_op jit(solution)/shard_map/sti,io->sto/dot_general | solution.py:1160
  217.9 1.3 copy-done.32
  221.7 81.1 %plane_mix.1 = (f32[2,128,2048]{2,1,0:T(8,128)S(1)}, bf16[4,512,2048]{2,1,0:T(8,128)(2,1)}, bf16[512,2048]{1,0:T(8,128)(2,1)S(1)}) custom-call(bf16[4,512,512]{2,1,0:T(8,128)(2,1)} %copy-done.32, bf16[2,128,2048]{2,1,0:T(8,128)(2,1)S(1)} %copy-done.2, bf16[4160,512]{1,0:T(8,128)(2,1)} %all-gather.4.cloned.1.call-done.gate_out, ...), custom_call_target="tpu_custom_call" | custom-call | tf_op jit(solution)/shard_map/plane_mix/pallas_call | solution.py:731
  302.8 1.4 copy-done.4
  304.2 1.3 copy-done.21
  306.2 11.7 %multiply_convert_fusion.2 = (bf16[4,512,512]{2,1,0:T(8,128)(2,1)}, f32[4,512,512]{2,1,0:T(8,128)}) fusion(f32[512]{0:T(512)S(1)} %bitcast.93, bf16[4,512,2048]{2,1,0:T(8,128)(2,1)} %get-tuple-element.47, bf16[2048,512]{1,0:T(8,128)(2,1)} %all-gather.8.cloned.1.call-done.weight), kind=kOutput, calls=%fused_computation.29 | convolution fusion | flops 4301258752 | bytes 16779264 | tf_op jit(solution)/shard_map/sti,io->sto/dot_general | solution.py:1160
  317.9 9.6 %fusion.8.grad = bf16[4,512,512]{2,1,0:T(8,128)(2,1)S(1)} fusion(f32[4,512,512]{2,1,0:T(8,128)} %get-tuple-element.93, bf16[4,512,2048]{2,1,0:T(8,128)(2,1)} %copy-done.20, bf16[512,2048]{1,0:T(8,128)(2,1)} %all-gather.6.cloned.1.call-done.refs_1_, f32[512]{0:T(512)S(1)} %bitcast.94), kind=kOutput, calls=%fused_computation.12 | convolution fusion | flops 4306501632 | bytes 16779264 | tf_op jit(solution)/shard_map/sto,io->sti/dot_general | solution.py:1164
  327.5 5.7 bitcast_convert_fusion.2.refs_1_
  334.3 8.6 %bitcast_convert_fusion.3 = bf16[512,2048]{1,0:T(8,128)(2,1)S(1)} fusion(bf16[4,512,512]{2,1,0:T(8,128)(2,1)} %get-tuple-element.92.refs_0_, bf16[4,512,2048]{2,1,0:T(8,128)(2,1)} %copy-done.20), kind=kOutput, calls=%fused_computation.23 | convolution fusion | flops 4296015872 | bytes 12582912 | tf_op jit(solution)/shard_map/sti,sto->io/dot_general | solution.py:1168
  342.9 1.6 pad_maximum_fusion.refs_0_
  344.6 1.6 copy-done.15
  346.2 81.7 %plane_turn.1 = (f32[2,128,2048]{2,1,0:T(8,128)S(1)}, bf16[4,512,2048]{2,1,0:T(8,128)(2,1)}) custom-call(bf16[4,512,512]{2,1,0:T(8,128)(2,1)S(1)} %copy-done.15, bf16[2048,512]{1,0:T(8,128)(2,1)} %all-gather.8.cloned.1.call-done.weight, f32[2,128,2048]{2,1,0:T(8,128)} %copy-done.4, bf16[2,128,2048]{2,1,0:T(8,128)(2,1)S(1)} %copy-done.8, ...), custom_call_target="tpu_custom_call" | custom-call | tf_op jit(solution)/shard_map/plane_turn/pallas_call | solution.py:778
  427.9 1.4 copy-done.11
  429.3 1.2 slice.86
  431.2 12.2 %fusion.39 = (f32[4,512]{1,0:T(4,128)S(1)}, f32[4,512]{1,0:T(4,128)S(1)}, f32[4,512,512]{2,1,0:T(8,128)}, bf16[4,512,512]{2,1,0:T(8,128)(2,1)S(1)}) fusion(f32[4,512]{1,0:T(4,128)S(1)} %get-tuple-element.81, f32[4,512,512]{2,1,0:T(8,128)} %copy-done.22, f32[4,512]{1,0:T(4,128)S(1)} %broadcast_multiply_fusion.2, ...), kind=kOutput, calls=%fused_computation.104 | convolution fusion | flops 4313837568 | bytes 23101444 | tf_op jit(solution)/shard_map/sto,io->sti/dot_general | solution.py:1164
  443.4 1.3 copy-done.34
  444.7 9.6 %bitcast_convert_fusion.1.refs_16_ = bf16[2048,512]{1,0:T(8,128)(2,1)} fusion(bf16[4,512,2048]{2,1,0:T(8,128)(2,1)} %get-tuple-element.40, bf16[4,512,512]{2,1,0:T(8,128)(2,1)S(1)} %get-tuple-element.73.refs_4_), kind=kOutput, calls=%fused_computation.21 | convolution fusion | flops 4296015872 | bytes 12582912 | tf_op jit(solution)/shard_map/sti,sto->io/dot_general | solution.py:1168
  454.4 1.2 slice.87
  456.3 9.2 %fusion.13.refs_17_ = bf16[512,2048]{1,0:T(8,128)(2,1)} fusion(bf16[4,512,512]{2,1,0:T(8,128)(2,1)S(1)} %copy-done.33, bf16[4,512,2048]{2,1,0:T(8,128)(2,1)} %get-tuple-element.50, f32[]{:T(128)} %bitcast.25), kind=kOutput, calls=%fused_computation.20 | convolution fusion | flops 4297064448 | bytes 12582916 | tf_op jit(solution)/shard_map/sti,sto->io/dot_general | solution.py:1168
  466.1 4.1 multiply_convert_fusion.1.refs_6_
  470.2 2.2 fusion.24.state
  472.5 85.9 %line_scan.3 = (bf16[4,256,512]{2,1,0:T(8,128)(2,1)}, bf16[2,128,2048]{2,1,0:T(8,128)(2,1)}, bf16[4,512,256]{2,1,0:T(8,128)(2,1)}, bf16[4,512,256]{2,1,0:T(8,128)(2,1)}, bf16[4,512,512]{2,1,0:T(8,128)(2,1)}) custom-call(f32[4,256,512]{2,1,0:T(8,128)} %fusion.24.state, f32[2,4]{1,0:T(2,128)} %stack.9.coef, bf16[4,512,512]{2,1,0:T(8,128)(2,1)} %get-tuple-element.92.refs_0_, ...), custom_call_target="tpu_custom_call" | custom-call | tf_op jit(solution)/shard_map/line_scan/pallas_call | solution.py:1035
  558.4 1.2 slice.88
  560.2 14.0 %bitcast_convert_fusion.refs_15_ = bf16[2048,1024]{1,0:T(8,128)(2,1)} fusion(bf16[4,512,2048]{2,1,0:T(8,128)(2,1)} %get-tuple-element.40, bf16[4,512,512]{2,1,0:T(8,128)(2,1)} %get-tuple-element.55.refs_2_, bf16[4,512,256]{2,1,0:T(8,128)(2,1)} %get-tuple-element.54.refs_1_, bf16[4,512,256]{2,1,0:T(8,128)(2,1)} %get-tuple-element.53.refs_0_, bf16[]{:T(256)} %bitcast.30), kind=kOutput, calls=%fused_computation | convolution fusion | flops 8608808960 | bytes 16777218 | tf_op jit(solution)/shard_map/sti,sto->io/dot_general | solution.py:1168
  574.3 1.4 convert_reduce_fusion
  575.6 62.6 %plane_last.1 = (f32[2,128,2048]{2,1,0:T(8,128)}, f32[64,4096]{1,0:T(8,128)}, f32[64,4096]{1,0:T(8,128)}, f32[64,1]{1,0:T(8,128)}, f32[64,1]{1,0:T(8,128)}, /*index=5*/f32[128,2048]{1,0:T(8,128)}) custom-call(bf16[4,512,256]{2,1,0:T(8,128)(2,1)} %get-tuple-element.53.refs_0_, bf16[4,512,256]{2,1,0:T(8,128)(2,1)} %get-tuple-element.54.refs_1_, ...), custom_call_target="tpu_custom_call" | custom-call | tf_op jit(solution)/shard_map/plane_last/pallas_call | solution.py:849
  638.3 1.2 slice.74
  640.1 1.4 reduce.1
  641.5 2.4 broadcast_add_fusion.1
  644.0 1.0 broadcast_add_fusion.4
  645.0 1.5 broadcast_add_fusion
  646.5 1.0 broadcast_add_fusion.3
  647.5 1.0 broadcast_add_fusion.2
  648.6 1.1 reduce-scatter.12.cloned.1.call-done
  649.8 1.2 copy-done.16
  651.0 1.0 copy-done.18
  652.0 29.1 %plane_final.1 = (f32[64,2048]{1,0:T(8,128)S(1)}, f32[64,2048]{1,0:T(8,128)S(1)}, f32[64,4096]{1,0:T(8,128)S(1)}, f32[128,2048]{1,0:T(8,128)S(1)}, f32[64,1]{1,0:T(8,128)S(1)}) custom-call(bf16[8,64,1024]{2,1,0:T(8,128)(2,1)S(1)} %bitcast.84, bf16[128,2048]{1,0:T(8,128)(2,1)S(1)} %copy-done.18, f32[64,2048]{1,0:T(8,128)S(1)} %copy-done.12, ...), custom_call_target="tpu_custom_call" | custom-call | tf_op jit(solution)/shard_map/plane_final/pallas_call | solution.py:1102
  (137 shorter events, 21.9 us)
Async XLA Ops:
  7.2 196.4 %all-gather.4.cloned.1.call-start = ((), (), s32[]{:S(2)}) async-start(), calls=%async_computation.5 | async-start | bytes 5324800 | tf_op jit(solution)/shard_map/all_gather | solution.py:1233
  99.8 206.4 %all-gather.8.cloned.1.call-start = ((), (), s32[]{:S(2)}) async-start(), calls=%async_computation.7 | async-start | bytes 2621440 | tf_op jit(solution)/shard_map/all_gather | solution.py:1233
  113.7 3.6 copy-start.1
  115.0 0.9 copy-start.30
  115.0 0.9 copy-start.31
  116.1 354.1 %copy-start = (bf16[4,512,256]{2,1,0:T(8,128)(2,1)}, bf16[4,512,256]{2,1,0:T(8,128)(2,1)S(1)}, u32[]{:S(2)}) copy-start(bf16[4,512,256]{2,1,0:T(8,128)(2,1)S(1)} %fusion.16.refs_2_.refs_3_) | copy-start | bytes 3145732
  116.3 53.5 %copy-start.3 = (bf16[4,512,256]{2,1,0:T(8,128)(2,1)}, bf16[4,512,256]{2,1,0:T(8,128)(2,1)S(1)}, u32[]{:S(2)}) copy-start(bf16[4,512,256]{2,1,0:T(8,128)(2,1)S(1)} %pad_maximum_fusion.1.refs_3_.refs_4_) | copy-start | bytes 3145732
  116.3 1.8 copy-start.7
  169.8 4.2 copy-start.20
  169.8 4.7 copy-start.6
  170.0 1.2 copy-start.26
  172.0 2.0 copy-start.24
  175.4 2.1 copy-start.22
  175.4 30.0 %copy-start.39 = (bf16[8,64,512]{2,1,0:T(8,128)(2,1)S(1)}, bf16[8,64,512]{2,1,0:T(8,128)(2,1)}, u32[]{:S(2)}) copy-start(bf16[8,64,512]{2,1,0:T(8,128)(2,1)} %get-tuple-element.48) | copy-start | bytes 1572868
  206.3 111.6 %all-gather.6.cloned.1.call-start = ((), (), s32[]{:S(2)}) async-start(), calls=%async_computation.6 | async-start | bytes 2621440 | tf_op jit(solution)/shard_map/all_gather | solution.py:1233
  206.3 2.8 copy-start.23
  208.2 9.7 %copy-start.27 = (bf16[4,512,512]{2,1,0:T(8,128)(2,1)}, bf16[4,512,512]{2,1,0:T(8,128)(2,1)S(1)}, u32[]{:S(2)}) copy-start(bf16[4,512,512]{2,1,0:T(8,128)(2,1)S(1)} %slice_add_fusion) | copy-start | bytes 6291460
  209.2 11.3 %copy-start.40 = (bf16[128,2048]{1,0:T(8,128)(2,1)S(1)}, bf16[128,2048]{1,0:T(8,128)(2,1)}, u32[]{:S(2)}) copy-start(bf16[128,2048]{1,0:T(8,128)(2,1)} %get-tuple-element.45) | copy-start | bytes 1572868
  209.2 12.5 %copy-start.2 = (bf16[2,128,2048]{2,1,0:T(8,128)(2,1)S(1)}, bf16[2,128,2048]{2,1,0:T(8,128)(2,1)}, u32[]{:S(2)}) copy-start(bf16[2,128,2048]{2,1,0:T(8,128)(2,1)} %refs_6_.1) | copy-start | bytes 3145732
  217.9 1.3 copy-start.32
  221.3 208.0 %reduce-scatter.6.cloned.1.call-start = ((), (), s32[]{:S(2)}) async-start(), calls=%async_computation.8 | async-start | bytes 2621440 | tf_op jit(solution)/shard_map/reduce_scatter | solution.py:1236
  221.6 81.2 %copy-start.9 = (f32[512,1]{1,0:T(8,128)}, f32[512,1]{1,0:T(8,128)S(1)}, u32[]{:S(2)}) copy-start(f32[512,1]{1,0:T(8,128)S(1)} %get-tuple-element.98.refs_2_.refs_11_) | copy-start | bytes 6148
  221.6 81.2 %copy-start.10 = (f32[512,1]{1,0:T(8,128)}, f32[512,1]{1,0:T(8,128)S(1)}, u32[]{:S(2)}) copy-start(f32[512,1]{1,0:T(8,128)S(1)} %get-tuple-element.99.refs_1_.refs_10_) | copy-start | bytes 6148
  302.8 1.4 copy-start.4
  304.2 1.3 copy-start.21
  317.9 9.6 %copy-start.41 = (bf16[4,512,2048]{2,1,0:T(8,128)(2,1)S(1)}, bf16[4,512,2048]{2,1,0:T(8,128)(2,1)}, u32[]{:S(2)}) copy-start(bf16[4,512,2048]{2,1,0:T(8,128)(2,1)} %get-tuple-element.47) | copy-start | bytes 25165828
  327.5 6.0 copy-start.14
  333.3 121.1 %reduce-scatter.8.cloned.1.call-start = ((), (), s32[]{:S(2)}) async-start(), calls=%async_computation.9 | async-start | bytes 2785280 | tf_op jit(solution)/shard_map/reduce_scatter | solution.py:1236
  342.9 1.7 copy-start.8
  344.5 213.8 %reduce-scatter.10.cloned.1.call-start = ((), (), s32[]{:S(2)}) async-start(), calls=%async_computation.10 | async-start | bytes 2621440 | tf_op jit(solution)/shard_map/reduce_scatter | solution.py:1236
  344.6 1.6 copy-start.15
  427.9 1.4 copy-start.11
  443.4 1.3 copy-start.34
  444.7 11.5 %copy-start.33 = (bf16[4,512,512]{2,1,0:T(8,128)(2,1)S(1)}, bf16[4,512,512]{2,1,0:T(8,128)(2,1)}, u32[]{:S(2)}) copy-start(bf16[4,512,512]{2,1,0:T(8,128)(2,1)} %copy-done.32) | copy-start | bytes 6291460
  454.3 194.3 %reduce-scatter.14.cloned.1.call-start = ((), (), s32[]{:S(2)}) async-start(), calls=%async_computation.12 | async-start | bytes 2621440 | tf_op jit(solution)/shard_map/reduce_scatter | solution.py:1236
  465.4 184.3 %reduce-scatter.12.cloned.1.call-start = ((), (), s32[]{:S(2)}) async-start(), calls=%async_computation.11 | async-start | bytes 5242880 | tf_op jit(solution)/shard_map/reduce_scatter | solution.py:1236
  470.2 2.2 copy-start.25
  575.6 68.3 %copy-start.36 = (bf16[2,128,2048]{2,1,0:T(8,128)(2,1)S(1)}, bf16[2,128,2048]{2,1,0:T(8,128)(2,1)}, u32[]{:S(2)}) copy-start(bf16[2,128,2048]{2,1,0:T(8,128)(2,1)} %get-tuple-element.52) | copy-start | bytes 3145732
  641.5 3.5 copy-start.35
  641.5 5.0 copy-start.38
  644.0 3.6 copy-start.37
  645.0 4.7 copy-start.5
  645.0 4.7 copy-start.12
  645.0 4.7 copy-start.13
  645.0 4.7 copy-start.17
  645.0 4.7 copy-start.19
  649.8 1.2 copy-start.16
  651.0 1.0 copy-start.18
  (2 other events, 1.5 us)
Sparse Core Ops, SparseCore 0:
  99.9 103.6 all-gather.3
  206.4 56.9 all-gather.7
  265.5 44.9 all-gather.5
  333.4 54.7 reduce-scatter.5
  390.5 45.3 reduce-scatter.7
  454.5 67.2 reduce-scatter.9
  524.0 48.3 reduce-scatter.13
  574.8 74.9 reduce-scatter.11
